TPU v7x, 256 devices: a whole 4x4x8 slice. The times are simulated.
256 devices in a mesh: expert: 128 (over y, x, z), row: 2 (over core).
Axes of the slice: x: 4, y: 4, z: 8, core: 2. Of those that a mesh axis runs over, the one named last changes fastest.
Arguments:
- calib_rows: bfloat16 [128, 128, 4096], P('expert', 'row'), may hold values from -6 to 6
- gate_weight: bfloat16 [128, 4096, 768], P('expert', 'row'), may hold values from -0.09375 to 0.09375
- up_weight: bfloat16 [128, 4096, 768], P('expert', 'row'), may hold values from -0.09375 to 0.09375
- cluster: int32 [128], replicated, may hold values from 0 to 31, never falling along the last dimension, each value on 1 to 8 neighbouring positions
- dominant_rank: int32 [32], replicated, may hold values from 0 to 7
Outputs:
- correlation: float32 [128, 768, 768], P('expert', 'row')
Inputs may be any that keep to these rules, and one draw needn't show every extreme that they name: cluster numbers never fall along the expert index; each of the 32 clusters holds 1 to 8 experts, and one holds exactly 8.
All inputs are finite; a program needn't handle non-finite values.
Results may differ from a plain program's by a relative error of at most 0.0039.
Values may be sent and summed in bfloat16 or wider, within the bound.
No kernel may reach another device: no remote copies, remote signals or barrier semaphores. Data moves between devices by JAX's collectives and lax.ppermute only.
A program may use at most 256 MiB of HBM per device.

v0:
```python
import functools

import jax
import jax.numpy as jnp
from jax import lax
from jax.experimental import pallas as pl
from jax.experimental.pallas import tpu as pltpu
from jax.sharding import PartitionSpec as P

ROWS = 128
LINE = 8
TILE = 512
OFFSETS = (1, 7, 2, 6, 3, 5, 4)
GROUPS = ((0, 1, 7), (2, 6), (3, 5), (4,))

NEAR, DOM, CORE, LINE_AT, PLACE, SIZE = 0, 24, 48, 49, 50, 51


def along_line(value, offset):
    count = lax.axis_size("expert")
    pairs = [(i, i // LINE * LINE + (i - offset) % LINE) for i in range(count)]
    return lax.ppermute(value, "expert", pairs)


def to_line(value, step):
    count = lax.axis_size("expert")
    return lax.ppermute(value, "expert", [(i, (i + step * LINE) % count) for i in range(count)])


def to_side(value, offset):
    count = lax.axis_size("expert")
    side = lambda i: LINE if i % LINE + offset < LINE else -LINE
    return lax.ppermute(value, "expert", [(i, (i + side(i)) % count) for i in range(count)])


def swap_cores(value):
    return lax.ppermute(value, "row", [(0, 1), (1, 0)])


def scalars(cluster, dominant_rank):
    expert_id = lax.axis_index("expert")
    line, place = expert_id // LINE, expert_id % LINE
    start = jnp.sum((cluster[None, :] < cluster[:, None]).astype(jnp.int32), axis=1)
    size = jnp.sum((cluster[None, :] == cluster[:, None]).astype(jnp.int32), axis=1)
    names = jnp.arange(dominant_rank.shape[0], dtype=jnp.int32)
    rank = jnp.sum(jnp.where(names[None, :] == cluster[:, None], dominant_rank[None, :], 0), axis=1)
    dom = start + rank % size
    tables = jnp.pad(jnp.stack([cluster, dom, size]), ((0, 0), (LINE, LINE)), constant_values=-1)
    three = lax.dynamic_slice_in_dim(tables, line * LINE, 3 * LINE, 1).reshape(3, 3, LINE)
    rolled = lax.dynamic_slice_in_dim(jnp.concatenate([three, three], axis=2), place, LINE, 2)
    here = jnp.stack([lax.axis_index("row"), line, place, rolled[2, 1, 0]])
    return jnp.concatenate([rolled[:2].reshape(-1), here]).astype(jnp.int32)


def near(table, line, k):
    return table[NEAR + LINE * line + k]


def hidden_kernel(group, table, *refs):
    many = len(group)
    xs, weights = refs[: 4 * many], refs[4 * many : 4 * many + 4]
    outs, (gate_sum, up_sum) = refs[4 * many + 4 : 5 * many + 4], refs[5 * many + 4 :]
    step = pl.program_id(0)
    mine = near(table, 1, 0)

    @pl.when(step == 0)
    def _():
        gate_sum[...] = jnp.zeros_like(gate_sum)
        up_sum[...] = jnp.zeros_like(up_sum)

    for side in range(2):
        rows = []
        for n, k in enumerate(group):
            ring, beside = xs[4 * n + side], xs[4 * n + 2 + side]
            rows.append(ring[...] if k == 0 else jnp.where(near(table, 1, k) == mine, ring[...], beside[...]))
        rows = jnp.concatenate(rows, axis=0)
        gate_sum[...] += jnp.dot(rows, weights[side][...], preferred_element_type=jnp.float32)
        up_sum[...] += jnp.dot(rows, weights[2 + side][...], preferred_element_type=jnp.float32)

    @pl.when(step == pl.num_programs(0) - 1)
    def _():
        gate = gate_sum[...]
        value = gate / (1.0 + jnp.exp(-gate)) * up_sum[...]
        part = outs[0].shape[0]
        for n, k in enumerate(group):
            block = value[n * part : (n + 1) * part].astype(jnp.bfloat16)
            inside = (near(table, 0, k) == mine) | (near(table, 1, k) == mine) | (near(table, 2, k) == mine)
            outs[n][...] = jnp.where(inside, block, jnp.zeros_like(block))


def hidden_of(table, group, ring, beside, weights):
    part, width = ring[0].shape
    half, units = weights[0].shape
    steps = half // TILE
    own_half = pl.BlockSpec((part, TILE), lambda i, t: (0, t[CORE] * steps + i))
    other_half = pl.BlockSpec((part, TILE), lambda i, t: (0, (1 - t[CORE]) * steps + i))
    weight = pl.BlockSpec((TILE, units), lambda i, t: (i, 0))
    args, specs = [], []
    for k in group:
        args += [ring[k], ring[k], beside.get(k, ring[k]), beside.get(k, ring[k])]
        specs += [own_half, other_half, own_half, other_half]
    rows = part * len(group)
    return pl.pallas_call(
        functools.partial(hidden_kernel, group),
        out_shape=[jax.ShapeDtypeStruct((part, units), jnp.bfloat16)] * len(group),
        grid_spec=pltpu.PrefetchScalarGridSpec(
            num_scalar_prefetch=1,
            grid=(steps,),
            in_specs=specs + [weight] * 4,
            out_specs=[pl.BlockSpec((part, units), lambda i, t: (0, 0))] * len(group),
            scratch_shapes=[pltpu.VMEM((rows, units), jnp.float32)] * 2,
        ),
        compiler_params=pltpu.CompilerParams(vmem_limit_bytes=40 << 20),
        cost_estimate=pl.CostEstimate(
            flops=4 * rows * width * units, bytes_accessed=8 * half * units + 4 * rows * width, transcendentals=rows * units
        ),
        name="hidden",
    )(table, *args, *weights)


def goes_on(table, to):
    edge = (LINE - 1 - table[PLACE]) if to == 0 else (LINE - table[PLACE]) % LINE
    return near(table, to, edge) == near(table, 1, 0)


def dom_of(table, line):
    return table[DOM + LINE * line]


def share_kernel(table, *refs):
    returned, outs = refs[:LINE], refs[LINE:]
    own = dom_of(table, 1)
    targets = (own, jnp.where(goes_on(table, 2), own, dom_of(table, 2)), jnp.where(goes_on(table, 0), own, dom_of(table, 0)))
    for out, target in zip(outs, targets):
        place = (target - table[PLACE]) & (LINE - 1)
        for k in range(LINE):

            @pl.when(place == k)
            def _():
                out[...] = returned[k][...]


def send_kernel(table, own, nxt, last, came_last, came_next, *outs):
    line = table[LINE_AT]
    dom = [lax.div(dom_of(table, n) + LINE, LINE) - 1 for n in range(3)]
    at_own = jnp.where(dom[1] == line, 0, jnp.where(dom[1] > line, 4, 3))
    at_last = jnp.where(dom[0] == line, 2, 3)
    at_next = jnp.where(dom[2] == line, 1, 4)
    sources = (own, nxt, last, came_last, came_next)
    for away in range(LINE):
        wanted = near(table, 1, away)
        source = jnp.where(wanted == near(table, 0, 0), at_last, jnp.where(wanted == near(table, 2, 0), at_next, at_own))
        for n, ref in enumerate(sources):

            @pl.when(source == n)
            def _():
                outs[away][...] = ref[...]


def choose(kernel, table, arrays, outs, name):
    whole = pl.BlockSpec(memory_space=pltpu.VMEM)
    shape = jax.ShapeDtypeStruct(arrays[0].shape, arrays[0].dtype)
    size = 2 * arrays[0].size
    return pl.pallas_call(
        kernel,
        out_shape=[shape] * outs,
        in_specs=[pl.BlockSpec(memory_space=pltpu.SMEM)] + [whole] * len(arrays),
        out_specs=[whole] * outs,
        compiler_params=pltpu.CompilerParams(vmem_limit_bytes=24 << 20),
        cost_estimate=pl.CostEstimate(flops=0, bytes_accessed=size * (len(arrays) + outs), transcendentals=0),
        name=name,
    )(table, *arrays)


def correlate_kernel(add, table, *refs):
    hidden, panel = refs[:LINE], refs[LINE : 2 * LINE]
    out = refs[-1]
    left = jnp.concatenate([ref[...] for ref in hidden], axis=0)
    right = jnp.concatenate([ref[...] for ref in panel], axis=0)
    sums = lax.dot_general(left, right, (((0,), (0,)), ((), ())), preferred_element_type=jnp.float32)
    if add:
        rows = jnp.full((1, 1), table[SIZE] * ROWS, jnp.int32).astype(jnp.float32)
        sums = (sums + refs[2 * LINE][...]) / jnp.sqrt(rows)
    out[...] = sums


def correlate(table, hidden, panel, received=None):
    part, units = hidden[0].shape
    add = received is not None
    core = (lambda t: t[CORE]) if add else (lambda t: 1 - t[CORE])
    tile = 128
    steps = units // 2 // tile
    left = pl.BlockSpec((part, tile), lambda i, t: (0, core(t) * steps + i))
    right = pl.BlockSpec((part, units), lambda i, t: (0, 0))
    result = pl.BlockSpec((tile, units), lambda i, t: (i, 0))
    extra = [received] if add else []
    return pl.pallas_call(
        functools.partial(correlate_kernel, add),
        out_shape=jax.ShapeDtypeStruct((units // 2, units), jnp.float32),
        grid_spec=pltpu.PrefetchScalarGridSpec(
            num_scalar_prefetch=1,
            grid=(steps,),
            in_specs=[left] * LINE + [right] * LINE + [result] * len(extra),
            out_specs=result,
        ),
        compiler_params=pltpu.CompilerParams(vmem_limit_bytes=24 << 20),
        cost_estimate=pl.CostEstimate(
            flops=LINE * part * units * units, bytes_accessed=32 * part * units, transcendentals=0
        ),
        name="correlate",
    )(table, *hidden, *panel, *extra)


def per_device(calib_rows, gate_weight, up_weight, cluster, dominant_rank):
    table = scalars(cluster, dominant_rank)

    ring, beside = {0: calib_rows[0]}, {}
    for step in range(1, LINE // 2 + 1):
        ring[step] = along_line(ring[step - 1], 1)
        if step < LINE // 2:
            ring[LINE - step] = along_line(ring[(LINE - step + 1) % LINE], -1)
    gate, up = gate_weight[0], up_weight[0]
    weights = (gate, swap_cores(gate), up, swap_cores(up))

    hidden, returned = {}, {}
    for group in GROUPS:
        for k in group:
            if k:
                beside[k] = to_side(ring[k], k)
        for k, block in zip(group, hidden_of(table, group, ring, beside, weights)):
            hidden[k] = block
            returned[(LINE - k) % LINE] = along_line(block, LINE - k) if k else block

    shares = choose(share_kernel, table, [returned[k] for k in range(LINE)], 3, "share")
    came_last, came_next = to_line(shares[1], 1), to_line(shares[2], -1)
    chunks = choose(send_kernel, table, [*shares, came_last, came_next], LINE, "send")
    panel = {k: along_line(chunks[(-k) % LINE], k) if k else chunks[0] for k in range(LINE)}

    hidden, panel = [hidden[k] for k in range(LINE)], [panel[k] for k in range(LINE)]
    received = swap_cores(correlate(table, hidden, panel))
    return correlate(table, hidden, panel, received)[None]


def solution(mesh):
    return jax.shard_map(
        per_device,
        mesh=mesh,
        in_specs=(
            P("expert", "row", None),
            P("expert", "row", None),
            P("expert", "row", None),
            P(),
            P(),
        ),
        out_specs=P("expert", "row", None),
        check_vma=False,
    )
```

profile of v0, /device:TPU:1, one launch (start us, length us, event | category | flops | bytes accessed | tf_op | source)
XLA Modules:
  0.0 176.0 jit_solution(4129721958489382533)
XLA Ops:
  0.0 3.2 %collective-permute-start.4 = (bf16[2048,768]{1,0:T(8,128)(2,1)}, bf16[2048,768]{1,0:T(8,128)(2,1)S(1)}, u32[]{:S(2)}, u32[]{:S(2)}) collective-permute-start(bf16[2048,768]{1,0:T(8,128)(2,1)} %bitcast.15), channel_id=1, source_target_pairs={{0,1},{1,0},{2,3},{3,2},{4,5},{5,4},{6,7},{7,6},{8,9},{9,8},{10,11... | collective-permute-start | bytes 9437192 | tf_op jit(solution)/shard_map/ppermute | solution.py:37
  3.2 3.8 %collective-permute-start = (bf16[64,4096]{1,0:T(8,128)(2,1)}, bf16[64,4096]{1,0:T(8,128)(2,1)S(1)}, u32[]{:S(2)}, u32[]{:S(2)}) collective-permute-start(bf16[64,4096]{1,0:T(8,128)(2,1)} %bitcast.25), channel_id=1, source_target_pairs={{0,14},{2,0},{4,2},{6,4},{8,6},{10,8},{12,10},{14,12},{16,30},{18,... | collective-permute-start | bytes 1572872 | tf_op jit(solution)/shard_map/ppermute | solution.py:22
  7.1 11.1 %collective-permute-done.refs_4_.refs_5_ = bf16[64,4096]{1,0:T(8,128)(2,1)S(1)} collective-permute-done((bf16[64,4096]{1,0:T(8,128)(2,1)}, bf16[64,4096]{1,0:T(8,128)(2,1)S(1)}, u32[]{:S(2)}, u32[]{:S(2)}) %collective-permute-start) | collective-permute-done | bytes 524320 | tf_op jit(solution)/shard_map/ppermute | solution.py:22
  18.2 3.3 %collective-permute-start.6 = (bf16[64,4096]{1,0:T(8,128)(2,1)S(1)}, bf16[64,4096]{1,0:T(8,128)(2,1)}, u32[]{:S(2)}, u32[]{:S(2)}) collective-permute-start(bf16[64,4096]{1,0:T(8,128)(2,1)S(1)} %collective-permute-done.refs_4_.refs_5_), channel_id=1, source_target_pairs={{0,14},{2,0},{4,2},{6,4},{8,6},{10,8},{12,10},{14,12},{16,30},{18,... | collective-permute-start | bytes 1572872 | tf_op jit(solution)/shard_map/ppermute | solution.py:22
  21.5 1.2 collective-permute-start.1
  23.5 7.8 %collective-permute-done.6.refs_0_.refs_1_ = bf16[64,4096]{1,0:T(8,128)(2,1)} collective-permute-done((bf16[64,4096]{1,0:T(8,128)(2,1)S(1)}, bf16[64,4096]{1,0:T(8,128)(2,1)}, u32[]{:S(2)}, u32[]{:S(2)}) %collective-permute-start.6) | collective-permute-done | bytes 524320 | tf_op jit(solution)/shard_map/ppermute | solution.py:22
  31.3 3.5 %collective-permute-start.10 = (bf16[64,4096]{1,0:T(8,128)(2,1)}, bf16[64,4096]{1,0:T(8,128)(2,1)}, u32[]{:S(2)}, u32[]{:S(2)}) collective-permute-start(bf16[64,4096]{1,0:T(8,128)(2,1)} %collective-permute-done.6.refs_0_.refs_1_), channel_id=1, source_target_pairs={{0,14},{2,0},{4,2},{6,4},{8,6},{10,8},{12,10},{14,12},{16,30},{18,... | collective-permute-start | bytes 1572872 | tf_op jit(solution)/shard_map/ppermute | solution.py:22
  34.9 2.0 %collective-permute-done.1.refs_6_.refs_7_ = bf16[64,4096]{1,0:T(8,128)(2,1)S(1)} collective-permute-done((bf16[64,4096]{1,0:T(8,128)(2,1)S(1)}, bf16[64,4096]{1,0:T(8,128)(2,1)S(1)}, u32[]{:S(2)}, u32[]{:S(2)}) %collective-permute-start.1) | collective-permute-done | bytes 524320 | tf_op jit(solution)/shard_map/ppermute | solution.py:33
  38.5 5.6 %collective-permute-done.10.refs_0_.refs_1_ = bf16[64,4096]{1,0:T(8,128)(2,1)} collective-permute-done((bf16[64,4096]{1,0:T(8,128)(2,1)}, bf16[64,4096]{1,0:T(8,128)(2,1)}, u32[]{:S(2)}, u32[]{:S(2)}) %collective-permute-start.10) | collective-permute-done | bytes 524320 | tf_op jit(solution)/shard_map/ppermute | solution.py:22
  44.1 3.4 %collective-permute-start.14 = (bf16[64,4096]{1,0:T(8,128)(2,1)}, bf16[64,4096]{1,0:T(8,128)(2,1)S(1)}, u32[]{:S(2)}, u32[]{:S(2)}) collective-permute-start(bf16[64,4096]{1,0:T(8,128)(2,1)} %collective-permute-done.10.refs_0_.refs_1_), channel_id=1, source_target_pairs={{0,14},{2,0},{4,2},{6,4},{8,6},{10,8},{12,10},{14,12},{16,30},{18,... | collective-permute-start | bytes 1572872 | tf_op jit(solution)/shard_map/ppermute | solution.py:22
  49.3 3.0 %collective-permute-done.3.refs_10_.refs_11_ = bf16[64,4096]{1,0:T(8,128)(2,1)} collective-permute-done((bf16[64,4096]{1,0:T(8,128)(2,1)}, bf16[64,4096]{1,0:T(8,128)(2,1)}, u32[]{:S(2)}, u32[]{:S(2)}) %collective-permute-start.3) | collective-permute-done | bytes 524320 | tf_op jit(solution)/shard_map/ppermute | solution.py:33
  53.3 2.6 %collective-permute-done.14.refs_0_.refs_1_ = bf16[64,4096]{1,0:T(8,128)(2,1)S(1)} collective-permute-done((bf16[64,4096]{1,0:T(8,128)(2,1)}, bf16[64,4096]{1,0:T(8,128)(2,1)S(1)}, u32[]{:S(2)}, u32[]{:S(2)}) %collective-permute-start.14) | collective-permute-done | bytes 524320 | tf_op jit(solution)/shard_map/ppermute | solution.py:22
  55.9 1.2 collective-permute-start.11
  57.1 1.2 collective-permute-start.13
  60.0 1.1 collective-permute-start.15
  61.1 1.9 %copy-done = bf16[1,2048,768]{2,1,0:T(8,128)(2,1)S(1)} copy-done((bf16[1,2048,768]{2,1,0:T(8,128)(2,1)S(1)}, bf16[1,2048,768]{2,1,0:T(8,128)(2,1)}, u32[]{:S(2)}) %copy-start) | copy-done | bytes 3145752
  63.0 1.9 %copy-done.2 = bf16[1,2048,768]{2,1,0:T(8,128)(2,1)S(1)} copy-done((bf16[1,2048,768]{2,1,0:T(8,128)(2,1)S(1)}, bf16[1,2048,768]{2,1,0:T(8,128)(2,1)}, u32[]{:S(2)}) %copy-start.2) | copy-done | bytes 3145752
  64.8 1.0 copy-done.4
  65.9 1.0 copy-done.6
  66.9 1.0 copy-done.8
  68.0 6.5 %hidden.4 = (bf16[64,768]{1,0:T(8,128)(2,1)S(1)}, bf16[64,768]{1,0:T(8,128)(2,1)S(1)}, bf16[64,768]{1,0:T(8,128)(2,1)S(1)}) custom-call(s32[52]{0:T(128)S(1)} %concatenate.7.table, bf16[64,4096]{1,0:T(8,128)(2,1)S(1)} %bitcast.27, bf16[64,4096]{1,0:T(8,128)(2,1)S(1)} %bitcast.28, bf16[64,4096]{1,0:T(8,128)(2,1)S(1)} %bitcast.29, ...), custom_call_target="tpu_custom_call" | custom-call | flops 2415919104 | bytes 15728640 | tf_op jit(solution)/shard_map/hidden/pallas_call | solution.py:103
  74.5 6.3 %collective-permute-start.16 = (bf16[64,768]{1,0:T(8,128)(2,1)S(1)}, bf16[64,768]{1,0:T(8,128)(2,1)S(1)}, u32[]{:S(2)}, u32[]{:S(2)}) collective-permute-start(bf16[64,768]{1,0:T(8,128)(2,1)S(1)} %get-tuple-element.29.refs_7_), channel_id=1, source_target_pairs={{0,14},{2,0},{4,2},{6,4},{8,6},{10,8},{12,10},{14,12},{16,30},{18,... | collective-permute-start | bytes 294920 | tf_op jit(solution)/shard_map/ppermute | solution.py:22
  80.9 5.6 %hidden.5 = (bf16[64,768]{1,0:T(8,128)(2,1)S(1)}, bf16[64,768]{1,0:T(8,128)(2,1)S(1)}) custom-call(s32[52]{0:T(128)S(1)} %concatenate.7.table, bf16[64,4096]{1,0:T(8,128)(2,1)} %collective-permute-done.6.refs_0_.refs_1_, bf16[64,4096]{1,0:T(8,128)(2,1)} %collective-permute-done.6.refs_0_.refs_1_, bf16[64,4096]{1,0:T(8,128)(2,1)} %collective-permute-done.7.refs_2_.refs_3_, ...), custom_call_target="tpu_custom_call" | custom-call | flops 1610612736 | bytes 14680064 | tf_op jit(solution)/shard_map/hidden/pallas_call | solution.py:103
  86.5 2.0 %collective-permute-done.11.refs_2_.refs_3_ = bf16[64,4096]{1,0:T(8,128)(2,1)} collective-permute-done((bf16[64,4096]{1,0:T(8,128)(2,1)}, bf16[64,4096]{1,0:T(8,128)(2,1)}, u32[]{:S(2)}, u32[]{:S(2)}) %collective-permute-start.11) | collective-permute-done | bytes 524320 | tf_op jit(solution)/shard_map/ppermute | solution.py:33
  88.5 11.2 %collective-permute-done.13.refs_6_.refs_7_ = bf16[64,4096]{1,0:T(8,128)(2,1)} collective-permute-done((bf16[64,4096]{1,0:T(8,128)(2,1)}, bf16[64,4096]{1,0:T(8,128)(2,1)}, u32[]{:S(2)}, u32[]{:S(2)}) %collective-permute-start.13) | collective-permute-done | bytes 524320 | tf_op jit(solution)/shard_map/ppermute | solution.py:33
  99.7 5.5 %hidden.6 = (bf16[64,768]{1,0:T(8,128)(2,1)S(1)}, bf16[64,768]{1,0:T(8,128)(2,1)S(1)}) custom-call(s32[52]{0:T(128)S(1)} %concatenate.7.table, bf16[64,4096]{1,0:T(8,128)(2,1)} %collective-permute-done.10.refs_0_.refs_1_, bf16[64,4096]{1,0:T(8,128)(2,1)} %collective-permute-done.10.refs_0_.refs_1_, bf16[64,4096]{1,0:T(8,128)(2,1)} %collective-permute-done.11.refs_2_.refs_3_, ...), custom_call_target="tpu_custom_call" | custom-call | flops 1610612736 | bytes 14680064 | tf_op jit(solution)/shard_map/hidden/pallas_call | solution.py:103
  105.4 5.5 %collective-permute-done.15.refs_2_.refs_3_ = bf16[64,4096]{1,0:T(8,128)(2,1)S(1)} collective-permute-done((bf16[64,4096]{1,0:T(8,128)(2,1)}, bf16[64,4096]{1,0:T(8,128)(2,1)S(1)}, u32[]{:S(2)}, u32[]{:S(2)}) %collective-permute-start.15) | collective-permute-done | bytes 524320 | tf_op jit(solution)/shard_map/ppermute | solution.py:33
  110.9 5.2 %hidden.7.refs_4_ = bf16[64,768]{1,0:T(8,128)(2,1)S(1)} custom-call(s32[52]{0:T(128)S(1)} %concatenate.7.table, bf16[64,4096]{1,0:T(8,128)(2,1)S(1)} %copy-done.10, bf16[64,4096]{1,0:T(8,128)(2,1)S(1)} %copy-done.10, bf16[64,4096]{1,0:T(8,128)(2,1)S(1)} %collective-permute-done.15.refs_2_.refs_3_, ...), custom_call_target="tpu_custom_call" | custom-call | flops 805306368 | bytes 13631488 | tf_op jit(solution)/shard_map/hidden/pallas_call | solution.py:103
  116.1 2.8 %collective-permute-start.20 = (bf16[64,768]{1,0:T(8,128)(2,1)S(1)}, bf16[64,768]{1,0:T(8,128)(2,1)S(1)}, u32[]{:S(2)}, u32[]{:S(2)}) collective-permute-start(bf16[64,768]{1,0:T(8,128)(2,1)S(1)} %get-tuple-element.26.refs_3_), channel_id=1, source_target_pairs={{0,6},{2,8},{4,10},{6,12},{8,14},{10,0},{12,2},{14,4},{16,22},{18,... | collective-permute-start | bytes 294920 | tf_op jit(solution)/shard_map/ppermute | solution.py:22
  118.9 3.0 %collective-permute-start.22 = (bf16[64,768]{1,0:T(8,128)(2,1)S(1)}, bf16[64,768]{1,0:T(8,128)(2,1)S(1)}, u32[]{:S(2)}, u32[]{:S(2)}) collective-permute-start(bf16[64,768]{1,0:T(8,128)(2,1)S(1)} %get-tuple-element.24.refs_1_), channel_id=1, source_target_pairs={{0,2},{2,4},{4,6},{6,8},{8,10},{10,12},{12,14},{14,0},{16,18},{18,... | collective-permute-start | bytes 294920 | tf_op jit(solution)/shard_map/ppermute | solution.py:22
  121.9 2.9 %collective-permute-done.19.refs_4_ = bf16[64,768]{1,0:T(8,128)(2,1)S(1)} collective-permute-done((bf16[64,768]{1,0:T(8,128)(2,1)S(1)}, bf16[64,768]{1,0:T(8,128)(2,1)S(1)}, u32[]{:S(2)}, u32[]{:S(2)}) %collective-permute-start.19) | collective-permute-done | bytes 98336 | tf_op jit(solution)/shard_map/ppermute | solution.py:22
  124.8 1.1 collective-permute-done.20.refs_5_
  126.0 2.8 %collective-permute-done.21.refs_6_ = bf16[64,768]{1,0:T(8,128)(2,1)S(1)} collective-permute-done((bf16[64,768]{1,0:T(8,128)(2,1)S(1)}, bf16[64,768]{1,0:T(8,128)(2,1)S(1)}, u32[]{:S(2)}, u32[]{:S(2)}) %collective-permute-start.21) | collective-permute-done | bytes 98336 | tf_op jit(solution)/shard_map/ppermute | solution.py:22
  128.8 3.5 %collective-permute-done.22.refs_7_ = bf16[64,768]{1,0:T(8,128)(2,1)S(1)} collective-permute-done((bf16[64,768]{1,0:T(8,128)(2,1)S(1)}, bf16[64,768]{1,0:T(8,128)(2,1)S(1)}, u32[]{:S(2)}, u32[]{:S(2)}) %collective-permute-start.22) | collective-permute-done | bytes 98336 | tf_op jit(solution)/shard_map/ppermute | solution.py:22
  133.1 4.8 %collective-permute-start.24 = (bf16[64,768]{1,0:T(8,128)(2,1)S(1)}, bf16[64,768]{1,0:T(8,128)(2,1)S(1)}, u32[]{:S(2)}, u32[]{:S(2)}) collective-permute-start(bf16[64,768]{1,0:T(8,128)(2,1)S(1)} %get-tuple-element.32.last), channel_id=1, source_target_pairs={{0,240},{2,242},{4,244},{6,246},{8,248},{10,250},{12,252},{14,254}... | collective-permute-start | bytes 294920 | tf_op jit(solution)/shard_map/ppermute | solution.py:27
  137.9 2.0 %collective-permute-done.23.came_last = bf16[64,768]{1,0:T(8,128)(2,1)S(1)} collective-permute-done((bf16[64,768]{1,0:T(8,128)(2,1)S(1)}, bf16[64,768]{1,0:T(8,128)(2,1)S(1)}, u32[]{:S(2)}, u32[]{:S(2)}) %collective-permute-start.23) | collective-permute-done | bytes 98336 | tf_op jit(solution)/shard_map/ppermute | solution.py:27
  140.7 1.0 collective-permute-start.25
  141.7 1.8 %collective-permute-start.26 = (bf16[64,768]{1,0:T(8,128)(2,1)S(1)}, bf16[64,768]{1,0:T(8,128)(2,1)S(1)}, u32[]{:S(2)}, u32[]{:S(2)}) collective-permute-start(bf16[64,768]{1,0:T(8,128)(2,1)S(1)} %get-tuple-element.35), channel_id=1, source_target_pairs={{0,12},{2,14},{4,0},{6,2},{8,4},{10,6},{12,8},{14,10},{16,28},{18,... | collective-permute-start | bytes 294920 | tf_op jit(solution)/shard_map/ppermute | solution.py:22
  143.5 2.9 %collective-permute-start.27 = (bf16[64,768]{1,0:T(8,128)(2,1)S(1)}, bf16[64,768]{1,0:T(8,128)(2,1)S(1)}, u32[]{:S(2)}, u32[]{:S(2)}) collective-permute-start(bf16[64,768]{1,0:T(8,128)(2,1)S(1)} %get-tuple-element.36), channel_id=1, source_target_pairs={{0,10},{2,12},{4,14},{6,0},{8,2},{10,4},{12,6},{14,8},{16,26},{18,... | collective-permute-start | bytes 294920 | tf_op jit(solution)/shard_map/ppermute | solution.py:22
  146.4 2.7 %collective-permute-start.28 = (bf16[64,768]{1,0:T(8,128)(2,1)S(1)}, bf16[64,768]{1,0:T(8,128)(2,1)S(1)}, u32[]{:S(2)}, u32[]{:S(2)}) collective-permute-start(bf16[64,768]{1,0:T(8,128)(2,1)S(1)} %get-tuple-element.37), channel_id=1, source_target_pairs={{0,8},{2,10},{4,12},{6,14},{8,0},{10,2},{12,4},{14,6},{16,24},{18,... | collective-permute-start | bytes 294920 | tf_op jit(solution)/shard_map/ppermute | solution.py:22
  149.5 1.9 %collective-permute-start.30 = (bf16[64,768]{1,0:T(8,128)(2,1)S(1)}, bf16[64,768]{1,0:T(8,128)(2,1)S(1)}, u32[]{:S(2)}, u32[]{:S(2)}) collective-permute-start(bf16[64,768]{1,0:T(8,128)(2,1)S(1)} %get-tuple-element.39), channel_id=1, source_target_pairs={{0,4},{2,6},{4,8},{6,10},{8,12},{10,14},{12,0},{14,2},{16,20},{18,... | collective-permute-start | bytes 294920 | tf_op jit(solution)/shard_map/ppermute | solution.py:22
  152.2 4.5 %collective-permute-done.28.refs_12_ = bf16[64,768]{1,0:T(8,128)(2,1)S(1)} collective-permute-done((bf16[64,768]{1,0:T(8,128)(2,1)S(1)}, bf16[64,768]{1,0:T(8,128)(2,1)S(1)}, u32[]{:S(2)}, u32[]{:S(2)}) %collective-permute-start.28) | collective-permute-done | bytes 98336 | tf_op jit(solution)/shard_map/ppermute | solution.py:22
  156.7 0.9 collective-permute-done.29.refs_13_
  158.1 4.0 %collective-permute-done.31.refs_15_ = bf16[64,768]{1,0:T(8,128)(2,1)S(1)} collective-permute-done((bf16[64,768]{1,0:T(8,128)(2,1)S(1)}, bf16[64,768]{1,0:T(8,128)(2,1)S(1)}, u32[]{:S(2)}, u32[]{:S(2)}) %collective-permute-start.31) | collective-permute-done | bytes 98336 | tf_op jit(solution)/shard_map/ppermute | solution.py:22
  162.2 1.9 %correlate.2 = f32[384,768]{1,0:T(8,128)S(1)} custom-call(s32[52]{0:T(128)S(1)} %concatenate.7.table, bf16[64,768]{1,0:T(8,128)(2,1)S(1)} %get-tuple-element.23.refs_0_, bf16[64,768]{1,0:T(8,128)(2,1)S(1)} %get-tuple-element.24.refs_1_, bf16[64,768]{1,0:T(8,128)(2,1)S(1)} %get-tuple-element.25.refs_2_, bf16[64,768]{1,0:T(8,128)(2,1)S(1)} %get-tuple-element.26.refs_3_, ...), custom_call_target="tpu_custom_call" | custom-call | flops 301989888 | bytes 1572864 | tf_op jit(solution)/shard_map/correlate/pallas_call | solution.py:197
  164.0 6.6 %collective-permute-start.32 = (f32[384,768]{1,0:T(8,128)S(1)}, f32[384,768]{1,0:T(8,128)S(1)}, u32[]{:S(2)}, u32[]{:S(2)}) collective-permute-start(f32[384,768]{1,0:T(8,128)S(1)} %correlate.2), channel_id=1, source_target_pairs={{0,1},{1,0},{2,3},{3,2},{4,5},{5,4},{6,7},{7,6},{8,9},{9,8},{10,11... | collective-permute-start | bytes 3538952 | tf_op jit(solution)/shard_map/ppermute | solution.py:37
  170.6 2.5 %collective-permute-done.32.refs_16_ = f32[384,768]{1,0:T(8,128)S(1)} collective-permute-done((f32[384,768]{1,0:T(8,128)S(1)}, f32[384,768]{1,0:T(8,128)S(1)}, u32[]{:S(2)}, u32[]{:S(2)}) %collective-permute-start.32) | collective-permute-done | bytes 1179680 | tf_op jit(solution)/shard_map/ppermute | solution.py:37
  173.1 2.9 %correlate.3 = f32[384,768]{1,0:T(8,128)} custom-call(s32[52]{0:T(128)S(1)} %concatenate.7.table, bf16[64,768]{1,0:T(8,128)(2,1)S(1)} %get-tuple-element.23.refs_0_, bf16[64,768]{1,0:T(8,128)(2,1)S(1)} %get-tuple-element.24.refs_1_, bf16[64,768]{1,0:T(8,128)(2,1)S(1)} %get-tuple-element.25.refs_2_, bf16[64,768]{1,0:T(8,128)(2,1)S(1)} %get-tuple-element.26.refs_3_, ...), custom_call_target="tpu_custom_call" | custom-call | flops 301989888 | bytes 1572864 | tf_op jit(solution)/shard_map/correlate/pallas_call | solution.py:197
  (59 shorter events, 10.5 us)
Async XLA Ops:
  0.0 57.1 %collective-permute-start.4 = (bf16[2048,768]{1,0:T(8,128)(2,1)}, bf16[2048,768]{1,0:T(8,128)(2,1)S(1)}, u32[]{:S(2)}, u32[]{:S(2)}) collective-permute-start(bf16[2048,768]{1,0:T(8,128)(2,1)} %bitcast.15), channel_id=1, source_target_pairs={{0,1},{1,0},{2,3},{3,2},{4,5},{5,4},{6,7},{7,6},{8,9},{9,8},{10,11... | collective-permute-start | bytes 9437192 | tf_op jit(solution)/shard_map/ppermute | solution.py:37
  3.2 56.7 %collective-permute-start.5 = (bf16[2048,768]{1,0:T(8,128)(2,1)}, bf16[2048,768]{1,0:T(8,128)(2,1)}, u32[]{:S(2)}, u32[]{:S(2)}) collective-permute-start(bf16[2048,768]{1,0:T(8,128)(2,1)} %bitcast.20), channel_id=1, source_target_pairs={{0,1},{1,0},{2,3},{3,2},{4,5},{5,4},{6,7},{7,6},{8,9},{9,8},{10,11... | collective-permute-start | bytes 9437192 | tf_op jit(solution)/shard_map/ppermute | solution.py:37
  3.2 14.9 %collective-permute-start = (bf16[64,4096]{1,0:T(8,128)(2,1)}, bf16[64,4096]{1,0:T(8,128)(2,1)S(1)}, u32[]{:S(2)}, u32[]{:S(2)}) collective-permute-start(bf16[64,4096]{1,0:T(8,128)(2,1)} %bitcast.25), channel_id=1, source_target_pairs={{0,14},{2,0},{4,2},{6,4},{8,6},{10,8},{12,10},{14,12},{16,30},{18,... | collective-permute-start | bytes 1572872 | tf_op jit(solution)/shard_map/ppermute | solution.py:22
  7.1 16.4 %collective-permute-start.2 = (bf16[64,4096]{1,0:T(8,128)(2,1)}, bf16[64,4096]{1,0:T(8,128)(2,1)}, u32[]{:S(2)}, u32[]{:S(2)}) collective-permute-start(bf16[64,4096]{1,0:T(8,128)(2,1)} %bitcast.26), channel_id=1, source_target_pairs={{0,2},{2,4},{4,6},{6,8},{8,10},{10,12},{12,14},{14,0},{16,18},{18,... | collective-permute-start | bytes 1572872 | tf_op jit(solution)/shard_map/ppermute | solution.py:22
  18.2 13.2 %collective-permute-start.6 = (bf16[64,4096]{1,0:T(8,128)(2,1)S(1)}, bf16[64,4096]{1,0:T(8,128)(2,1)}, u32[]{:S(2)}, u32[]{:S(2)}) collective-permute-start(bf16[64,4096]{1,0:T(8,128)(2,1)S(1)} %collective-permute-done.refs_4_.refs_5_), channel_id=1, source_target_pairs={{0,14},{2,0},{4,2},{6,4},{8,6},{10,8},{12,10},{14,12},{16,30},{18,... | collective-permute-start | bytes 1572872 | tf_op jit(solution)/shard_map/ppermute | solution.py:22
  21.5 15.4 %collective-permute-start.1 = (bf16[64,4096]{1,0:T(8,128)(2,1)S(1)}, bf16[64,4096]{1,0:T(8,128)(2,1)S(1)}, u32[]{:S(2)}, u32[]{:S(2)}) collective-permute-start(bf16[64,4096]{1,0:T(8,128)(2,1)S(1)} %collective-permute-done.refs_4_.refs_5_), channel_id=1, source_target_pairs={{0,16},{2,18},{4,20},{6,22},{8,24},{10,26},{12,28},{14,254},{16,32... | collective-permute-start | bytes 1572872 | tf_op jit(solution)/shard_map/ppermute | solution.py:33
  22.7 0.8 copy-start.5
  23.5 14.6 %collective-permute-start.8 = (bf16[64,4096]{1,0:T(8,128)(2,1)}, bf16[64,4096]{1,0:T(8,128)(2,1)}, u32[]{:S(2)}, u32[]{:S(2)}) collective-permute-start(bf16[64,4096]{1,0:T(8,128)(2,1)} %collective-permute-done.2.refs_8_.refs_9_), channel_id=1, source_target_pairs={{0,2},{2,4},{4,6},{6,8},{8,10},{10,12},{12,14},{14,0},{16,18},{18,... | collective-permute-start | bytes 1572872 | tf_op jit(solution)/shard_map/ppermute | solution.py:22
  31.3 12.8 %collective-permute-start.10 = (bf16[64,4096]{1,0:T(8,128)(2,1)}, bf16[64,4096]{1,0:T(8,128)(2,1)}, u32[]{:S(2)}, u32[]{:S(2)}) collective-permute-start(bf16[64,4096]{1,0:T(8,128)(2,1)} %collective-permute-done.6.refs_0_.refs_1_), channel_id=1, source_target_pairs={{0,14},{2,0},{4,2},{6,4},{8,6},{10,8},{12,10},{14,12},{16,30},{18,... | collective-permute-start | bytes 1572872 | tf_op jit(solution)/shard_map/ppermute | solution.py:22
  36.9 0.8 copy-start.7
  37.7 14.6 %collective-permute-start.3 = (bf16[64,4096]{1,0:T(8,128)(2,1)}, bf16[64,4096]{1,0:T(8,128)(2,1)}, u32[]{:S(2)}, u32[]{:S(2)}) collective-permute-start(bf16[64,4096]{1,0:T(8,128)(2,1)} %collective-permute-done.2.refs_8_.refs_9_), channel_id=1, source_target_pairs={{0,16},{2,242},{4,244},{6,246},{8,248},{10,250},{12,252},{14,254},... | collective-permute-start | bytes 1572872 | tf_op jit(solution)/shard_map/ppermute | solution.py:33
  38.1 14.5 %collective-permute-start.12 = (bf16[64,4096]{1,0:T(8,128)(2,1)}, bf16[64,4096]{1,0:T(8,128)(2,1)}, u32[]{:S(2)}, u32[]{:S(2)}) collective-permute-start(bf16[64,4096]{1,0:T(8,128)(2,1)} %collective-permute-done.8.refs_4_.refs_5_), channel_id=1, source_target_pairs={{0,2},{2,4},{4,6},{6,8},{8,10},{10,12},{12,14},{14,0},{16,18},{18,... | collective-permute-start | bytes 1572872 | tf_op jit(solution)/shard_map/ppermute | solution.py:22
  44.1 11.7 %collective-permute-start.14 = (bf16[64,4096]{1,0:T(8,128)(2,1)}, bf16[64,4096]{1,0:T(8,128)(2,1)S(1)}, u32[]{:S(2)}, u32[]{:S(2)}) collective-permute-start(bf16[64,4096]{1,0:T(8,128)(2,1)} %collective-permute-done.10.refs_0_.refs_1_), channel_id=1, source_target_pairs={{0,14},{2,0},{4,2},{6,4},{8,6},{10,8},{12,10},{14,12},{16,30},{18,... | collective-permute-start | bytes 1572872 | tf_op jit(solution)/shard_map/ppermute | solution.py:22
  52.3 22.2 %collective-permute-start.7 = (bf16[64,4096]{1,0:T(8,128)(2,1)}, bf16[64,4096]{1,0:T(8,128)(2,1)}, u32[]{:S(2)}, u32[]{:S(2)}) collective-permute-start(bf16[64,4096]{1,0:T(8,128)(2,1)} %collective-permute-done.6.refs_0_.refs_1_), channel_id=1, source_target_pairs={{0,16},{2,18},{4,20},{6,22},{8,24},{10,26},{12,252},{14,254},{16,3... | collective-permute-start | bytes 1572872 | tf_op jit(solution)/shard_map/ppermute | solution.py:33
  52.6 28.3 %collective-permute-start.9 = (bf16[64,4096]{1,0:T(8,128)(2,1)}, bf16[64,4096]{1,0:T(8,128)(2,1)}, u32[]{:S(2)}, u32[]{:S(2)}) collective-permute-start(bf16[64,4096]{1,0:T(8,128)(2,1)} %collective-permute-done.8.refs_4_.refs_5_), channel_id=1, source_target_pairs={{0,16},{2,18},{4,244},{6,246},{8,248},{10,250},{12,252},{14,254},{... | collective-permute-start | bytes 1572872 | tf_op jit(solution)/shard_map/ppermute | solution.py:33
  55.9 1.2 copy-start.9
  55.9 32.6 %collective-permute-start.11 = (bf16[64,4096]{1,0:T(8,128)(2,1)}, bf16[64,4096]{1,0:T(8,128)(2,1)}, u32[]{:S(2)}, u32[]{:S(2)}) collective-permute-start(bf16[64,4096]{1,0:T(8,128)(2,1)} %collective-permute-done.10.refs_0_.refs_1_), channel_id=1, source_target_pairs={{0,16},{2,18},{4,20},{6,22},{8,24},{10,250},{12,252},{14,254},{16,... | collective-permute-start | bytes 1572872 | tf_op jit(solution)/shard_map/ppermute | solution.py:33
  57.1 42.7 %collective-permute-start.13 = (bf16[64,4096]{1,0:T(8,128)(2,1)}, bf16[64,4096]{1,0:T(8,128)(2,1)}, u32[]{:S(2)}, u32[]{:S(2)}) collective-permute-start(bf16[64,4096]{1,0:T(8,128)(2,1)} %collective-permute-done.12.refs_4_.refs_5_), channel_id=1, source_target_pairs={{0,16},{2,18},{4,20},{6,246},{8,248},{10,250},{12,252},{14,254},{1... | collective-permute-start | bytes 1572872 | tf_op jit(solution)/shard_map/ppermute | solution.py:33
  60.0 50.9 %collective-permute-start.15 = (bf16[64,4096]{1,0:T(8,128)(2,1)}, bf16[64,4096]{1,0:T(8,128)(2,1)S(1)}, u32[]{:S(2)}, u32[]{:S(2)}) collective-permute-start(bf16[64,4096]{1,0:T(8,128)(2,1)} %copy-done.9), channel_id=1, source_target_pairs={{0,16},{2,18},{4,20},{6,22},{8,248},{10,250},{12,252},{14,254},{16... | collective-permute-start | bytes 1572872 | tf_op jit(solution)/shard_map/ppermute | solution.py:33
  61.1 1.9 %copy-start = (bf16[1,2048,768]{2,1,0:T(8,128)(2,1)S(1)}, bf16[1,2048,768]{2,1,0:T(8,128)(2,1)}, u32[]{:S(2)}) copy-start(bf16[1,2048,768]{2,1,0:T(8,128)(2,1)} %param.6) | copy-start | bytes 9437188
  63.0 1.9 %copy-start.2 = (bf16[1,2048,768]{2,1,0:T(8,128)(2,1)S(1)}, bf16[1,2048,768]{2,1,0:T(8,128)(2,1)}, u32[]{:S(2)}) copy-start(bf16[1,2048,768]{2,1,0:T(8,128)(2,1)} %param.7) | copy-start | bytes 9437188
  64.8 1.0 copy-start.4
  65.9 1.0 copy-start.6
  66.9 1.0 copy-start.8
  68.0 12.9 %copy-start.1 = (bf16[1,2048,768]{2,1,0:T(8,128)(2,1)S(1)}, bf16[1,2048,768]{2,1,0:T(8,128)(2,1)}, u32[]{:S(2)}) copy-start(bf16[1,2048,768]{2,1,0:T(8,128)(2,1)} %param.6) | copy-start | bytes 9437188
  68.0 12.9 %copy-start.3 = (bf16[1,2048,768]{2,1,0:T(8,128)(2,1)S(1)}, bf16[1,2048,768]{2,1,0:T(8,128)(2,1)}, u32[]{:S(2)}) copy-start(bf16[1,2048,768]{2,1,0:T(8,128)(2,1)} %param.7) | copy-start | bytes 9437188
  74.5 44.4 %collective-permute-start.16 = (bf16[64,768]{1,0:T(8,128)(2,1)S(1)}, bf16[64,768]{1,0:T(8,128)(2,1)S(1)}, u32[]{:S(2)}, u32[]{:S(2)}) collective-permute-start(bf16[64,768]{1,0:T(8,128)(2,1)S(1)} %get-tuple-element.29.refs_7_), channel_id=1, source_target_pairs={{0,14},{2,0},{4,2},{6,4},{8,6},{10,8},{12,10},{14,12},{16,30},{18,... | collective-permute-start | bytes 294920 | tf_op jit(solution)/shard_map/ppermute | solution.py:22
  86.4 24.4 %copy-start.10 = (bf16[64,4096]{1,0:T(8,128)(2,1)S(1)}, bf16[64,4096]{1,0:T(8,128)(2,1)}, u32[]{:S(2)}) copy-start(bf16[64,4096]{1,0:T(8,128)(2,1)} %copy-done.9) | copy-start | bytes 1572868
  86.4 32.4 %collective-permute-start.17 = (bf16[64,768]{1,0:T(8,128)(2,1)S(1)}, bf16[64,768]{1,0:T(8,128)(2,1)S(1)}, u32[]{:S(2)}, u32[]{:S(2)}) collective-permute-start(bf16[64,768]{1,0:T(8,128)(2,1)S(1)} %get-tuple-element.28.refs_6_), channel_id=1, source_target_pairs={{0,12},{2,14},{4,0},{6,2},{8,4},{10,6},{12,8},{14,10},{16,28},{18,... | collective-permute-start | bytes 294920 | tf_op jit(solution)/shard_map/ppermute | solution.py:22
  105.3 16.6 %collective-permute-start.18 = (bf16[64,768]{1,0:T(8,128)(2,1)S(1)}, bf16[64,768]{1,0:T(8,128)(2,1)S(1)}, u32[]{:S(2)}, u32[]{:S(2)}) collective-permute-start(bf16[64,768]{1,0:T(8,128)(2,1)S(1)} %get-tuple-element.27.refs_5_), channel_id=1, source_target_pairs={{0,10},{2,12},{4,14},{6,0},{8,2},{10,4},{12,6},{14,8},{16,26},{18,... | collective-permute-start | bytes 294920 | tf_op jit(solution)/shard_map/ppermute | solution.py:22
  116.0 8.8 %collective-permute-start.19 = (bf16[64,768]{1,0:T(8,128)(2,1)S(1)}, bf16[64,768]{1,0:T(8,128)(2,1)S(1)}, u32[]{:S(2)}, u32[]{:S(2)}) collective-permute-start(bf16[64,768]{1,0:T(8,128)(2,1)S(1)} %hidden.7.refs_4_), channel_id=1, source_target_pairs={{0,8},{2,10},{4,12},{6,14},{8,0},{10,2},{12,4},{14,6},{16,24},{18,... | collective-permute-start | bytes 294920 | tf_op jit(solution)/shard_map/ppermute | solution.py:22
  116.1 9.8 %collective-permute-start.20 = (bf16[64,768]{1,0:T(8,128)(2,1)S(1)}, bf16[64,768]{1,0:T(8,128)(2,1)S(1)}, u32[]{:S(2)}, u32[]{:S(2)}) collective-permute-start(bf16[64,768]{1,0:T(8,128)(2,1)S(1)} %get-tuple-element.26.refs_3_), channel_id=1, source_target_pairs={{0,6},{2,8},{4,10},{6,12},{8,14},{10,0},{12,2},{14,4},{16,22},{18,... | collective-permute-start | bytes 294920 | tf_op jit(solution)/shard_map/ppermute | solution.py:22
  118.9 9.9 %collective-permute-start.21 = (bf16[64,768]{1,0:T(8,128)(2,1)S(1)}, bf16[64,768]{1,0:T(8,128)(2,1)S(1)}, u32[]{:S(2)}, u32[]{:S(2)}) collective-permute-start(bf16[64,768]{1,0:T(8,128)(2,1)S(1)} %get-tuple-element.25.refs_2_), channel_id=1, source_target_pairs={{0,4},{2,6},{4,8},{6,10},{8,12},{10,14},{12,0},{14,2},{16,20},{18,... | collective-permute-start | bytes 294920 | tf_op jit(solution)/shard_map/ppermute | solution.py:22
  118.9 13.4 %collective-permute-start.22 = (bf16[64,768]{1,0:T(8,128)(2,1)S(1)}, bf16[64,768]{1,0:T(8,128)(2,1)S(1)}, u32[]{:S(2)}, u32[]{:S(2)}) collective-permute-start(bf16[64,768]{1,0:T(8,128)(2,1)S(1)} %get-tuple-element.24.refs_1_), channel_id=1, source_target_pairs={{0,2},{2,4},{4,6},{6,8},{8,10},{10,12},{12,14},{14,0},{16,18},{18,... | collective-permute-start | bytes 294920 | tf_op jit(solution)/shard_map/ppermute | solution.py:22
  133.0 6.9 %collective-permute-start.23 = (bf16[64,768]{1,0:T(8,128)(2,1)S(1)}, bf16[64,768]{1,0:T(8,128)(2,1)S(1)}, u32[]{:S(2)}, u32[]{:S(2)}) collective-permute-start(bf16[64,768]{1,0:T(8,128)(2,1)S(1)} %get-tuple-element.31.nxt), channel_id=1, source_target_pairs={{0,16},{2,18},{4,20},{6,22},{8,24},{10,26},{12,28},{14,30},{16,32}... | collective-permute-start | bytes 294920 | tf_op jit(solution)/shard_map/ppermute | solution.py:27
  133.1 6.8 %collective-permute-start.24 = (bf16[64,768]{1,0:T(8,128)(2,1)S(1)}, bf16[64,768]{1,0:T(8,128)(2,1)S(1)}, u32[]{:S(2)}, u32[]{:S(2)}) collective-permute-start(bf16[64,768]{1,0:T(8,128)(2,1)S(1)} %get-tuple-element.32.last), channel_id=1, source_target_pairs={{0,240},{2,242},{4,244},{6,246},{8,248},{10,250},{12,252},{14,254}... | collective-permute-start | bytes 294920 | tf_op jit(solution)/shard_map/ppermute | solution.py:27
  140.7 8.8 %collective-permute-start.25 = (bf16[64,768]{1,0:T(8,128)(2,1)S(1)}, bf16[64,768]{1,0:T(8,128)(2,1)S(1)}, u32[]{:S(2)}, u32[]{:S(2)}) collective-permute-start(bf16[64,768]{1,0:T(8,128)(2,1)S(1)} %get-tuple-element.34), channel_id=1, source_target_pairs={{0,14},{2,0},{4,2},{6,4},{8,6},{10,8},{12,10},{14,12},{16,30},{18,... | collective-permute-start | bytes 294920 | tf_op jit(solution)/shard_map/ppermute | solution.py:22
  141.7 9.7 %collective-permute-start.26 = (bf16[64,768]{1,0:T(8,128)(2,1)S(1)}, bf16[64,768]{1,0:T(8,128)(2,1)S(1)}, u32[]{:S(2)}, u32[]{:S(2)}) collective-permute-start(bf16[64,768]{1,0:T(8,128)(2,1)S(1)} %get-tuple-element.35), channel_id=1, source_target_pairs={{0,12},{2,14},{4,0},{6,2},{8,4},{10,6},{12,8},{14,10},{16,28},{18,... | collective-permute-start | bytes 294920 | tf_op jit(solution)/shard_map/ppermute | solution.py:22
  143.5 8.6 %collective-permute-start.27 = (bf16[64,768]{1,0:T(8,128)(2,1)S(1)}, bf16[64,768]{1,0:T(8,128)(2,1)S(1)}, u32[]{:S(2)}, u32[]{:S(2)}) collective-permute-start(bf16[64,768]{1,0:T(8,128)(2,1)S(1)} %get-tuple-element.36), channel_id=1, source_target_pairs={{0,10},{2,12},{4,14},{6,0},{8,2},{10,4},{12,6},{14,8},{16,26},{18,... | collective-permute-start | bytes 294920 | tf_op jit(solution)/shard_map/ppermute | solution.py:22
  146.4 10.3 %collective-permute-start.28 = (bf16[64,768]{1,0:T(8,128)(2,1)S(1)}, bf16[64,768]{1,0:T(8,128)(2,1)S(1)}, u32[]{:S(2)}, u32[]{:S(2)}) collective-permute-start(bf16[64,768]{1,0:T(8,128)(2,1)S(1)} %get-tuple-element.37), channel_id=1, source_target_pairs={{0,8},{2,10},{4,12},{6,14},{8,0},{10,2},{12,4},{14,6},{16,24},{18,... | collective-permute-start | bytes 294920 | tf_op jit(solution)/shard_map/ppermute | solution.py:22
  149.1 8.5 %collective-permute-start.29 = (bf16[64,768]{1,0:T(8,128)(2,1)S(1)}, bf16[64,768]{1,0:T(8,128)(2,1)S(1)}, u32[]{:S(2)}, u32[]{:S(2)}) collective-permute-start(bf16[64,768]{1,0:T(8,128)(2,1)S(1)} %get-tuple-element.38), channel_id=1, source_target_pairs={{0,6},{2,8},{4,10},{6,12},{8,14},{10,0},{12,2},{14,4},{16,22},{18,... | collective-permute-start | bytes 294920 | tf_op jit(solution)/shard_map/ppermute | solution.py:22
  149.5 8.6 %collective-permute-start.30 = (bf16[64,768]{1,0:T(8,128)(2,1)S(1)}, bf16[64,768]{1,0:T(8,128)(2,1)S(1)}, u32[]{:S(2)}, u32[]{:S(2)}) collective-permute-start(bf16[64,768]{1,0:T(8,128)(2,1)S(1)} %get-tuple-element.39), channel_id=1, source_target_pairs={{0,4},{2,6},{4,8},{6,10},{8,12},{10,14},{12,0},{14,2},{16,20},{18,... | collective-permute-start | bytes 294920 | tf_op jit(solution)/shard_map/ppermute | solution.py:22
  151.4 10.8 %collective-permute-start.31 = (bf16[64,768]{1,0:T(8,128)(2,1)S(1)}, bf16[64,768]{1,0:T(8,128)(2,1)S(1)}, u32[]{:S(2)}, u32[]{:S(2)}) collective-permute-start(bf16[64,768]{1,0:T(8,128)(2,1)S(1)} %get-tuple-element.40), channel_id=1, source_target_pairs={{0,2},{2,4},{4,6},{6,8},{8,10},{10,12},{12,14},{14,0},{16,18},{18,... | collective-permute-start | bytes 294920 | tf_op jit(solution)/shard_map/ppermute | solution.py:22
  164.0 9.0 %collective-permute-start.32 = (f32[384,768]{1,0:T(8,128)S(1)}, f32[384,768]{1,0:T(8,128)S(1)}, u32[]{:S(2)}, u32[]{:S(2)}) collective-permute-start(f32[384,768]{1,0:T(8,128)S(1)} %correlate.2), channel_id=1, source_target_pairs={{0,1},{1,0},{2,3},{3,2},{4,5},{5,4},{6,7},{7,6},{8,9},{9,8},{10,11... | collective-permute-start | bytes 3538952 | tf_op jit(solution)/shard_map/ppermute | solution.py:37
where the time goes:
time: 177 us; the launch traced here: 176 us
  waiting for transfers between devices  76.4 us (43%)
  starting transfers between devices  57.7 us (33%)
  Pallas kernels  29.1 us (16%)
  local copies, waits for them, and re-layouts  10.1 us (6%)
  other arithmetic  2.53 us (1%)
    ppermute x21, waiting for transfers between devices, along_line(): return lax.ppermute(value, 'expert', pairs)  48.3 us
    ppermute x21, starting transfers between devices, along_line(): return lax.ppermute(value, 'expert', pairs)  38.3 us
    ppermute x7, waiting for transfers between devices, to_side(): lax.ppermute(value, 'expert', [(i, (i + side(i)) % count) for i in range(...  23.7 us
    pallas_call x4, Pallas kernels, hidden_of(): pl.pallas_call(functools.partial(hidden_kernel, group), out_shape=[jax.Sh...  22.8 us
    ppermute x3, starting transfers between devices, swap_cores(): return lax.ppermute(value, 'row', [(0, 1), (1, 0)])  9.8 us
    unnamed x22, local copies, waits for them, and re-layouts  8.51 us
    ppermute x2, starting transfers between devices, to_line(): lax.ppermute(value, 'expert', [(i, (i + step * LINE) % count) for i in ra...  4.86 us
    pallas_call x2, Pallas kernels, correlate(): pl.pallas_call(functools.partial(correlate_kernel, add), out_shape=jax.Sh...  4.78 us
  transfers between devices with their start and end apart: 33, of which 21 were waited for; matrix products, arithmetic and copies ran while one was open for 2% of the time, Pallas kernels for 13%

commit v1 on v0

--- a/solution.py
+++ b/solution.py
@@ -10,8 +10,6 @@
 ROWS = 128
 LINE = 8
 TILE = 512
-OFFSETS = (1, 7, 2, 6, 3, 5, 4)
-GROUPS = ((0, 1, 7), (2, 6), (3, 5), (4,))
 
 NEAR, DOM, CORE, LINE_AT, PLACE, SIZE = 0, 24, 48, 49, 50, 51
 
@@ -22,19 +20,17 @@
     return lax.ppermute(value, "expert", pairs)
 
 
-def to_line(value, step):
+def shift(value, step):
     count = lax.axis_size("expert")
-    return lax.ppermute(value, "expert", [(i, (i + step * LINE) % count) for i in range(count)])
-
-
-def to_side(value, offset):
-    count = lax.axis_size("expert")
-    side = lambda i: LINE if i % LINE + offset < LINE else -LINE
-    return lax.ppermute(value, "expert", [(i, (i + side(i)) % count) for i in range(count)])
+    return lax.ppermute(value, "expert", [(i, (i + step) % count) for i in range(count)])
 
 
 def swap_cores(value):
     return lax.ppermute(value, "row", [(0, 1), (1, 0)])
+
+
+def after(*values):
+    return lax.optimization_barrier(values)
 
 
 def scalars(cluster, dominant_rank):
@@ -56,6 +52,12 @@
     return table[NEAR + LINE * line + k]
 
 
+def cluster_at(table, k):
+    if k >= 0:
+        return jnp.where(table[PLACE] + k < LINE, near(table, 1, k), near(table, 2, k))
+    return jnp.where(table[PLACE] + k >= 0, near(table, 1, k + LINE), near(table, 0, k + LINE))
+
+
 def hidden_kernel(group, table, *refs):
     many = len(group)
     xs, weights = refs[: 4 * many], refs[4 * many : 4 * many + 4]
@@ -71,8 +73,8 @@
     for side in range(2):
         rows = []
         for n, k in enumerate(group):
-            ring, beside = xs[4 * n + side], xs[4 * n + 2 + side]
-            rows.append(ring[...] if k == 0 else jnp.where(near(table, 1, k) == mine, ring[...], beside[...]))
+            ahead, behind = xs[4 * n + side], xs[4 * n + 2 + side]
+            rows.append(ahead[...] if k == 0 else jnp.where(cluster_at(table, k) == mine, ahead[...], behind[...]))
         rows = jnp.concatenate(rows, axis=0)
         gate_sum[...] += jnp.dot(rows, weights[side][...], preferred_element_type=jnp.float32)
         up_sum[...] += jnp.dot(rows, weights[2 + side][...], preferred_element_type=jnp.float32)
@@ -84,12 +86,12 @@
         part = outs[0].shape[0]
         for n, k in enumerate(group):
             block = value[n * part : (n + 1) * part].astype(jnp.bfloat16)
-            inside = (near(table, 0, k) == mine) | (near(table, 1, k) == mine) | (near(table, 2, k) == mine)
+            inside = (cluster_at(table, k) == mine) | (cluster_at(table, k - LINE if k else 0) == mine)
             outs[n][...] = jnp.where(inside, block, jnp.zeros_like(block))
 
 
-def hidden_of(table, group, ring, beside, weights):
-    part, width = ring[0].shape
+def hidden_of(table, group, ahead, behind, weights):
+    part, width = ahead[0].shape
     half, units = weights[0].shape
     steps = half // TILE
     own_half = pl.BlockSpec((part, TILE), lambda i, t: (0, t[CORE] * steps + i))
@@ -97,7 +99,7 @@
     weight = pl.BlockSpec((TILE, units), lambda i, t: (i, 0))
     args, specs = [], []
     for k in group:
-        args += [ring[k], ring[k], beside.get(k, ring[k]), beside.get(k, ring[k])]
+        args += [ahead[k], ahead[k], behind[k], behind[k]]
         specs += [own_half, other_half, own_half, other_half]
     rows = part * len(group)
     return pl.pallas_call(
@@ -155,6 +157,22 @@
             @pl.when(source == n)
             def _():
                 outs[away][...] = ref[...]
+
+
+def forward_kernel(table, back_three, ahead_six, ahead_three, back_six, to_next, to_last):
+    def pick(out, far, near_by, receiver):
+        wants_far = cluster_at(table, 6 * receiver) == cluster_at(table, receiver)
+
+        @pl.when(wants_far)
+        def _():
+            out[...] = far[...]
+
+        @pl.when(jnp.logical_not(wants_far))
+        def _():
+            out[...] = near_by[...]
+
+    pick(to_next, ahead_six, back_three, 1)
+    pick(to_last, back_six, ahead_three, -1)
 
 
 def choose(kernel, table, arrays, outs, name):
@@ -214,25 +232,36 @@
 def per_device(calib_rows, gate_weight, up_weight, cluster, dominant_rank):
     table = scalars(cluster, dominant_rank)
 
-    ring, beside = {0: calib_rows[0]}, {}
-    for step in range(1, LINE // 2 + 1):
-        ring[step] = along_line(ring[step - 1], 1)
-        if step < LINE // 2:
-            ring[LINE - step] = along_line(ring[(LINE - step + 1) % LINE], -1)
     gate, up = gate_weight[0], up_weight[0]
-    weights = (gate, swap_cores(gate), up, swap_cores(up))
+    gate_other, up_other = swap_cores(gate), swap_cores(up)
+    own = calib_rows[0]
+    ahead, behind = {0: own}, {0: own}
+    ahead[1], behind[7] = shift(own, -1), shift(own, 1)
+    ahead[1], behind[7], gate_other, up_other = after(ahead[1], behind[7], gate_other, up_other)
+    weights = (gate, gate_other, up, up_other)
+    ahead[2], behind[6] = shift(ahead[1], -1), shift(behind[7], 1)
+    behind[1], ahead[7] = shift(ahead[1], LINE), shift(behind[7], -LINE)
+    ahead[2], behind[6], behind[1], ahead[7] = after(ahead[2], behind[6], behind[1], ahead[7])
+    ahead[3], behind[5] = shift(ahead[2], -1), shift(behind[6], 1)
+    behind[2], ahead[6] = shift(ahead[2], LINE), shift(behind[6], -LINE)
 
     hidden, returned = {}, {}
-    for group in GROUPS:
-        for k in group:
-            if k:
-                beside[k] = to_side(ring[k], k)
-        for k, block in zip(group, hidden_of(table, group, ring, beside, weights)):
+
+    def compute(group):
+        for k, block in zip(group, hidden_of(table, group, ahead, behind, weights)):
             hidden[k] = block
             returned[(LINE - k) % LINE] = along_line(block, LINE - k) if k else block
 
+    compute((0, 1, 7))
+    ahead[3], behind[5], ahead[6], behind[2], hidden[0] = after(ahead[3], behind[5], ahead[6], behind[2], hidden[0])
+    to_next, to_last = choose(forward_kernel, table, [behind[5], ahead[6], ahead[3], behind[2]], 2, "forward")
+    from_last, from_next = shift(to_next, 1), shift(to_last, -1)
+    ahead[4], behind[3], behind[4], ahead[5] = from_next, from_next, from_last, from_last
+    compute((2, 6))
+    compute((3, 5, 4))
+
     shares = choose(share_kernel, table, [returned[k] for k in range(LINE)], 3, "share")
-    came_last, came_next = to_line(shares[1], 1), to_line(shares[2], -1)
+    came_last, came_next = shift(shares[1], LINE), shift(shares[2], -LINE)
     chunks = choose(send_kernel, table, [*shares, came_last, came_next], LINE, "send")
     panel = {k: along_line(chunks[(-k) % LINE], k) if k else chunks[0] for k in range(LINE)}
 

time: 177 us -> 166 us (0.938)
  waiting for transfers between devices: 76.4 us -> 50 us
  starting transfers between devices: 57.7 us -> 80 us
  local copies, waits for them, and re-layouts: 10.1 us -> 6.2 us
  Pallas kernels: 29.1 us -> 26.3 us
    ppermute x21 -> x14, waiting for transfers between devices: 48.3 us -> 11.2 us  [along_line(): return lax.ppermute(value, 'expert', pairs)]
    ppermute x9 -> x14, starting transfers between devices: 9.61 us -> 40.7 us  [shift(): lax.ppermute(value, 'expert', [(i, (i + step) % count) for i in range(cou...]
    ppermute x21 -> x14, starting transfers between devices: 38.3 us -> 25.4 us  [along_line(): return lax.ppermute(value, 'expert', pairs)]
    ppermute x9 -> x14, waiting for transfers between devices: 25.7 us -> 36.3 us  [shift(): lax.ppermute(value, 'expert', [(i, (i + step) % count) for i in range(cou...]
    pallas_call x4 -> x3, Pallas kernels: 22.8 us -> 18.5 us  [hidden_of(): pl.pallas_call(functools.partial(hidden_kernel, group), out_shape=[jax.Sh...]
    ppermute x3, starting transfers between devices: 9.8 us -> 13.9 us  [swap_cores(): return lax.ppermute(value, 'row', [(0, 1), (1, 0)])]
    unnamed x22 -> x10, local copies, waits for them, and re-layouts: 8.51 us -> 4.83 us
  transfers between devices with their start and end apart: 33 -> 31, of which waited for: 21 -> 15; matrix products, arithmetic and copies ran while one was open for 2% -> 2% of each run, Pallas kernels for 13% -> 11%
where the time goes in v1:
time: 166 us; the launch traced here: 165 us
  starting transfers between devices  80 us (48%)
  waiting for transfers between devices  50 us (30%)
  Pallas kernels  26.3 us (16%)
  local copies, waits for them, and re-layouts  6.2 us (4%)
  other arithmetic  2.53 us (2%)
    ppermute x14, starting transfers between devices, shift(): lax.ppermute(value, 'expert', [(i, (i + step) % count) for i in range(cou...  40.7 us
    ppermute x14, waiting for transfers between devices, shift(): lax.ppermute(value, 'expert', [(i, (i + step) % count) for i in range(cou...  36.3 us
    ppermute x14, starting transfers between devices, along_line(): return lax.ppermute(value, 'expert', pairs)  25.4 us
    pallas_call x3, Pallas kernels, hidden_of(): pl.pallas_call(functools.partial(hidden_kernel, group), out_shape=[jax.Sh...  18.5 us
    ppermute x3, starting transfers between devices, swap_cores(): return lax.ppermute(value, 'row', [(0, 1), (1, 0)])  13.9 us
    ppermute x14, waiting for transfers between devices, along_line(): return lax.ppermute(value, 'expert', pairs)  11.2 us
    unnamed x10, local copies, waits for them, and re-layouts  4.83 us
    pallas_call x2, Pallas kernels, correlate(): pl.pallas_call(functools.partial(correlate_kernel, add), out_shape=jax.Sh...  4.76 us
  transfers between devices with their start and end apart: 31, of which 15 were waited for; matrix products, arithmetic and copies ran while one was open for 2% of the time, Pallas kernels for 11%

profile of v1, /device:TPU:1, one launch (start us, length us, event | category | flops | bytes accessed | tf_op | source)
XLA Modules:
  0.0 165.3 jit_solution(17904333123850149787)
XLA Ops:
  0.0 3.2 %collective-permute-start.2 = (bf16[2048,768]{1,0:T(8,128)(2,1)}, bf16[2048,768]{1,0:T(8,128)(2,1)S(1)}, u32[]{:S(2)}, u32[]{:S(2)}) collective-permute-start(bf16[2048,768]{1,0:T(8,128)(2,1)} %bitcast.15), channel_id=1, source_target_pairs={{0,1},{1,0},{2,3},{3,2},{4,5},{5,4},{6,7},{7,6},{8,9},{9,8},{10,11... | collective-permute-start | bytes 9437192 | tf_op jit(solution)/shard_map/ppermute | solution.py:29
  3.2 8.5 %collective-permute-start = (bf16[64,4096]{1,0:T(8,128)(2,1)}, bf16[64,4096]{1,0:T(8,128)(2,1)}, u32[]{:S(2)}, u32[]{:S(2)}) collective-permute-start(bf16[64,4096]{1,0:T(8,128)(2,1)} %bitcast.24), channel_id=1, source_target_pairs={{0,254},{2,0},{4,2},{6,4},{8,6},{10,8},{12,10},{14,12},{16,14},{18... | collective-permute-start | bytes 1572872 | tf_op jit(solution)/shard_map/ppermute | solution.py:25
  11.7 12.1 %collective-permute-done.1.refs_10_.refs_11_ = bf16[64,4096]{1,0:T(8,128)(2,1)} collective-permute-done((bf16[64,4096]{1,0:T(8,128)(2,1)}, bf16[64,4096]{1,0:T(8,128)(2,1)}, u32[]{:S(2)}, u32[]{:S(2)}) %collective-permute-start.1) | collective-permute-done | bytes 524320 | tf_op jit(solution)/shard_map/ppermute | solution.py:25
  24.0 6.6 %collective-permute-start.4 = (bf16[64,4096]{1,0:T(8,128)(2,1)}, bf16[64,4096]{1,0:T(8,128)(2,1)}, u32[]{:S(2)}, u32[]{:S(2)}) collective-permute-start(bf16[64,4096]{1,0:T(8,128)(2,1)} %collective-permute-done.refs_4_.refs_5_), channel_id=1, source_target_pairs={{0,254},{2,0},{4,2},{6,4},{8,6},{10,8},{12,10},{14,12},{16,14},{18... | collective-permute-start | bytes 1572872 | tf_op jit(solution)/shard_map/ppermute | solution.py:25
  30.6 1.4 collective-permute-start.7
  31.9 0.8 select_reduce_fusion
  32.7 0.9 convert_reduce_fusion.1
  33.7 6.2 %collective-permute-done.6.refs_6_.refs_7_ = bf16[64,4096]{1,0:T(8,128)(2,1)} collective-permute-done((bf16[64,4096]{1,0:T(8,128)(2,1)}, bf16[64,4096]{1,0:T(8,128)(2,1)}, u32[]{:S(2)}, u32[]{:S(2)}) %collective-permute-start.6) | collective-permute-done | bytes 524320 | tf_op jit(solution)/shard_map/ppermute | solution.py:25
  40.0 0.8 collective-permute-done.4.refs_0_.refs_1_
  40.8 1.9 %collective-permute-done.7.refs_8_.refs_9_ = bf16[64,4096]{1,0:T(8,128)(2,1)} collective-permute-done((bf16[64,4096]{1,0:T(8,128)(2,1)}, bf16[64,4096]{1,0:T(8,128)(2,1)}, u32[]{:S(2)}, u32[]{:S(2)}) %collective-permute-start.7) | collective-permute-done | bytes 524320 | tf_op jit(solution)/shard_map/ppermute | solution.py:25
  42.6 6.3 %collective-permute-done.5.refs_6_.refs_7_ = bf16[64,4096]{1,0:T(8,128)(2,1)} collective-permute-done((bf16[64,4096]{1,0:T(8,128)(2,1)}, bf16[64,4096]{1,0:T(8,128)(2,1)}, u32[]{:S(2)}, u32[]{:S(2)}) %collective-permute-start.5) | collective-permute-done | bytes 524320 | tf_op jit(solution)/shard_map/ppermute | solution.py:25
  49.0 8.6 %collective-permute-start.8 = (bf16[64,4096]{1,0:T(8,128)(2,1)}, bf16[64,4096]{1,0:T(8,128)(2,1)}, u32[]{:S(2)}, u32[]{:S(2)}) collective-permute-start(bf16[64,4096]{1,0:T(8,128)(2,1)} %collective-permute-done.4.refs_0_.refs_1_), channel_id=1, source_target_pairs={{0,254},{2,0},{4,2},{6,4},{8,6},{10,8},{12,10},{14,12},{16,14},{18... | collective-permute-start | bytes 1572872 | tf_op jit(solution)/shard_map/ppermute | solution.py:25
  57.6 1.5 collective-permute-start.10
  59.0 0.7 pad_add_fusion
  60.0 0.5 slice.9
  60.5 0.6 concatenate.7.table
  61.2 1.9 %copy-done = bf16[1,2048,768]{2,1,0:T(8,128)(2,1)S(1)} copy-done((bf16[1,2048,768]{2,1,0:T(8,128)(2,1)S(1)}, bf16[1,2048,768]{2,1,0:T(8,128)(2,1)}, u32[]{:S(2)}) %copy-start) | copy-done | bytes 3145752
  63.1 1.9 %copy-done.2 = bf16[1,2048,768]{2,1,0:T(8,128)(2,1)S(1)} copy-done((bf16[1,2048,768]{2,1,0:T(8,128)(2,1)S(1)}, bf16[1,2048,768]{2,1,0:T(8,128)(2,1)}, u32[]{:S(2)}) %copy-start.2) | copy-done | bytes 3145752
  65.0 1.0 copy-done.4
  66.0 6.7 %hidden.3 = (bf16[64,768]{1,0:T(8,128)(2,1)S(1)}, bf16[64,768]{1,0:T(8,128)(2,1)S(1)}, bf16[64,768]{1,0:T(8,128)(2,1)S(1)}) custom-call(s32[52]{0:T(128)S(1)} %concatenate.7.table, bf16[64,4096]{1,0:T(8,128)(2,1)S(1)} %bitcast.25, bf16[64,4096]{1,0:T(8,128)(2,1)S(1)} %bitcast.26, bf16[64,4096]{1,0:T(8,128)(2,1)S(1)} %bitcast.27, ...), custom_call_target="tpu_custom_call" | custom-call | flops 2415919104 | bytes 15728640 | tf_op jit(solution)/shard_map/hidden/pallas_call | solution.py:105
  72.7 2.4 %collective-permute-done.9.back_three.refs_6_.refs_7_ = bf16[64,4096]{1,0:T(8,128)(2,1)} collective-permute-done((bf16[64,4096]{1,0:T(8,128)(2,1)}, bf16[64,4096]{1,0:T(8,128)(2,1)}, u32[]{:S(2)}, u32[]{:S(2)}) %collective-permute-start.9) | collective-permute-done | bytes 524320 | tf_op jit(solution)/shard_map/ppermute | solution.py:25
  75.1 1.6 forward.1
  76.7 9.3 %collective-permute-start.12 = (bf16[64,4096]{1,0:T(8,128)(2,1)S(1)}, bf16[64,4096]{1,0:T(8,128)(2,1)S(1)}, u32[]{:S(2)}, u32[]{:S(2)}) collective-permute-start(bf16[64,4096]{1,0:T(8,128)(2,1)S(1)} %get-tuple-element.55), channel_id=1, source_target_pairs={{0,254},{2,0},{4,2},{6,4},{8,6},{10,8},{12,10},{14,12},{16,14},{18... | collective-permute-start | bytes 1572872 | tf_op jit(solution)/shard_map/ppermute | solution.py:25
  86.0 2.7 %collective-permute-start.14 = (bf16[64,768]{1,0:T(8,128)(2,1)S(1)}, bf16[64,768]{1,0:T(8,128)(2,1)S(1)}, u32[]{:S(2)}, u32[]{:S(2)}) collective-permute-start(bf16[64,768]{1,0:T(8,128)(2,1)S(1)} %get-tuple-element.61.refs_7_), channel_id=1, source_target_pairs={{0,14},{2,0},{4,2},{6,4},{8,6},{10,8},{12,10},{14,12},{16,30},{18,... | collective-permute-start | bytes 294920 | tf_op jit(solution)/shard_map/ppermute | solution.py:20
  88.7 5.6 %hidden.4 = (bf16[64,768]{1,0:T(8,128)(2,1)S(1)}, bf16[64,768]{1,0:T(8,128)(2,1)S(1)}) custom-call(s32[52]{0:T(128)S(1)} %concatenate.7.table, bf16[64,4096]{1,0:T(8,128)(2,1)} %collective-permute-done.4.refs_0_.refs_1_, bf16[64,4096]{1,0:T(8,128)(2,1)} %collective-permute-done.4.refs_0_.refs_1_, ...), custom_call_target="tpu_custom_call" | custom-call | flops 1610612736 | bytes 14680064 | tf_op jit(solution)/shard_map/hidden/pallas_call | solution.py:105
  94.3 0.3 collective-permute-done.12.refs_2_.refs_3_.refs_8_.refs_9_
  94.6 3.3 %collective-permute-start.15 = (bf16[64,768]{1,0:T(8,128)(2,1)S(1)}, bf16[64,768]{1,0:T(8,128)(2,1)S(1)}, u32[]{:S(2)}, u32[]{:S(2)}) collective-permute-start(bf16[64,768]{1,0:T(8,128)(2,1)S(1)} %get-tuple-element.60.refs_6_), channel_id=1, source_target_pairs={{0,12},{2,14},{4,0},{6,2},{8,4},{10,6},{12,8},{14,10},{16,28},{18,... | collective-permute-start | bytes 294920 | tf_op jit(solution)/shard_map/ppermute | solution.py:20
  97.9 4.1 %collective-permute-done.13.refs_4_.refs_5_.refs_10_.refs_11_ = bf16[64,4096]{1,0:T(8,128)(2,1)S(1)} collective-permute-done((bf16[64,4096]{1,0:T(8,128)(2,1)S(1)}, bf16[64,4096]{1,0:T(8,128)(2,1)S(1)}, u32[]{:S(2)}, u32[]{:S(2)}) %collective-permute-start.13) | collective-permute-done | bytes 524320 | tf_op jit(solution)/shard_map/ppermute | solution.py:25
  102.0 6.2 %hidden.5 = (bf16[64,768]{1,0:T(8,128)(2,1)S(1)}, bf16[64,768]{1,0:T(8,128)(2,1)S(1)}, bf16[64,768]{1,0:T(8,128)(2,1)S(1)}) custom-call(s32[52]{0:T(128)S(1)} %concatenate.7.table, bf16[64,4096]{1,0:T(8,128)(2,1)} %collective-permute-done.8.ahead_three.refs_0_.refs_1_, bf16[64,4096]{1,0:T(8,128)(2,1)} %collective-permute-done.8.ahead_three.refs_0_.refs_1_, ...), custom_call_target="tpu_custom_call" | custom-call | flops 2415919104 | bytes 15728640 | tf_op jit(solution)/shard_map/hidden/pallas_call | solution.py:105
  108.4 4.4 %collective-permute-start.16 = (bf16[64,768]{1,0:T(8,128)(2,1)S(1)}, bf16[64,768]{1,0:T(8,128)(2,1)S(1)}, u32[]{:S(2)}, u32[]{:S(2)}) collective-permute-start(bf16[64,768]{1,0:T(8,128)(2,1)S(1)} %get-tuple-element.59.refs_5_), channel_id=1, source_target_pairs={{0,10},{2,12},{4,14},{6,0},{8,2},{10,4},{12,6},{14,8},{16,26},{18,... | collective-permute-start | bytes 294920 | tf_op jit(solution)/shard_map/ppermute | solution.py:20
  112.9 3.9 %collective-permute-done.18.refs_5_ = bf16[64,768]{1,0:T(8,128)(2,1)S(1)} collective-permute-done((bf16[64,768]{1,0:T(8,128)(2,1)S(1)}, bf16[64,768]{1,0:T(8,128)(2,1)S(1)}, u32[]{:S(2)}, u32[]{:S(2)}) %collective-permute-start.18) | collective-permute-done | bytes 98336 | tf_op jit(solution)/shard_map/ppermute | solution.py:20
  116.8 0.7 share.1
  117.6 4.8 %collective-permute-start.22 = (bf16[64,768]{1,0:T(8,128)(2,1)S(1)}, bf16[64,768]{1,0:T(8,128)(2,1)S(1)}, u32[]{:S(2)}, u32[]{:S(2)}) collective-permute-start(bf16[64,768]{1,0:T(8,128)(2,1)S(1)} %get-tuple-element.64.last), channel_id=1, source_target_pairs={{0,240},{2,242},{4,244},{6,246},{8,248},{10,250},{12,252},{14,254}... | collective-permute-start | bytes 294920 | tf_op jit(solution)/shard_map/ppermute | solution.py:25
  122.4 2.2 %collective-permute-done.21.came_last = bf16[64,768]{1,0:T(8,128)(2,1)S(1)} collective-permute-done((bf16[64,768]{1,0:T(8,128)(2,1)S(1)}, bf16[64,768]{1,0:T(8,128)(2,1)S(1)}, u32[]{:S(2)}, u32[]{:S(2)}) %collective-permute-start.21) | collective-permute-done | bytes 98336 | tf_op jit(solution)/shard_map/ppermute | solution.py:25
  124.5 0.8 send.1
  125.4 6.8 %collective-permute-start.24 = (bf16[64,768]{1,0:T(8,128)(2,1)S(1)}, bf16[64,768]{1,0:T(8,128)(2,1)S(1)}, u32[]{:S(2)}, u32[]{:S(2)}) collective-permute-start(bf16[64,768]{1,0:T(8,128)(2,1)S(1)} %get-tuple-element.67), channel_id=1, source_target_pairs={{0,12},{2,14},{4,0},{6,2},{8,4},{10,6},{12,8},{14,10},{16,28},{18,... | collective-permute-start | bytes 294920 | tf_op jit(solution)/shard_map/ppermute | solution.py:20
  132.3 2.2 %collective-permute-start.26 = (bf16[64,768]{1,0:T(8,128)(2,1)S(1)}, bf16[64,768]{1,0:T(8,128)(2,1)S(1)}, u32[]{:S(2)}, u32[]{:S(2)}) collective-permute-start(bf16[64,768]{1,0:T(8,128)(2,1)S(1)} %get-tuple-element.69), channel_id=1, source_target_pairs={{0,8},{2,10},{4,12},{6,14},{8,0},{10,2},{12,4},{14,6},{16,24},{18,... | collective-permute-start | bytes 294920 | tf_op jit(solution)/shard_map/ppermute | solution.py:20
  134.5 2.1 %collective-permute-start.27 = (bf16[64,768]{1,0:T(8,128)(2,1)S(1)}, bf16[64,768]{1,0:T(8,128)(2,1)S(1)}, u32[]{:S(2)}, u32[]{:S(2)}) collective-permute-start(bf16[64,768]{1,0:T(8,128)(2,1)S(1)} %get-tuple-element.70), channel_id=1, source_target_pairs={{0,6},{2,8},{4,10},{6,12},{8,14},{10,0},{12,2},{14,4},{16,22},{18,... | collective-permute-start | bytes 294920 | tf_op jit(solution)/shard_map/ppermute | solution.py:20
  136.7 2.2 %collective-permute-start.28 = (bf16[64,768]{1,0:T(8,128)(2,1)S(1)}, bf16[64,768]{1,0:T(8,128)(2,1)S(1)}, u32[]{:S(2)}, u32[]{:S(2)}) collective-permute-start(bf16[64,768]{1,0:T(8,128)(2,1)S(1)} %get-tuple-element.71), channel_id=1, source_target_pairs={{0,4},{2,6},{4,8},{6,10},{8,12},{10,14},{12,0},{14,2},{16,20},{18,... | collective-permute-start | bytes 294920 | tf_op jit(solution)/shard_map/ppermute | solution.py:20
  138.8 1.3 collective-permute-start.29
  140.1 1.5 collective-permute-done.25.refs_11_
  141.6 0.2 collective-permute-done.27.refs_13_
  141.8 4.3 %collective-permute-done.28.refs_14_ = bf16[64,768]{1,0:T(8,128)(2,1)S(1)} collective-permute-done((bf16[64,768]{1,0:T(8,128)(2,1)S(1)}, bf16[64,768]{1,0:T(8,128)(2,1)S(1)}, u32[]{:S(2)}, u32[]{:S(2)}) %collective-permute-start.28) | collective-permute-done | bytes 98336 | tf_op jit(solution)/shard_map/ppermute | solution.py:20
  146.1 1.3 collective-permute-done.29.refs_15_
  147.4 1.9 %correlate.2 = f32[384,768]{1,0:T(8,128)S(1)} custom-call(s32[52]{0:T(128)S(1)} %concatenate.7.table, bf16[64,768]{1,0:T(8,128)(2,1)S(1)} %get-tuple-element.48.refs_0_, bf16[64,768]{1,0:T(8,128)(2,1)S(1)} %get-tuple-element.49.refs_1_, bf16[64,768]{1,0:T(8,128)(2,1)S(1)} %get-tuple-element.52.refs_2_, bf16[64,768]{1,0:T(8,128)(2,1)S(1)} %get-tuple-element.57.refs_3_, ...), custom_call_target="tpu_custom_call" | custom-call | flops 301989888 | bytes 1572864 | tf_op jit(solution)/shard_map/correlate/pallas_call | solution.py:215
  149.2 10.7 %collective-permute-start.30 = (f32[384,768]{1,0:T(8,128)S(1)}, f32[384,768]{1,0:T(8,128)S(1)}, u32[]{:S(2)}, u32[]{:S(2)}) collective-permute-start(f32[384,768]{1,0:T(8,128)S(1)} %correlate.2), channel_id=1, source_target_pairs={{0,1},{1,0},{2,3},{3,2},{4,5},{5,4},{6,7},{7,6},{8,9},{9,8},{10,11... | collective-permute-start | bytes 3538952 | tf_op jit(solution)/shard_map/ppermute | solution.py:29
  159.9 2.5 %collective-permute-done.30.refs_16_ = f32[384,768]{1,0:T(8,128)S(1)} collective-permute-done((f32[384,768]{1,0:T(8,128)S(1)}, f32[384,768]{1,0:T(8,128)S(1)}, u32[]{:S(2)}, u32[]{:S(2)}) %collective-permute-start.30) | collective-permute-done | bytes 1179680 | tf_op jit(solution)/shard_map/ppermute | solution.py:29
  162.4 2.9 %correlate.3 = f32[384,768]{1,0:T(8,128)} custom-call(s32[52]{0:T(128)S(1)} %concatenate.7.table, bf16[64,768]{1,0:T(8,128)(2,1)S(1)} %get-tuple-element.48.refs_0_, bf16[64,768]{1,0:T(8,128)(2,1)S(1)} %get-tuple-element.49.refs_1_, bf16[64,768]{1,0:T(8,128)(2,1)S(1)} %get-tuple-element.52.refs_2_, bf16[64,768]{1,0:T(8,128)(2,1)S(1)} %get-tuple-element.57.refs_3_, ...), custom_call_target="tpu_custom_call" | custom-call | flops 301989888 | bytes 1572864 | tf_op jit(solution)/shard_map/correlate/pallas_call | solution.py:215
  (43 shorter events, 1.0 us)
Async XLA Ops:
  0.0 23.9 %collective-permute-start.2 = (bf16[2048,768]{1,0:T(8,128)(2,1)}, bf16[2048,768]{1,0:T(8,128)(2,1)S(1)}, u32[]{:S(2)}, u32[]{:S(2)}) collective-permute-start(bf16[2048,768]{1,0:T(8,128)(2,1)} %bitcast.15), channel_id=1, source_target_pairs={{0,1},{1,0},{2,3},{3,2},{4,5},{5,4},{6,7},{7,6},{8,9},{9,8},{10,11... | collective-permute-start | bytes 9437192 | tf_op jit(solution)/shard_map/ppermute | solution.py:29
  3.2 20.6 %collective-permute-start.3 = (bf16[2048,768]{1,0:T(8,128)(2,1)}, bf16[2048,768]{1,0:T(8,128)(2,1)}, u32[]{:S(2)}, u32[]{:S(2)}) collective-permute-start(bf16[2048,768]{1,0:T(8,128)(2,1)} %bitcast.19), channel_id=1, source_target_pairs={{0,1},{1,0},{2,3},{3,2},{4,5},{5,4},{6,7},{7,6},{8,9},{9,8},{10,11... | collective-permute-start | bytes 9437192 | tf_op jit(solution)/shard_map/ppermute | solution.py:29
  3.2 20.6 %collective-permute-start.1 = (bf16[64,4096]{1,0:T(8,128)(2,1)}, bf16[64,4096]{1,0:T(8,128)(2,1)}, u32[]{:S(2)}, u32[]{:S(2)}) collective-permute-start(bf16[64,4096]{1,0:T(8,128)(2,1)} %bitcast.23), channel_id=1, source_target_pairs={{0,2},{2,4},{4,6},{6,8},{8,10},{10,12},{12,14},{14,16},{16,18},{18... | collective-permute-start | bytes 1572872 | tf_op jit(solution)/shard_map/ppermute | solution.py:25
  3.2 20.6 %collective-permute-start = (bf16[64,4096]{1,0:T(8,128)(2,1)}, bf16[64,4096]{1,0:T(8,128)(2,1)}, u32[]{:S(2)}, u32[]{:S(2)}) collective-permute-start(bf16[64,4096]{1,0:T(8,128)(2,1)} %bitcast.24), channel_id=1, source_target_pairs={{0,254},{2,0},{4,2},{6,4},{8,6},{10,8},{12,10},{14,12},{16,14},{18... | collective-permute-start | bytes 1572872 | tf_op jit(solution)/shard_map/ppermute | solution.py:25
  23.9 16.1 %collective-permute-start.6 = (bf16[64,4096]{1,0:T(8,128)(2,1)}, bf16[64,4096]{1,0:T(8,128)(2,1)}, u32[]{:S(2)}, u32[]{:S(2)}) collective-permute-start(bf16[64,4096]{1,0:T(8,128)(2,1)} %collective-permute-done.refs_4_.refs_5_), channel_id=1, source_target_pairs={{0,16},{2,18},{4,20},{6,22},{8,24},{10,26},{12,28},{14,30},{16,32}... | collective-permute-start | bytes 1572872 | tf_op jit(solution)/shard_map/ppermute | solution.py:25
  24.0 16.8 %collective-permute-start.4 = (bf16[64,4096]{1,0:T(8,128)(2,1)}, bf16[64,4096]{1,0:T(8,128)(2,1)}, u32[]{:S(2)}, u32[]{:S(2)}) collective-permute-start(bf16[64,4096]{1,0:T(8,128)(2,1)} %collective-permute-done.refs_4_.refs_5_), channel_id=1, source_target_pairs={{0,254},{2,0},{4,2},{6,4},{8,6},{10,8},{12,10},{14,12},{16,14},{18... | collective-permute-start | bytes 1572872 | tf_op jit(solution)/shard_map/ppermute | solution.py:25
  30.6 12.1 %collective-permute-start.7 = (bf16[64,4096]{1,0:T(8,128)(2,1)}, bf16[64,4096]{1,0:T(8,128)(2,1)}, u32[]{:S(2)}, u32[]{:S(2)}) collective-permute-start(bf16[64,4096]{1,0:T(8,128)(2,1)} %collective-permute-done.1.refs_10_.refs_11_), channel_id=1, source_target_pairs={{0,240},{2,242},{4,244},{6,246},{8,248},{10,250},{12,252},{14,254}... | collective-permute-start | bytes 1572872 | tf_op jit(solution)/shard_map/ppermute | solution.py:25
  31.9 17.1 %collective-permute-start.5 = (bf16[64,4096]{1,0:T(8,128)(2,1)}, bf16[64,4096]{1,0:T(8,128)(2,1)}, u32[]{:S(2)}, u32[]{:S(2)}) collective-permute-start(bf16[64,4096]{1,0:T(8,128)(2,1)} %collective-permute-done.1.refs_10_.refs_11_), channel_id=1, source_target_pairs={{0,2},{2,4},{4,6},{6,8},{8,10},{10,12},{12,14},{14,16},{16,18},{18... | collective-permute-start | bytes 1572872 | tf_op jit(solution)/shard_map/ppermute | solution.py:25
  49.0 23.7 %collective-permute-start.11 = (bf16[64,4096]{1,0:T(8,128)(2,1)}, bf16[64,4096]{1,0:T(8,128)(2,1)}, u32[]{:S(2)}, u32[]{:S(2)}) collective-permute-start(bf16[64,4096]{1,0:T(8,128)(2,1)} %collective-permute-done.4.refs_0_.refs_1_), channel_id=1, source_target_pairs={{0,16},{2,18},{4,20},{6,22},{8,24},{10,26},{12,28},{14,30},{16,32}... | collective-permute-start | bytes 1572872 | tf_op jit(solution)/shard_map/ppermute | solution.py:25
  49.0 23.7 %collective-permute-start.8 = (bf16[64,4096]{1,0:T(8,128)(2,1)}, bf16[64,4096]{1,0:T(8,128)(2,1)}, u32[]{:S(2)}, u32[]{:S(2)}) collective-permute-start(bf16[64,4096]{1,0:T(8,128)(2,1)} %collective-permute-done.4.refs_0_.refs_1_), channel_id=1, source_target_pairs={{0,254},{2,0},{4,2},{6,4},{8,6},{10,8},{12,10},{14,12},{16,14},{18... | collective-permute-start | bytes 1572872 | tf_op jit(solution)/shard_map/ppermute | solution.py:25
  57.6 15.1 %collective-permute-start.10 = (bf16[64,4096]{1,0:T(8,128)(2,1)}, bf16[64,4096]{1,0:T(8,128)(2,1)}, u32[]{:S(2)}, u32[]{:S(2)}) collective-permute-start(bf16[64,4096]{1,0:T(8,128)(2,1)} %collective-permute-done.5.refs_6_.refs_7_), channel_id=1, source_target_pairs={{0,240},{2,242},{4,244},{6,246},{8,248},{10,250},{12,252},{14,254}... | collective-permute-start | bytes 1572872 | tf_op jit(solution)/shard_map/ppermute | solution.py:25
  59.0 16.0 %collective-permute-start.9 = (bf16[64,4096]{1,0:T(8,128)(2,1)}, bf16[64,4096]{1,0:T(8,128)(2,1)}, u32[]{:S(2)}, u32[]{:S(2)}) collective-permute-start(bf16[64,4096]{1,0:T(8,128)(2,1)} %collective-permute-done.5.refs_6_.refs_7_), channel_id=1, source_target_pairs={{0,2},{2,4},{4,6},{6,8},{8,10},{10,12},{12,14},{14,16},{16,18},{18... | collective-permute-start | bytes 1572872 | tf_op jit(solution)/shard_map/ppermute | solution.py:25
  61.2 1.9 %copy-start = (bf16[1,2048,768]{2,1,0:T(8,128)(2,1)S(1)}, bf16[1,2048,768]{2,1,0:T(8,128)(2,1)}, u32[]{:S(2)}) copy-start(bf16[1,2048,768]{2,1,0:T(8,128)(2,1)} %param.6) | copy-start | bytes 9437188
  63.1 1.9 %copy-start.2 = (bf16[1,2048,768]{2,1,0:T(8,128)(2,1)S(1)}, bf16[1,2048,768]{2,1,0:T(8,128)(2,1)}, u32[]{:S(2)}) copy-start(bf16[1,2048,768]{2,1,0:T(8,128)(2,1)} %param.7) | copy-start | bytes 9437188
  65.0 1.0 copy-start.4
  66.0 22.7 %copy-start.1 = (bf16[1,2048,768]{2,1,0:T(8,128)(2,1)S(1)}, bf16[1,2048,768]{2,1,0:T(8,128)(2,1)}, u32[]{:S(2)}) copy-start(bf16[1,2048,768]{2,1,0:T(8,128)(2,1)} %param.6) | copy-start | bytes 9437188
  66.0 22.7 %copy-start.3 = (bf16[1,2048,768]{2,1,0:T(8,128)(2,1)S(1)}, bf16[1,2048,768]{2,1,0:T(8,128)(2,1)}, u32[]{:S(2)}) copy-start(bf16[1,2048,768]{2,1,0:T(8,128)(2,1)} %param.7) | copy-start | bytes 9437188
  76.7 17.9 %collective-permute-start.12 = (bf16[64,4096]{1,0:T(8,128)(2,1)S(1)}, bf16[64,4096]{1,0:T(8,128)(2,1)S(1)}, u32[]{:S(2)}, u32[]{:S(2)}) collective-permute-start(bf16[64,4096]{1,0:T(8,128)(2,1)S(1)} %get-tuple-element.55), channel_id=1, source_target_pairs={{0,254},{2,0},{4,2},{6,4},{8,6},{10,8},{12,10},{14,12},{16,14},{18... | collective-permute-start | bytes 1572872 | tf_op jit(solution)/shard_map/ppermute | solution.py:25
  86.0 16.0 %collective-permute-start.13 = (bf16[64,4096]{1,0:T(8,128)(2,1)S(1)}, bf16[64,4096]{1,0:T(8,128)(2,1)S(1)}, u32[]{:S(2)}, u32[]{:S(2)}) collective-permute-start(bf16[64,4096]{1,0:T(8,128)(2,1)S(1)} %get-tuple-element.56), channel_id=1, source_target_pairs={{0,2},{2,4},{4,6},{6,8},{8,10},{10,12},{12,14},{14,16},{16,18},{18... | collective-permute-start | bytes 1572872 | tf_op jit(solution)/shard_map/ppermute | solution.py:25
  86.0 22.3 %collective-permute-start.20 = (bf16[64,768]{1,0:T(8,128)(2,1)S(1)}, bf16[64,768]{1,0:T(8,128)(2,1)S(1)}, u32[]{:S(2)}, u32[]{:S(2)}) collective-permute-start(bf16[64,768]{1,0:T(8,128)(2,1)S(1)} %get-tuple-element.49.refs_1_), channel_id=1, source_target_pairs={{0,2},{2,4},{4,6},{6,8},{8,10},{10,12},{12,14},{14,0},{16,18},{18,... | collective-permute-start | bytes 294920 | tf_op jit(solution)/shard_map/ppermute | solution.py:20
  86.0 22.4 %collective-permute-start.14 = (bf16[64,768]{1,0:T(8,128)(2,1)S(1)}, bf16[64,768]{1,0:T(8,128)(2,1)S(1)}, u32[]{:S(2)}, u32[]{:S(2)}) collective-permute-start(bf16[64,768]{1,0:T(8,128)(2,1)S(1)} %get-tuple-element.61.refs_7_), channel_id=1, source_target_pairs={{0,14},{2,0},{4,2},{6,4},{8,6},{10,8},{12,10},{14,12},{16,30},{18,... | collective-permute-start | bytes 294920 | tf_op jit(solution)/shard_map/ppermute | solution.py:20
  94.2 18.6 %collective-permute-start.19 = (bf16[64,768]{1,0:T(8,128)(2,1)S(1)}, bf16[64,768]{1,0:T(8,128)(2,1)S(1)}, u32[]{:S(2)}, u32[]{:S(2)}) collective-permute-start(bf16[64,768]{1,0:T(8,128)(2,1)S(1)} %get-tuple-element.52.refs_2_), channel_id=1, source_target_pairs={{0,4},{2,6},{4,8},{6,10},{8,12},{10,14},{12,0},{14,2},{16,20},{18,... | collective-permute-start | bytes 294920 | tf_op jit(solution)/shard_map/ppermute | solution.py:20
  94.6 18.2 %collective-permute-start.15 = (bf16[64,768]{1,0:T(8,128)(2,1)S(1)}, bf16[64,768]{1,0:T(8,128)(2,1)S(1)}, u32[]{:S(2)}, u32[]{:S(2)}) collective-permute-start(bf16[64,768]{1,0:T(8,128)(2,1)S(1)} %get-tuple-element.60.refs_6_), channel_id=1, source_target_pairs={{0,12},{2,14},{4,0},{6,2},{8,4},{10,6},{12,8},{14,10},{16,28},{18,... | collective-permute-start | bytes 294920 | tf_op jit(solution)/shard_map/ppermute | solution.py:20
  108.2 8.6 %collective-permute-start.18 = (bf16[64,768]{1,0:T(8,128)(2,1)S(1)}, bf16[64,768]{1,0:T(8,128)(2,1)S(1)}, u32[]{:S(2)}, u32[]{:S(2)}) collective-permute-start(bf16[64,768]{1,0:T(8,128)(2,1)S(1)} %get-tuple-element.57.refs_3_), channel_id=1, source_target_pairs={{0,6},{2,8},{4,10},{6,12},{8,14},{10,0},{12,2},{14,4},{16,22},{18,... | collective-permute-start | bytes 294920 | tf_op jit(solution)/shard_map/ppermute | solution.py:20
  108.3 8.5 %collective-permute-start.17 = (bf16[64,768]{1,0:T(8,128)(2,1)S(1)}, bf16[64,768]{1,0:T(8,128)(2,1)S(1)}, u32[]{:S(2)}, u32[]{:S(2)}) collective-permute-start(bf16[64,768]{1,0:T(8,128)(2,1)S(1)} %get-tuple-element.58.refs_4_), channel_id=1, source_target_pairs={{0,8},{2,10},{4,12},{6,14},{8,0},{10,2},{12,4},{14,6},{16,24},{18,... | collective-permute-start | bytes 294920 | tf_op jit(solution)/shard_map/ppermute | solution.py:20
  108.4 8.4 %collective-permute-start.16 = (bf16[64,768]{1,0:T(8,128)(2,1)S(1)}, bf16[64,768]{1,0:T(8,128)(2,1)S(1)}, u32[]{:S(2)}, u32[]{:S(2)}) collective-permute-start(bf16[64,768]{1,0:T(8,128)(2,1)S(1)} %get-tuple-element.59.refs_5_), channel_id=1, source_target_pairs={{0,10},{2,12},{4,14},{6,0},{8,2},{10,4},{12,6},{14,8},{16,26},{18,... | collective-permute-start | bytes 294920 | tf_op jit(solution)/shard_map/ppermute | solution.py:20
  117.5 7.0 %collective-permute-start.21 = (bf16[64,768]{1,0:T(8,128)(2,1)S(1)}, bf16[64,768]{1,0:T(8,128)(2,1)S(1)}, u32[]{:S(2)}, u32[]{:S(2)}) collective-permute-start(bf16[64,768]{1,0:T(8,128)(2,1)S(1)} %get-tuple-element.63.nxt), channel_id=1, source_target_pairs={{0,16},{2,18},{4,20},{6,22},{8,24},{10,26},{12,28},{14,30},{16,32}... | collective-permute-start | bytes 294920 | tf_op jit(solution)/shard_map/ppermute | solution.py:25
  117.6 6.9 %collective-permute-start.22 = (bf16[64,768]{1,0:T(8,128)(2,1)S(1)}, bf16[64,768]{1,0:T(8,128)(2,1)S(1)}, u32[]{:S(2)}, u32[]{:S(2)}) collective-permute-start(bf16[64,768]{1,0:T(8,128)(2,1)S(1)} %get-tuple-element.64.last), channel_id=1, source_target_pairs={{0,240},{2,242},{4,244},{6,246},{8,248},{10,250},{12,252},{14,254}... | collective-permute-start | bytes 294920 | tf_op jit(solution)/shard_map/ppermute | solution.py:25
  125.4 11.3 %collective-permute-start.23 = (bf16[64,768]{1,0:T(8,128)(2,1)S(1)}, bf16[64,768]{1,0:T(8,128)(2,1)S(1)}, u32[]{:S(2)}, u32[]{:S(2)}) collective-permute-start(bf16[64,768]{1,0:T(8,128)(2,1)S(1)} %get-tuple-element.66), channel_id=1, source_target_pairs={{0,14},{2,0},{4,2},{6,4},{8,6},{10,8},{12,10},{14,12},{16,30},{18,... | collective-permute-start | bytes 294920 | tf_op jit(solution)/shard_map/ppermute | solution.py:20
  125.4 13.4 %collective-permute-start.24 = (bf16[64,768]{1,0:T(8,128)(2,1)S(1)}, bf16[64,768]{1,0:T(8,128)(2,1)S(1)}, u32[]{:S(2)}, u32[]{:S(2)}) collective-permute-start(bf16[64,768]{1,0:T(8,128)(2,1)S(1)} %get-tuple-element.67), channel_id=1, source_target_pairs={{0,12},{2,14},{4,0},{6,2},{8,4},{10,6},{12,8},{14,10},{16,28},{18,... | collective-permute-start | bytes 294920 | tf_op jit(solution)/shard_map/ppermute | solution.py:20
  132.3 9.3 %collective-permute-start.25 = (bf16[64,768]{1,0:T(8,128)(2,1)S(1)}, bf16[64,768]{1,0:T(8,128)(2,1)S(1)}, u32[]{:S(2)}, u32[]{:S(2)}) collective-permute-start(bf16[64,768]{1,0:T(8,128)(2,1)S(1)} %get-tuple-element.68), channel_id=1, source_target_pairs={{0,10},{2,12},{4,14},{6,0},{8,2},{10,4},{12,6},{14,8},{16,26},{18,... | collective-permute-start | bytes 294920 | tf_op jit(solution)/shard_map/ppermute | solution.py:20
  132.3 9.3 %collective-permute-start.26 = (bf16[64,768]{1,0:T(8,128)(2,1)S(1)}, bf16[64,768]{1,0:T(8,128)(2,1)S(1)}, u32[]{:S(2)}, u32[]{:S(2)}) collective-permute-start(bf16[64,768]{1,0:T(8,128)(2,1)S(1)} %get-tuple-element.69), channel_id=1, source_target_pairs={{0,8},{2,10},{4,12},{6,14},{8,0},{10,2},{12,4},{14,6},{16,24},{18,... | collective-permute-start | bytes 294920 | tf_op jit(solution)/shard_map/ppermute | solution.py:20
  134.5 7.3 %collective-permute-start.27 = (bf16[64,768]{1,0:T(8,128)(2,1)S(1)}, bf16[64,768]{1,0:T(8,128)(2,1)S(1)}, u32[]{:S(2)}, u32[]{:S(2)}) collective-permute-start(bf16[64,768]{1,0:T(8,128)(2,1)S(1)} %get-tuple-element.70), channel_id=1, source_target_pairs={{0,6},{2,8},{4,10},{6,12},{8,14},{10,0},{12,2},{14,4},{16,22},{18,... | collective-permute-start | bytes 294920 | tf_op jit(solution)/shard_map/ppermute | solution.py:20
  136.7 9.4 %collective-permute-start.28 = (bf16[64,768]{1,0:T(8,128)(2,1)S(1)}, bf16[64,768]{1,0:T(8,128)(2,1)S(1)}, u32[]{:S(2)}, u32[]{:S(2)}) collective-permute-start(bf16[64,768]{1,0:T(8,128)(2,1)S(1)} %get-tuple-element.71), channel_id=1, source_target_pairs={{0,4},{2,6},{4,8},{6,10},{8,12},{10,14},{12,0},{14,2},{16,20},{18,... | collective-permute-start | bytes 294920 | tf_op jit(solution)/shard_map/ppermute | solution.py:20
  138.8 8.5 %collective-permute-start.29 = (bf16[64,768]{1,0:T(8,128)(2,1)S(1)}, bf16[64,768]{1,0:T(8,128)(2,1)S(1)}, u32[]{:S(2)}, u32[]{:S(2)}) collective-permute-start(bf16[64,768]{1,0:T(8,128)(2,1)S(1)} %get-tuple-element.72), channel_id=1, source_target_pairs={{0,2},{2,4},{4,6},{6,8},{8,10},{10,12},{12,14},{14,0},{16,18},{18,... | collective-permute-start | bytes 294920 | tf_op jit(solution)/shard_map/ppermute | solution.py:20
  149.2 13.1 %collective-permute-start.30 = (f32[384,768]{1,0:T(8,128)S(1)}, f32[384,768]{1,0:T(8,128)S(1)}, u32[]{:S(2)}, u32[]{:S(2)}) collective-permute-start(f32[384,768]{1,0:T(8,128)S(1)} %correlate.2), channel_id=1, source_target_pairs={{0,1},{1,0},{2,3},{3,2},{4,5},{5,4},{6,7},{7,6},{8,9},{9,8},{10,11... | collective-permute-start | bytes 3538952 | tf_op jit(solution)/shard_map/ppermute | solution.py:29

commit v2 on v1

--- a/solution.py
+++ b/solution.py
@@ -14,15 +14,26 @@
 NEAR, DOM, CORE, LINE_AT, PLACE, SIZE = 0, 24, 48, 49, 50, 51
 
 
-def along_line(value, offset):
+def moved(value, target):
     count = lax.axis_size("expert")
-    pairs = [(i, i // LINE * LINE + (i - offset) % LINE) for i in range(count)]
-    return lax.ppermute(value, "expert", pairs)
-
-
-def shift(value, step):
-    count = lax.axis_size("expert")
-    return lax.ppermute(value, "expert", [(i, (i + step) % count) for i in range(count)])
+    return lax.ppermute(value, "expert", [(i, target(i) % count) for i in range(count)])
+
+
+def with_next(value):
+    return moved(value, lambda i: i + 1 - 2 * (i % 2))
+
+
+def with_last(value):
+    return moved(value, lambda i: i - 1 + 2 * (i % 2))
+
+
+def to_line(value, step):
+    return moved(value, lambda i: i + step * LINE * (1 - 2 * (i % 2)))
+
+
+def round_line(value, offset):
+    turn = lambda i: i // LINE * LINE + (i + offset * (1 - 2 * (i % 2))) % LINE
+    return moved(value, turn), (offset if offset % 2 else LINE - offset)
 
 
 def swap_cores(value):
@@ -35,13 +46,17 @@
 
 def scalars(cluster, dominant_rank):
     expert_id = lax.axis_index("expert")
+    top = cluster.shape[0] - 1
+    mirrored = expert_id % 2 == 1
+    expert_id = jnp.where(mirrored, top - expert_id, expert_id)
     line, place = expert_id // LINE, expert_id % LINE
     start = jnp.sum((cluster[None, :] < cluster[:, None]).astype(jnp.int32), axis=1)
     size = jnp.sum((cluster[None, :] == cluster[:, None]).astype(jnp.int32), axis=1)
     names = jnp.arange(dominant_rank.shape[0], dtype=jnp.int32)
     rank = jnp.sum(jnp.where(names[None, :] == cluster[:, None], dominant_rank[None, :], 0), axis=1)
     dom = start + rank % size
-    tables = jnp.pad(jnp.stack([cluster, dom, size]), ((0, 0), (LINE, LINE)), constant_values=-1)
+    tables = jnp.where(mirrored, jnp.stack([cluster, top - dom, size])[:, ::-1], jnp.stack([cluster, dom, size]))
+    tables = jnp.pad(tables, ((0, 0), (LINE, LINE)), constant_values=-1)
     three = lax.dynamic_slice_in_dim(tables, line * LINE, 3 * LINE, 1).reshape(3, 3, LINE)
     rolled = lax.dynamic_slice_in_dim(jnp.concatenate([three, three], axis=2), place, LINE, 2)
     here = jnp.stack([lax.axis_index("row"), line, place, rolled[2, 1, 0]])
@@ -236,34 +251,41 @@
     gate_other, up_other = swap_cores(gate), swap_cores(up)
     own = calib_rows[0]
     ahead, behind = {0: own}, {0: own}
-    ahead[1], behind[7] = shift(own, -1), shift(own, 1)
+    ahead[1], behind[7] = with_next(own), with_last(own)
     ahead[1], behind[7], gate_other, up_other = after(ahead[1], behind[7], gate_other, up_other)
     weights = (gate, gate_other, up, up_other)
-    ahead[2], behind[6] = shift(ahead[1], -1), shift(behind[7], 1)
-    behind[1], ahead[7] = shift(ahead[1], LINE), shift(behind[7], -LINE)
+    behind[6], ahead[2] = with_last(ahead[1]), with_next(behind[7])
+    behind[1], ahead[7] = to_line(ahead[1], 1), to_line(behind[7], -1)
     ahead[2], behind[6], behind[1], ahead[7] = after(ahead[2], behind[6], behind[1], ahead[7])
-    ahead[3], behind[5] = shift(ahead[2], -1), shift(behind[6], 1)
-    behind[2], ahead[6] = shift(ahead[2], LINE), shift(behind[6], -LINE)
+    behind[5], ahead[3] = with_last(ahead[2]), with_next(behind[6])
+    behind[2], ahead[6] = to_line(ahead[2], 1), to_line(behind[6], -1)
 
     hidden, returned = {}, {}
 
     def compute(group):
         for k, block in zip(group, hidden_of(table, group, ahead, behind, weights)):
             hidden[k] = block
-            returned[(LINE - k) % LINE] = along_line(block, LINE - k) if k else block
+            if k:
+                block, seen_at = round_line(block, k)
+                returned[seen_at] = block
 
     compute((0, 1, 7))
-    ahead[3], behind[5], ahead[6], behind[2], hidden[0] = after(ahead[3], behind[5], ahead[6], behind[2], hidden[0])
+    own_hidden = hidden[0]
+    ahead[3], behind[5], ahead[6], behind[2], own_hidden = after(ahead[3], behind[5], ahead[6], behind[2], own_hidden)
     to_next, to_last = choose(forward_kernel, table, [behind[5], ahead[6], ahead[3], behind[2]], 2, "forward")
-    from_last, from_next = shift(to_next, 1), shift(to_last, -1)
+    from_next, from_last = with_next(to_next), with_last(to_last)
     ahead[4], behind[3], behind[4], ahead[5] = from_next, from_next, from_last, from_last
     compute((2, 6))
     compute((3, 5, 4))
+    hidden[0] = returned[0] = own_hidden
 
     shares = choose(share_kernel, table, [returned[k] for k in range(LINE)], 3, "share")
-    came_last, came_next = shift(shares[1], LINE), shift(shares[2], -LINE)
+    came_last, came_next = to_line(shares[1], 1), to_line(shares[2], -1)
     chunks = choose(send_kernel, table, [*shares, came_last, came_next], LINE, "send")
-    panel = {k: along_line(chunks[(-k) % LINE], k) if k else chunks[0] for k in range(LINE)}
+    panel = {0: chunks[0]}
+    for away in range(1, LINE):
+        block, seen_at = round_line(chunks[away], away)
+        panel[seen_at] = block
 
     hidden, panel = [hidden[k] for k in range(LINE)], [panel[k] for k in range(LINE)]
     received = swap_cores(correlate(table, hidden, panel))

time: 166 us -> 161 us (0.970)
  starting transfers between devices: 80 us -> 68.7 us
  waiting for transfers between devices: 50 us -> 56 us
    ppermute x28, starting transfers between devices: 66.1 us -> 54 us  [moved(): lax.ppermute(value, 'expert', [(i, target(i) % count) for i in range(coun...]
    ppermute x28, waiting for transfers between devices: 47.5 us -> 53.5 us  [moved(): lax.ppermute(value, 'expert', [(i, target(i) % count) for i in range(coun...]
  transfers between devices with their start and end apart: 31 -> 31, of which waited for: 15 -> 16; matrix products, arithmetic and copies ran while one was open for 2% -> 3% of each run, Pallas kernels for 11% -> 12%
where the time goes in v2:
time: 161 us
  starting transfers between devices  68.7 us (43%)
  waiting for transfers between devices  56 us (35%)
  Pallas kernels  26.4 us (16%)
  local copies, waits for them, and re-layouts  6.33 us (4%)
  other arithmetic  3.2 us (2%)
    ppermute x28, starting transfers between devices, moved(): lax.ppermute(value, 'expert', [(i, target(i) % count) for i in range(coun...  54 us
    ppermute x28, waiting for transfers between devices, moved(): lax.ppermute(value, 'expert', [(i, target(i) % count) for i in range(coun...  53.5 us
    pallas_call x3, Pallas kernels, hidden_of(): pl.pallas_call(functools.partial(hidden_kernel, group), out_shape=[jax.Sh...  18.5 us
    ppermute x3, starting transfers between devices, swap_cores(): return lax.ppermute(value, 'row', [(0, 1), (1, 0)])  14.7 us
    unnamed x10, local copies, waits for them, and re-layouts  4.83 us
    pallas_call x2, Pallas kernels, correlate(): pl.pallas_call(functools.partial(correlate_kernel, add), out_shape=jax.Sh...  4.76 us
  transfers between devices with their start and end apart: 31, of which 16 were waited for; matrix products, arithmetic and copies ran while one was open for 3% of the time, Pallas kernels for 12%

profile of v2, /device:TPU:1, one launch (start us, length us, event | category | flops | bytes accessed | tf_op | source)
XLA Modules:
  0.0 160.7 jit_solution(14677346174479355841)
XLA Ops:
  0.0 3.2 %collective-permute-start.2 = (bf16[2048,768]{1,0:T(8,128)(2,1)}, bf16[2048,768]{1,0:T(8,128)(2,1)S(1)}, u32[]{:S(2)}, u32[]{:S(2)}) collective-permute-start(bf16[2048,768]{1,0:T(8,128)(2,1)} %bitcast.18), channel_id=1, source_target_pairs={{0,1},{1,0},{2,3},{3,2},{4,5},{5,4},{6,7},{7,6},{8,9},{9,8},{10,11... | collective-permute-start | bytes 9437192 | tf_op jit(solution)/shard_map/ppermute | solution.py:40
  3.2 8.5 %collective-permute-start.1 = (bf16[64,4096]{1,0:T(8,128)(2,1)}, bf16[64,4096]{1,0:T(8,128)(2,1)}, u32[]{:S(2)}, u32[]{:S(2)}) collective-permute-start(bf16[64,4096]{1,0:T(8,128)(2,1)} %bitcast.26), channel_id=1, source_target_pairs={{0,254},{2,4},{4,2},{6,8},{8,6},{10,12},{12,10},{14,16},{16,14},{1... | collective-permute-start | bytes 1572872 | tf_op jit(solution)/shard_map/ppermute | solution.py:19
  11.7 12.1 %collective-permute-done.1.refs_10_.refs_11_ = bf16[64,4096]{1,0:T(8,128)(2,1)} collective-permute-done((bf16[64,4096]{1,0:T(8,128)(2,1)}, bf16[64,4096]{1,0:T(8,128)(2,1)}, u32[]{:S(2)}, u32[]{:S(2)}) %collective-permute-start.1) | collective-permute-done | bytes 524320 | tf_op jit(solution)/shard_map/ppermute | solution.py:19
  23.9 0.8 collective-permute-done.refs_4_.refs_5_
  24.7 0.6 collective-permute-start.7
  25.3 0.9 collective-permute-start.6
  26.2 5.8 %collective-permute-start.5 = (bf16[64,4096]{1,0:T(8,128)(2,1)}, bf16[64,4096]{1,0:T(8,128)(2,1)}, u32[]{:S(2)}, u32[]{:S(2)}) collective-permute-start(bf16[64,4096]{1,0:T(8,128)(2,1)} %collective-permute-done.refs_4_.refs_5_), channel_id=1, source_target_pairs={{0,254},{2,4},{4,2},{6,8},{8,6},{10,12},{12,10},{14,16},{16,14},{1... | collective-permute-start | bytes 1572872 | tf_op jit(solution)/shard_map/ppermute | solution.py:19
  32.0 0.8 select_reduce_fusion
  32.8 0.9 convert_reduce_fusion.1
  33.8 0.7 pad_add_fusion.1
  34.6 2.2 %collective-permute-done.7.refs_8_.refs_9_ = bf16[64,4096]{1,0:T(8,128)(2,1)} collective-permute-done((bf16[64,4096]{1,0:T(8,128)(2,1)}, bf16[64,4096]{1,0:T(8,128)(2,1)}, u32[]{:S(2)}, u32[]{:S(2)}) %collective-permute-start.7) | collective-permute-done | bytes 524320 | tf_op jit(solution)/shard_map/ppermute | solution.py:19
  37.0 14.6 %collective-permute-done.6.refs_6_.refs_7_ = bf16[64,4096]{1,0:T(8,128)(2,1)} collective-permute-done((bf16[64,4096]{1,0:T(8,128)(2,1)}, bf16[64,4096]{1,0:T(8,128)(2,1)}, u32[]{:S(2)}, u32[]{:S(2)}) %collective-permute-start.6) | collective-permute-done | bytes 524320 | tf_op jit(solution)/shard_map/ppermute | solution.py:19
  51.6 1.3 collective-permute-start.10
  53.1 6.1 %collective-permute-start.9 = (bf16[64,4096]{1,0:T(8,128)(2,1)}, bf16[64,4096]{1,0:T(8,128)(2,1)}, u32[]{:S(2)}, u32[]{:S(2)}) collective-permute-start(bf16[64,4096]{1,0:T(8,128)(2,1)} %collective-permute-done.4.refs_0_.refs_1_), channel_id=1, source_target_pairs={{0,254},{2,4},{4,2},{6,8},{8,6},{10,12},{12,10},{14,16},{16,14},{1... | collective-permute-start | bytes 1572872 | tf_op jit(solution)/shard_map/ppermute | solution.py:19
  59.1 0.7 fusion
  60.7 0.6 concatenate.7.table
  61.3 1.9 %copy-done = bf16[1,2048,768]{2,1,0:T(8,128)(2,1)S(1)} copy-done((bf16[1,2048,768]{2,1,0:T(8,128)(2,1)S(1)}, bf16[1,2048,768]{2,1,0:T(8,128)(2,1)}, u32[]{:S(2)}) %copy-start) | copy-done | bytes 3145752
  63.2 1.9 %copy-done.2 = bf16[1,2048,768]{2,1,0:T(8,128)(2,1)S(1)} copy-done((bf16[1,2048,768]{2,1,0:T(8,128)(2,1)S(1)}, bf16[1,2048,768]{2,1,0:T(8,128)(2,1)}, u32[]{:S(2)}) %copy-start.2) | copy-done | bytes 3145752
  65.1 1.0 copy-done.4
  66.1 6.7 %hidden.3 = (bf16[64,768]{1,0:T(8,128)(2,1)S(1)}, bf16[64,768]{1,0:T(8,128)(2,1)S(1)}, bf16[64,768]{1,0:T(8,128)(2,1)S(1)}) custom-call(s32[52]{0:T(128)S(1)} %concatenate.7.table, bf16[64,4096]{1,0:T(8,128)(2,1)S(1)} %bitcast.28, bf16[64,4096]{1,0:T(8,128)(2,1)S(1)} %bitcast.29, bf16[64,4096]{1,0:T(8,128)(2,1)S(1)} %bitcast.30, ...), custom_call_target="tpu_custom_call" | custom-call | flops 2415919104 | bytes 15728640 | tf_op jit(solution)/shard_map/hidden/pallas_call | solution.py:120
  72.9 6.5 %collective-permute-done.11.refs_2_.refs_3_.back_six = bf16[64,4096]{1,0:T(8,128)(2,1)} collective-permute-done((bf16[64,4096]{1,0:T(8,128)(2,1)}, bf16[64,4096]{1,0:T(8,128)(2,1)}, u32[]{:S(2)}, u32[]{:S(2)}) %collective-permute-start.11) | collective-permute-done | bytes 524320 | tf_op jit(solution)/shard_map/ppermute | solution.py:19
  79.3 1.6 %forward.1 = (bf16[64,4096]{1,0:T(8,128)(2,1)S(1)}, bf16[64,4096]{1,0:T(8,128)(2,1)S(1)}) custom-call(s32[52]{0:T(128)S(1)} %concatenate.7.table, bf16[64,4096]{1,0:T(8,128)(2,1)} %collective-permute-done.9.back_three.refs_6_.refs_7_, bf16[64,4096]{1,0:T(8,128)(2,1)} %collective-permute-done.10.refs_4_.refs_5_.ahead_six, ...), custom_call_target="tpu_custom_call" | custom-call | bytes 3145728 | tf_op jit(solution)/shard_map/forward/pallas_call | solution.py:197
  81.0 4.5 %collective-permute-start.13 = (bf16[64,4096]{1,0:T(8,128)(2,1)S(1)}, bf16[64,4096]{1,0:T(8,128)(2,1)S(1)}, u32[]{:S(2)}, u32[]{:S(2)}) collective-permute-start(bf16[64,4096]{1,0:T(8,128)(2,1)S(1)} %get-tuple-element.56), channel_id=1, source_target_pairs={{0,254},{2,4},{4,2},{6,8},{8,6},{10,12},{12,10},{14,16},{16,14},{1... | collective-permute-start | bytes 1572872 | tf_op jit(solution)/shard_map/ppermute | solution.py:19
  85.6 5.6 %hidden.4 = (bf16[64,768]{1,0:T(8,128)(2,1)S(1)}, bf16[64,768]{1,0:T(8,128)(2,1)S(1)}) custom-call(s32[52]{0:T(128)S(1)} %concatenate.7.table, bf16[64,4096]{1,0:T(8,128)(2,1)} %collective-permute-done.4.refs_0_.refs_1_, bf16[64,4096]{1,0:T(8,128)(2,1)} %collective-permute-done.4.refs_0_.refs_1_, ...), custom_call_target="tpu_custom_call" | custom-call | flops 1610612736 | bytes 14680064 | tf_op jit(solution)/shard_map/hidden/pallas_call | solution.py:120
  91.2 2.7 %collective-permute-start.19 = (bf16[64,768]{1,0:T(8,128)(2,1)S(1)}, bf16[64,768]{1,0:T(8,128)(2,1)S(1)}, u32[]{:S(2)}, u32[]{:S(2)}) collective-permute-start(bf16[64,768]{1,0:T(8,128)(2,1)S(1)} %get-tuple-element.52.refs_2_), channel_id=1, source_target_pairs={{0,4},{2,14},{4,8},{6,2},{8,12},{10,6},{12,0},{14,10},{16,20},{18,... | collective-permute-start | bytes 294920 | tf_op jit(solution)/shard_map/ppermute | solution.py:19
  93.9 1.0 collective-permute-start.15
  94.8 2.3 %collective-permute-done.13.refs_4_.refs_5_.refs_10_.refs_11_ = bf16[64,4096]{1,0:T(8,128)(2,1)S(1)} collective-permute-done((bf16[64,4096]{1,0:T(8,128)(2,1)S(1)}, bf16[64,4096]{1,0:T(8,128)(2,1)S(1)}, u32[]{:S(2)}, u32[]{:S(2)}) %collective-permute-start.13) | collective-permute-done | bytes 524320 | tf_op jit(solution)/shard_map/ppermute | solution.py:19
  97.2 6.2 %hidden.5 = (bf16[64,768]{1,0:T(8,128)(2,1)S(1)}, bf16[64,768]{1,0:T(8,128)(2,1)S(1)}, bf16[64,768]{1,0:T(8,128)(2,1)S(1)}) custom-call(s32[52]{0:T(128)S(1)} %concatenate.7.table, bf16[64,4096]{1,0:T(8,128)(2,1)} %collective-permute-done.8.ahead_three.refs_0_.refs_1_, bf16[64,4096]{1,0:T(8,128)(2,1)} %collective-permute-done.8.ahead_three.refs_0_.refs_1_, ...), custom_call_target="tpu_custom_call" | custom-call | flops 2415919104 | bytes 15728640 | tf_op jit(solution)/shard_map/hidden/pallas_call | solution.py:120
  103.5 3.3 %collective-permute-start.17 = (bf16[64,768]{1,0:T(8,128)(2,1)S(1)}, bf16[64,768]{1,0:T(8,128)(2,1)S(1)}, u32[]{:S(2)}, u32[]{:S(2)}) collective-permute-start(bf16[64,768]{1,0:T(8,128)(2,1)S(1)} %get-tuple-element.58.refs_4_), channel_id=1, source_target_pairs={{0,8},{2,10},{4,12},{6,14},{8,0},{10,2},{12,4},{14,6},{16,24},{18,... | collective-permute-start | bytes 294920 | tf_op jit(solution)/shard_map/ppermute | solution.py:19
  106.8 4.0 %collective-permute-done.16.refs_3_ = bf16[64,768]{1,0:T(8,128)(2,1)S(1)} collective-permute-done((bf16[64,768]{1,0:T(8,128)(2,1)S(1)}, bf16[64,768]{1,0:T(8,128)(2,1)S(1)}, u32[]{:S(2)}, u32[]{:S(2)}) %collective-permute-start.16) | collective-permute-done | bytes 98336 | tf_op jit(solution)/shard_map/ppermute | solution.py:19
  110.9 1.3 collective-permute-done.17.refs_4_
  112.1 1.2 collective-permute-done.18.refs_5_
  113.4 0.7 share.1
  114.1 4.8 %collective-permute-start.22 = (bf16[64,768]{1,0:T(8,128)(2,1)S(1)}, bf16[64,768]{1,0:T(8,128)(2,1)S(1)}, u32[]{:S(2)}, u32[]{:S(2)}) collective-permute-start(bf16[64,768]{1,0:T(8,128)(2,1)S(1)} %get-tuple-element.64.last), channel_id=1, source_target_pairs={{0,240},{2,18},{4,244},{6,22},{8,248},{10,26},{12,252},{14,30},{16... | collective-permute-start | bytes 294920 | tf_op jit(solution)/shard_map/ppermute | solution.py:19
  118.9 2.1 %collective-permute-done.21.came_last = bf16[64,768]{1,0:T(8,128)(2,1)S(1)} collective-permute-done((bf16[64,768]{1,0:T(8,128)(2,1)S(1)}, bf16[64,768]{1,0:T(8,128)(2,1)S(1)}, u32[]{:S(2)}, u32[]{:S(2)}) %collective-permute-start.21) | collective-permute-done | bytes 98336 | tf_op jit(solution)/shard_map/ppermute | solution.py:19
  121.0 0.8 send.1
  121.8 3.9 %collective-permute-start.23 = (bf16[64,768]{1,0:T(8,128)(2,1)S(1)}, bf16[64,768]{1,0:T(8,128)(2,1)S(1)}, u32[]{:S(2)}, u32[]{:S(2)}) collective-permute-start(bf16[64,768]{1,0:T(8,128)(2,1)S(1)} %get-tuple-element.66), channel_id=1, source_target_pairs={{0,2},{2,0},{4,6},{6,4},{8,10},{10,8},{12,14},{14,12},{16,18},{18,... | collective-permute-start | bytes 294920 | tf_op jit(solution)/shard_map/ppermute | solution.py:19
  125.7 2.4 %collective-permute-start.24 = (bf16[64,768]{1,0:T(8,128)(2,1)S(1)}, bf16[64,768]{1,0:T(8,128)(2,1)S(1)}, u32[]{:S(2)}, u32[]{:S(2)}) collective-permute-start(bf16[64,768]{1,0:T(8,128)(2,1)S(1)} %get-tuple-element.67), channel_id=1, source_target_pairs={{0,12},{2,6},{4,0},{6,10},{8,4},{10,14},{12,8},{14,2},{16,28},{18,... | collective-permute-start | bytes 294920 | tf_op jit(solution)/shard_map/ppermute | solution.py:19
  128.2 3.1 %collective-permute-start.26 = (bf16[64,768]{1,0:T(8,128)(2,1)S(1)}, bf16[64,768]{1,0:T(8,128)(2,1)S(1)}, u32[]{:S(2)}, u32[]{:S(2)}) collective-permute-start(bf16[64,768]{1,0:T(8,128)(2,1)S(1)} %get-tuple-element.69), channel_id=1, source_target_pairs={{0,8},{2,10},{4,12},{6,14},{8,0},{10,2},{12,4},{14,6},{16,24},{18,... | collective-permute-start | bytes 294920 | tf_op jit(solution)/shard_map/ppermute | solution.py:19
  131.2 2.3 %collective-permute-start.27 = (bf16[64,768]{1,0:T(8,128)(2,1)S(1)}, bf16[64,768]{1,0:T(8,128)(2,1)S(1)}, u32[]{:S(2)}, u32[]{:S(2)}) collective-permute-start(bf16[64,768]{1,0:T(8,128)(2,1)S(1)} %get-tuple-element.70), channel_id=1, source_target_pairs={{0,10},{2,8},{4,14},{6,12},{8,2},{10,0},{12,6},{14,4},{16,26},{18,... | collective-permute-start | bytes 294920 | tf_op jit(solution)/shard_map/ppermute | solution.py:19
  133.5 2.4 %collective-permute-start.28 = (bf16[64,768]{1,0:T(8,128)(2,1)S(1)}, bf16[64,768]{1,0:T(8,128)(2,1)S(1)}, u32[]{:S(2)}, u32[]{:S(2)}) collective-permute-start(bf16[64,768]{1,0:T(8,128)(2,1)S(1)} %get-tuple-element.71), channel_id=1, source_target_pairs={{0,4},{2,14},{4,8},{6,2},{8,12},{10,6},{12,0},{14,10},{16,20},{18,... | collective-permute-start | bytes 294920 | tf_op jit(solution)/shard_map/ppermute | solution.py:19
  136.4 2.0 %collective-permute-done.27.refs_13_ = bf16[64,768]{1,0:T(8,128)(2,1)S(1)} collective-permute-done((bf16[64,768]{1,0:T(8,128)(2,1)S(1)}, bf16[64,768]{1,0:T(8,128)(2,1)S(1)}, u32[]{:S(2)}, u32[]{:S(2)}) %collective-permute-start.27) | collective-permute-done | bytes 98336 | tf_op jit(solution)/shard_map/ppermute | solution.py:19
  138.4 1.0 collective-permute-done.28.refs_14_
  139.5 2.5 %collective-permute-done.29.refs_15_ = bf16[64,768]{1,0:T(8,128)(2,1)S(1)} collective-permute-done((bf16[64,768]{1,0:T(8,128)(2,1)S(1)}, bf16[64,768]{1,0:T(8,128)(2,1)S(1)}, u32[]{:S(2)}, u32[]{:S(2)}) %collective-permute-start.29) | collective-permute-done | bytes 98336 | tf_op jit(solution)/shard_map/ppermute | solution.py:19
  142.0 1.9 %correlate.2 = f32[384,768]{1,0:T(8,128)S(1)} custom-call(s32[52]{0:T(128)S(1)} %concatenate.7.table, bf16[64,768]{1,0:T(8,128)(2,1)S(1)} %get-tuple-element.48.refs_0_, bf16[64,768]{1,0:T(8,128)(2,1)S(1)} %get-tuple-element.49.refs_1_, bf16[64,768]{1,0:T(8,128)(2,1)S(1)} %get-tuple-element.52.refs_2_, bf16[64,768]{1,0:T(8,128)(2,1)S(1)} %get-tuple-element.57.refs_3_, ...), custom_call_target="tpu_custom_call" | custom-call | flops 301989888 | bytes 1572864 | tf_op jit(solution)/shard_map/correlate/pallas_call | solution.py:230
  143.9 11.5 %collective-permute-start.30 = (f32[384,768]{1,0:T(8,128)S(1)}, f32[384,768]{1,0:T(8,128)S(1)}, u32[]{:S(2)}, u32[]{:S(2)}) collective-permute-start(f32[384,768]{1,0:T(8,128)S(1)} %correlate.2), channel_id=1, source_target_pairs={{0,1},{1,0},{2,3},{3,2},{4,5},{5,4},{6,7},{7,6},{8,9},{9,8},{10,11... | collective-permute-start | bytes 3538952 | tf_op jit(solution)/shard_map/ppermute | solution.py:40
  155.4 2.5 %collective-permute-done.30.refs_16_ = f32[384,768]{1,0:T(8,128)S(1)} collective-permute-done((f32[384,768]{1,0:T(8,128)S(1)}, f32[384,768]{1,0:T(8,128)S(1)}, u32[]{:S(2)}, u32[]{:S(2)}) %collective-permute-start.30) | collective-permute-done | bytes 1179680 | tf_op jit(solution)/shard_map/ppermute | solution.py:40
  157.8 2.9 %correlate.3 = f32[384,768]{1,0:T(8,128)} custom-call(s32[52]{0:T(128)S(1)} %concatenate.7.table, bf16[64,768]{1,0:T(8,128)(2,1)S(1)} %get-tuple-element.48.refs_0_, bf16[64,768]{1,0:T(8,128)(2,1)S(1)} %get-tuple-element.49.refs_1_, bf16[64,768]{1,0:T(8,128)(2,1)S(1)} %get-tuple-element.52.refs_2_, bf16[64,768]{1,0:T(8,128)(2,1)S(1)} %get-tuple-element.57.refs_3_, ...), custom_call_target="tpu_custom_call" | custom-call | flops 301989888 | bytes 1572864 | tf_op jit(solution)/shard_map/correlate/pallas_call | solution.py:230
  (45 shorter events, 2.3 us)
Async XLA Ops:
  0.0 24.7 %collective-permute-start.2 = (bf16[2048,768]{1,0:T(8,128)(2,1)}, bf16[2048,768]{1,0:T(8,128)(2,1)S(1)}, u32[]{:S(2)}, u32[]{:S(2)}) collective-permute-start(bf16[2048,768]{1,0:T(8,128)(2,1)} %bitcast.18), channel_id=1, source_target_pairs={{0,1},{1,0},{2,3},{3,2},{4,5},{5,4},{6,7},{7,6},{8,9},{9,8},{10,11... | collective-permute-start | bytes 9437192 | tf_op jit(solution)/shard_map/ppermute | solution.py:40
  3.2 21.5 %collective-permute-start.3 = (bf16[2048,768]{1,0:T(8,128)(2,1)}, bf16[2048,768]{1,0:T(8,128)(2,1)}, u32[]{:S(2)}, u32[]{:S(2)}) collective-permute-start(bf16[2048,768]{1,0:T(8,128)(2,1)} %bitcast.22), channel_id=1, source_target_pairs={{0,1},{1,0},{2,3},{3,2},{4,5},{5,4},{6,7},{7,6},{8,9},{9,8},{10,11... | collective-permute-start | bytes 9437192 | tf_op jit(solution)/shard_map/ppermute | solution.py:40
  3.2 20.6 %collective-permute-start.1 = (bf16[64,4096]{1,0:T(8,128)(2,1)}, bf16[64,4096]{1,0:T(8,128)(2,1)}, u32[]{:S(2)}, u32[]{:S(2)}) collective-permute-start(bf16[64,4096]{1,0:T(8,128)(2,1)} %bitcast.26), channel_id=1, source_target_pairs={{0,254},{2,4},{4,2},{6,8},{8,6},{10,12},{12,10},{14,16},{16,14},{1... | collective-permute-start | bytes 1572872 | tf_op jit(solution)/shard_map/ppermute | solution.py:19
  11.7 13.0 %collective-permute-start = (bf16[64,4096]{1,0:T(8,128)(2,1)}, bf16[64,4096]{1,0:T(8,128)(2,1)}, u32[]{:S(2)}, u32[]{:S(2)}) collective-permute-start(bf16[64,4096]{1,0:T(8,128)(2,1)} %bitcast.27), channel_id=1, source_target_pairs={{0,2},{2,0},{4,6},{6,4},{8,10},{10,8},{12,14},{14,12},{16,18},{18,... | collective-permute-start | bytes 1572872 | tf_op jit(solution)/shard_map/ppermute | solution.py:19
  24.7 12.1 %collective-permute-start.7 = (bf16[64,4096]{1,0:T(8,128)(2,1)}, bf16[64,4096]{1,0:T(8,128)(2,1)}, u32[]{:S(2)}, u32[]{:S(2)}) collective-permute-start(bf16[64,4096]{1,0:T(8,128)(2,1)} %collective-permute-done.1.refs_10_.refs_11_), channel_id=1, source_target_pairs={{0,240},{2,18},{4,244},{6,22},{8,248},{10,26},{12,252},{14,30},{16... | collective-permute-start | bytes 1572872 | tf_op jit(solution)/shard_map/ppermute | solution.py:19
  25.3 11.8 %collective-permute-start.4 = (bf16[64,4096]{1,0:T(8,128)(2,1)}, bf16[64,4096]{1,0:T(8,128)(2,1)}, u32[]{:S(2)}, u32[]{:S(2)}) collective-permute-start(bf16[64,4096]{1,0:T(8,128)(2,1)} %collective-permute-done.1.refs_10_.refs_11_), channel_id=1, source_target_pairs={{0,2},{2,0},{4,6},{6,4},{8,10},{10,8},{12,14},{14,12},{16,18},{18,... | collective-permute-start | bytes 1572872 | tf_op jit(solution)/shard_map/ppermute | solution.py:19
  25.3 26.3 %collective-permute-start.6 = (bf16[64,4096]{1,0:T(8,128)(2,1)}, bf16[64,4096]{1,0:T(8,128)(2,1)}, u32[]{:S(2)}, u32[]{:S(2)}) collective-permute-start(bf16[64,4096]{1,0:T(8,128)(2,1)} %collective-permute-done.refs_4_.refs_5_), channel_id=1, source_target_pairs={{0,16},{2,242},{4,20},{6,246},{8,24},{10,250},{12,28},{14,254},{16... | collective-permute-start | bytes 1572872 | tf_op jit(solution)/shard_map/ppermute | solution.py:19
  26.2 25.4 %collective-permute-start.5 = (bf16[64,4096]{1,0:T(8,128)(2,1)}, bf16[64,4096]{1,0:T(8,128)(2,1)}, u32[]{:S(2)}, u32[]{:S(2)}) collective-permute-start(bf16[64,4096]{1,0:T(8,128)(2,1)} %collective-permute-done.refs_4_.refs_5_), channel_id=1, source_target_pairs={{0,254},{2,4},{4,2},{6,8},{8,6},{10,12},{12,10},{14,16},{16,14},{1... | collective-permute-start | bytes 1572872 | tf_op jit(solution)/shard_map/ppermute | solution.py:19
  51.6 21.2 %collective-permute-start.10 = (bf16[64,4096]{1,0:T(8,128)(2,1)}, bf16[64,4096]{1,0:T(8,128)(2,1)}, u32[]{:S(2)}, u32[]{:S(2)}) collective-permute-start(bf16[64,4096]{1,0:T(8,128)(2,1)} %collective-permute-done.5.refs_6_.refs_7_), channel_id=1, source_target_pairs={{0,240},{2,18},{4,244},{6,22},{8,248},{10,26},{12,252},{14,30},{16... | collective-permute-start | bytes 1572872 | tf_op jit(solution)/shard_map/ppermute | solution.py:19
  52.9 19.9 %collective-permute-start.8 = (bf16[64,4096]{1,0:T(8,128)(2,1)}, bf16[64,4096]{1,0:T(8,128)(2,1)}, u32[]{:S(2)}, u32[]{:S(2)}) collective-permute-start(bf16[64,4096]{1,0:T(8,128)(2,1)} %collective-permute-done.5.refs_6_.refs_7_), channel_id=1, source_target_pairs={{0,2},{2,0},{4,6},{6,4},{8,10},{10,8},{12,14},{14,12},{16,18},{18,... | collective-permute-start | bytes 1572872 | tf_op jit(solution)/shard_map/ppermute | solution.py:19
  52.9 26.4 %collective-permute-start.11 = (bf16[64,4096]{1,0:T(8,128)(2,1)}, bf16[64,4096]{1,0:T(8,128)(2,1)}, u32[]{:S(2)}, u32[]{:S(2)}) collective-permute-start(bf16[64,4096]{1,0:T(8,128)(2,1)} %collective-permute-done.4.refs_0_.refs_1_), channel_id=1, source_target_pairs={{0,16},{2,242},{4,20},{6,246},{8,24},{10,250},{12,28},{14,254},{16... | collective-permute-start | bytes 1572872 | tf_op jit(solution)/shard_map/ppermute | solution.py:19
  53.1 26.2 %collective-permute-start.9 = (bf16[64,4096]{1,0:T(8,128)(2,1)}, bf16[64,4096]{1,0:T(8,128)(2,1)}, u32[]{:S(2)}, u32[]{:S(2)}) collective-permute-start(bf16[64,4096]{1,0:T(8,128)(2,1)} %collective-permute-done.4.refs_0_.refs_1_), channel_id=1, source_target_pairs={{0,254},{2,4},{4,2},{6,8},{8,6},{10,12},{12,10},{14,16},{16,14},{1... | collective-permute-start | bytes 1572872 | tf_op jit(solution)/shard_map/ppermute | solution.py:19
  61.3 1.9 %copy-start = (bf16[1,2048,768]{2,1,0:T(8,128)(2,1)S(1)}, bf16[1,2048,768]{2,1,0:T(8,128)(2,1)}, u32[]{:S(2)}) copy-start(bf16[1,2048,768]{2,1,0:T(8,128)(2,1)} %param.6) | copy-start | bytes 9437188
  63.2 1.9 %copy-start.2 = (bf16[1,2048,768]{2,1,0:T(8,128)(2,1)S(1)}, bf16[1,2048,768]{2,1,0:T(8,128)(2,1)}, u32[]{:S(2)}) copy-start(bf16[1,2048,768]{2,1,0:T(8,128)(2,1)} %param.7) | copy-start | bytes 9437188
  65.1 1.0 copy-start.4
  66.1 19.5 %copy-start.1 = (bf16[1,2048,768]{2,1,0:T(8,128)(2,1)S(1)}, bf16[1,2048,768]{2,1,0:T(8,128)(2,1)}, u32[]{:S(2)}) copy-start(bf16[1,2048,768]{2,1,0:T(8,128)(2,1)} %param.6) | copy-start | bytes 9437188
  66.1 19.5 %copy-start.3 = (bf16[1,2048,768]{2,1,0:T(8,128)(2,1)S(1)}, bf16[1,2048,768]{2,1,0:T(8,128)(2,1)}, u32[]{:S(2)}) copy-start(bf16[1,2048,768]{2,1,0:T(8,128)(2,1)} %param.7) | copy-start | bytes 9437188
  80.9 12.9 %collective-permute-start.12 = (bf16[64,4096]{1,0:T(8,128)(2,1)S(1)}, bf16[64,4096]{1,0:T(8,128)(2,1)S(1)}, u32[]{:S(2)}, u32[]{:S(2)}) collective-permute-start(bf16[64,4096]{1,0:T(8,128)(2,1)S(1)} %get-tuple-element.55), channel_id=1, source_target_pairs={{0,2},{2,0},{4,6},{6,4},{8,10},{10,8},{12,14},{14,12},{16,18},{18,... | collective-permute-start | bytes 1572872 | tf_op jit(solution)/shard_map/ppermute | solution.py:19
  81.0 16.1 %collective-permute-start.13 = (bf16[64,4096]{1,0:T(8,128)(2,1)S(1)}, bf16[64,4096]{1,0:T(8,128)(2,1)S(1)}, u32[]{:S(2)}, u32[]{:S(2)}) collective-permute-start(bf16[64,4096]{1,0:T(8,128)(2,1)S(1)} %get-tuple-element.56), channel_id=1, source_target_pairs={{0,254},{2,4},{4,2},{6,8},{8,6},{10,12},{12,10},{14,16},{16,14},{1... | collective-permute-start | bytes 1572872 | tf_op jit(solution)/shard_map/ppermute | solution.py:19
  85.6 17.9 %collective-permute-start.14 = (bf16[64,768]{1,0:T(8,128)(2,1)S(1)}, bf16[64,768]{1,0:T(8,128)(2,1)S(1)}, u32[]{:S(2)}, u32[]{:S(2)}) collective-permute-start(bf16[64,768]{1,0:T(8,128)(2,1)S(1)} %get-tuple-element.49.refs_1_), channel_id=1, source_target_pairs={{0,2},{2,0},{4,6},{6,4},{8,10},{10,8},{12,14},{14,12},{16,18},{18,... | collective-permute-start | bytes 294920 | tf_op jit(solution)/shard_map/ppermute | solution.py:19
  85.6 21.2 %collective-permute-start.20 = (bf16[64,768]{1,0:T(8,128)(2,1)S(1)}, bf16[64,768]{1,0:T(8,128)(2,1)S(1)}, u32[]{:S(2)}, u32[]{:S(2)}) collective-permute-start(bf16[64,768]{1,0:T(8,128)(2,1)S(1)} %get-tuple-element.61.refs_7_), channel_id=1, source_target_pairs={{0,14},{2,4},{4,2},{6,8},{8,6},{10,12},{12,10},{14,0},{16,30},{18,... | collective-permute-start | bytes 294920 | tf_op jit(solution)/shard_map/ppermute | solution.py:19
  91.2 15.6 %collective-permute-start.19 = (bf16[64,768]{1,0:T(8,128)(2,1)S(1)}, bf16[64,768]{1,0:T(8,128)(2,1)S(1)}, u32[]{:S(2)}, u32[]{:S(2)}) collective-permute-start(bf16[64,768]{1,0:T(8,128)(2,1)S(1)} %get-tuple-element.52.refs_2_), channel_id=1, source_target_pairs={{0,4},{2,14},{4,8},{6,2},{8,12},{10,6},{12,0},{14,10},{16,20},{18,... | collective-permute-start | bytes 294920 | tf_op jit(solution)/shard_map/ppermute | solution.py:19
  93.9 12.9 %collective-permute-start.15 = (bf16[64,768]{1,0:T(8,128)(2,1)S(1)}, bf16[64,768]{1,0:T(8,128)(2,1)S(1)}, u32[]{:S(2)}, u32[]{:S(2)}) collective-permute-start(bf16[64,768]{1,0:T(8,128)(2,1)S(1)} %get-tuple-element.60.refs_6_), channel_id=1, source_target_pairs={{0,12},{2,6},{4,0},{6,10},{8,4},{10,14},{12,8},{14,2},{16,28},{18,... | collective-permute-start | bytes 294920 | tf_op jit(solution)/shard_map/ppermute | solution.py:19
  103.4 7.5 %collective-permute-start.16 = (bf16[64,768]{1,0:T(8,128)(2,1)S(1)}, bf16[64,768]{1,0:T(8,128)(2,1)S(1)}, u32[]{:S(2)}, u32[]{:S(2)}) collective-permute-start(bf16[64,768]{1,0:T(8,128)(2,1)S(1)} %get-tuple-element.57.refs_3_), channel_id=1, source_target_pairs={{0,6},{2,12},{4,10},{6,0},{8,14},{10,4},{12,2},{14,8},{16,22},{18,... | collective-permute-start | bytes 294920 | tf_op jit(solution)/shard_map/ppermute | solution.py:19
  103.5 8.6 %collective-permute-start.17 = (bf16[64,768]{1,0:T(8,128)(2,1)S(1)}, bf16[64,768]{1,0:T(8,128)(2,1)S(1)}, u32[]{:S(2)}, u32[]{:S(2)}) collective-permute-start(bf16[64,768]{1,0:T(8,128)(2,1)S(1)} %get-tuple-element.58.refs_4_), channel_id=1, source_target_pairs={{0,8},{2,10},{4,12},{6,14},{8,0},{10,2},{12,4},{14,6},{16,24},{18,... | collective-permute-start | bytes 294920 | tf_op jit(solution)/shard_map/ppermute | solution.py:19
  106.8 6.6 %collective-permute-start.18 = (bf16[64,768]{1,0:T(8,128)(2,1)S(1)}, bf16[64,768]{1,0:T(8,128)(2,1)S(1)}, u32[]{:S(2)}, u32[]{:S(2)}) collective-permute-start(bf16[64,768]{1,0:T(8,128)(2,1)S(1)} %get-tuple-element.59.refs_5_), channel_id=1, source_target_pairs={{0,10},{2,8},{4,14},{6,12},{8,2},{10,0},{12,6},{14,4},{16,26},{18,... | collective-permute-start | bytes 294920 | tf_op jit(solution)/shard_map/ppermute | solution.py:19
  114.0 7.0 %collective-permute-start.21 = (bf16[64,768]{1,0:T(8,128)(2,1)S(1)}, bf16[64,768]{1,0:T(8,128)(2,1)S(1)}, u32[]{:S(2)}, u32[]{:S(2)}) collective-permute-start(bf16[64,768]{1,0:T(8,128)(2,1)S(1)} %get-tuple-element.63.nxt), channel_id=1, source_target_pairs={{0,16},{2,242},{4,20},{6,246},{8,24},{10,250},{12,28},{14,254},{16... | collective-permute-start | bytes 294920 | tf_op jit(solution)/shard_map/ppermute | solution.py:19
  114.1 6.9 %collective-permute-start.22 = (bf16[64,768]{1,0:T(8,128)(2,1)S(1)}, bf16[64,768]{1,0:T(8,128)(2,1)S(1)}, u32[]{:S(2)}, u32[]{:S(2)}) collective-permute-start(bf16[64,768]{1,0:T(8,128)(2,1)S(1)} %get-tuple-element.64.last), channel_id=1, source_target_pairs={{0,240},{2,18},{4,244},{6,22},{8,248},{10,26},{12,252},{14,30},{16... | collective-permute-start | bytes 294920 | tf_op jit(solution)/shard_map/ppermute | solution.py:19
  121.8 11.7 %collective-permute-start.23 = (bf16[64,768]{1,0:T(8,128)(2,1)S(1)}, bf16[64,768]{1,0:T(8,128)(2,1)S(1)}, u32[]{:S(2)}, u32[]{:S(2)}) collective-permute-start(bf16[64,768]{1,0:T(8,128)(2,1)S(1)} %get-tuple-element.66), channel_id=1, source_target_pairs={{0,2},{2,0},{4,6},{6,4},{8,10},{10,8},{12,14},{14,12},{16,18},{18,... | collective-permute-start | bytes 294920 | tf_op jit(solution)/shard_map/ppermute | solution.py:19
  125.7 10.2 %collective-permute-start.24 = (bf16[64,768]{1,0:T(8,128)(2,1)S(1)}, bf16[64,768]{1,0:T(8,128)(2,1)S(1)}, u32[]{:S(2)}, u32[]{:S(2)}) collective-permute-start(bf16[64,768]{1,0:T(8,128)(2,1)S(1)} %get-tuple-element.67), channel_id=1, source_target_pairs={{0,12},{2,6},{4,0},{6,10},{8,4},{10,14},{12,8},{14,2},{16,28},{18,... | collective-permute-start | bytes 294920 | tf_op jit(solution)/shard_map/ppermute | solution.py:19
  128.2 7.8 %collective-permute-start.25 = (bf16[64,768]{1,0:T(8,128)(2,1)S(1)}, bf16[64,768]{1,0:T(8,128)(2,1)S(1)}, u32[]{:S(2)}, u32[]{:S(2)}) collective-permute-start(bf16[64,768]{1,0:T(8,128)(2,1)S(1)} %get-tuple-element.68), channel_id=1, source_target_pairs={{0,6},{2,12},{4,10},{6,0},{8,14},{10,4},{12,2},{14,8},{16,22},{18,... | collective-permute-start | bytes 294920 | tf_op jit(solution)/shard_map/ppermute | solution.py:19
  128.2 8.2 %collective-permute-start.26 = (bf16[64,768]{1,0:T(8,128)(2,1)S(1)}, bf16[64,768]{1,0:T(8,128)(2,1)S(1)}, u32[]{:S(2)}, u32[]{:S(2)}) collective-permute-start(bf16[64,768]{1,0:T(8,128)(2,1)S(1)} %get-tuple-element.69), channel_id=1, source_target_pairs={{0,8},{2,10},{4,12},{6,14},{8,0},{10,2},{12,4},{14,6},{16,24},{18,... | collective-permute-start | bytes 294920 | tf_op jit(solution)/shard_map/ppermute | solution.py:19
  131.2 7.2 %collective-permute-start.27 = (bf16[64,768]{1,0:T(8,128)(2,1)S(1)}, bf16[64,768]{1,0:T(8,128)(2,1)S(1)}, u32[]{:S(2)}, u32[]{:S(2)}) collective-permute-start(bf16[64,768]{1,0:T(8,128)(2,1)S(1)} %get-tuple-element.70), channel_id=1, source_target_pairs={{0,10},{2,8},{4,14},{6,12},{8,2},{10,0},{12,6},{14,4},{16,26},{18,... | collective-permute-start | bytes 294920 | tf_op jit(solution)/shard_map/ppermute | solution.py:19
  133.5 6.0 %collective-permute-start.28 = (bf16[64,768]{1,0:T(8,128)(2,1)S(1)}, bf16[64,768]{1,0:T(8,128)(2,1)S(1)}, u32[]{:S(2)}, u32[]{:S(2)}) collective-permute-start(bf16[64,768]{1,0:T(8,128)(2,1)S(1)} %get-tuple-element.71), channel_id=1, source_target_pairs={{0,4},{2,14},{4,8},{6,2},{8,12},{10,6},{12,0},{14,10},{16,20},{18,... | collective-permute-start | bytes 294920 | tf_op jit(solution)/shard_map/ppermute | solution.py:19
  135.9 6.1 %collective-permute-start.29 = (bf16[64,768]{1,0:T(8,128)(2,1)S(1)}, bf16[64,768]{1,0:T(8,128)(2,1)S(1)}, u32[]{:S(2)}, u32[]{:S(2)}) collective-permute-start(bf16[64,768]{1,0:T(8,128)(2,1)S(1)} %get-tuple-element.72), channel_id=1, source_target_pairs={{0,14},{2,4},{4,2},{6,8},{8,6},{10,12},{12,10},{14,0},{16,30},{18,... | collective-permute-start | bytes 294920 | tf_op jit(solution)/shard_map/ppermute | solution.py:19
  143.9 14.0 %collective-permute-start.30 = (f32[384,768]{1,0:T(8,128)S(1)}, f32[384,768]{1,0:T(8,128)S(1)}, u32[]{:S(2)}, u32[]{:S(2)}) collective-permute-start(f32[384,768]{1,0:T(8,128)S(1)} %correlate.2), channel_id=1, source_target_pairs={{0,1},{1,0},{2,3},{3,2},{4,5},{5,4},{6,7},{7,6},{8,9},{9,8},{10,11... | collective-permute-start | bytes 3538952 | tf_op jit(solution)/shard_map/ppermute | solution.py:40

commit v3 on v2

--- a/solution.py
+++ b/solution.py
@@ -16,23 +16,32 @@
 
 def moved(value, target):
     count = lax.axis_size("expert")
-    return lax.ppermute(value, "expert", [(i, target(i) % count) for i in range(count)])
+    return lax.ppermute(value, "expert", [(i, target(i, count)) for i in range(count)])
 
 
 def with_next(value):
-    return moved(value, lambda i: i + 1 - 2 * (i % 2))
-
-
-def with_last(value):
-    return moved(value, lambda i: i - 1 + 2 * (i % 2))
-
-
-def to_line(value, step):
-    return moved(value, lambda i: i + step * LINE * (1 - 2 * (i % 2)))
+    return moved(value, lambda i, count: i + 1 - 2 * (i % 2))
+
+
+def with_last(value, cyclic=True):
+    def target(i, count):
+        other = i - 1 + 2 * (i % 2)
+        return other if 0 <= other < count else other % count if cyclic else i
+
+    return moved(value, target)
+
+
+def to_line(value, step, cyclic=True):
+    def target(i, count):
+        turn = 1 - 2 * (i % 2)
+        other = i + step * LINE * turn
+        return other if 0 <= other < count else other % count if cyclic else i + turn
+
+    return moved(value, target)
 
 
 def round_line(value, offset):
-    turn = lambda i: i // LINE * LINE + (i + offset * (1 - 2 * (i % 2))) % LINE
+    turn = lambda i, count: i // LINE * LINE + (i + offset * (1 - 2 * (i % 2))) % LINE
     return moved(value, turn), (offset if offset % 2 else LINE - offset)
 
 
@@ -257,7 +266,7 @@
     behind[6], ahead[2] = with_last(ahead[1]), with_next(behind[7])
     behind[1], ahead[7] = to_line(ahead[1], 1), to_line(behind[7], -1)
     ahead[2], behind[6], behind[1], ahead[7] = after(ahead[2], behind[6], behind[1], ahead[7])
-    behind[5], ahead[3] = with_last(ahead[2]), with_next(behind[6])
+    behind[5], ahead[3] = with_last(ahead[2], cyclic=False), with_next(behind[6])
     behind[2], ahead[6] = to_line(ahead[2], 1), to_line(behind[6], -1)
 
     hidden, returned = {}, {}
@@ -280,7 +289,7 @@
     hidden[0] = returned[0] = own_hidden
 
     shares = choose(share_kernel, table, [returned[k] for k in range(LINE)], 3, "share")
-    came_last, came_next = to_line(shares[1], 1), to_line(shares[2], -1)
+    came_last, came_next = to_line(shares[1], 1, cyclic=False), to_line(shares[2], -1, cyclic=False)
     chunks = choose(send_kernel, table, [*shares, came_last, came_next], LINE, "send")
     panel = {0: chunks[0]}
     for away in range(1, LINE):

time: 161 us -> 153 us (0.950); the launches traced: 161 us -> 151 us
  waiting for transfers between devices: 56 us -> 49.9 us
  starting transfers between devices: 68.7 us -> 65 us
    ppermute x28, waiting for transfers between devices: 53.5 us -> 47.4 us  [moved(): lax.ppermute(value, 'expert', [(i, target(i, count)) for i in range(count)])]
    ppermute x3, starting transfers between devices: 14.7 us -> 11.4 us  [swap_cores(): return lax.ppermute(value, 'row', [(0, 1), (1, 0)])]
  transfers between devices with their start and end apart: 31 -> 31, of which waited for: 16 -> 14; matrix products, arithmetic and copies ran while one was open for 3% -> 3% of each run, Pallas kernels for 12% -> 12%
where the time goes in v3:
time: 153 us; the launch traced here: 151 us
  starting transfers between devices  65 us (42%)
  waiting for transfers between devices  49.9 us (33%)
  Pallas kernels  26.4 us (17%)
  local copies, waits for them, and re-layouts  6.33 us (4%)
  other arithmetic  3.2 us (2%)
    ppermute x28, starting transfers between devices, moved(): lax.ppermute(value, 'expert', [(i, target(i, count)) for i in range(count)])  53.6 us
    ppermute x28, waiting for transfers between devices, moved(): lax.ppermute(value, 'expert', [(i, target(i, count)) for i in range(count)])  47.4 us
    pallas_call x3, Pallas kernels, hidden_of(): pl.pallas_call(functools.partial(hidden_kernel, group), out_shape=[jax.Sh...  18.5 us
    ppermute x3, starting transfers between devices, swap_cores(): return lax.ppermute(value, 'row', [(0, 1), (1, 0)])  11.4 us
    unnamed x10, local copies, waits for them, and re-layouts  4.83 us
    pallas_call x2, Pallas kernels, correlate(): pl.pallas_call(functools.partial(correlate_kernel, add), out_shape=jax.Sh...  4.76 us
    pallas_call x3, Pallas kernels, choose(): pl.pallas_call(kernel, out_shape=[shape] * outs, in_specs=[pl.BlockSpec(m...  3.1 us
  transfers between devices with their start and end apart: 31, of which 14 were waited for; matrix products, arithmetic and copies ran while one was open for 3% of the time, Pallas kernels for 12%

profile of v3, /device:TPU:1, one launch (start us, length us, event | category | flops | bytes accessed | tf_op | source)
XLA Modules:
  0.0 151.0 jit_solution(7109506674149163923)
XLA Ops:
  0.0 3.2 %collective-permute-start.2 = (bf16[2048,768]{1,0:T(8,128)(2,1)}, bf16[2048,768]{1,0:T(8,128)(2,1)S(1)}, u32[]{:S(2)}, u32[]{:S(2)}) collective-permute-start(bf16[2048,768]{1,0:T(8,128)(2,1)} %bitcast.18), channel_id=1, source_target_pairs={{0,1},{1,0},{2,3},{3,2},{4,5},{5,4},{6,7},{7,6},{8,9},{9,8},{10,11... | collective-permute-start | bytes 9437192 | tf_op jit(solution)/shard_map/ppermute | solution.py:49
  3.2 8.5 %collective-permute-start.1 = (bf16[64,4096]{1,0:T(8,128)(2,1)}, bf16[64,4096]{1,0:T(8,128)(2,1)}, u32[]{:S(2)}, u32[]{:S(2)}) collective-permute-start(bf16[64,4096]{1,0:T(8,128)(2,1)} %bitcast.26), channel_id=1, source_target_pairs={{0,254},{2,4},{4,2},{6,8},{8,6},{10,12},{12,10},{14,16},{16,14},{1... | collective-permute-start | bytes 1572872 | tf_op jit(solution)/shard_map/ppermute | solution.py:19
  11.7 12.1 %collective-permute-done.1.refs_10_.refs_11_ = bf16[64,4096]{1,0:T(8,128)(2,1)} collective-permute-done((bf16[64,4096]{1,0:T(8,128)(2,1)}, bf16[64,4096]{1,0:T(8,128)(2,1)}, u32[]{:S(2)}, u32[]{:S(2)}) %collective-permute-start.1) | collective-permute-done | bytes 524320 | tf_op jit(solution)/shard_map/ppermute | solution.py:19
  23.9 0.8 collective-permute-done.refs_4_.refs_5_
  24.7 0.6 collective-permute-start.7
  25.3 0.9 collective-permute-start.6
  26.2 5.8 %collective-permute-start.5 = (bf16[64,4096]{1,0:T(8,128)(2,1)}, bf16[64,4096]{1,0:T(8,128)(2,1)}, u32[]{:S(2)}, u32[]{:S(2)}) collective-permute-start(bf16[64,4096]{1,0:T(8,128)(2,1)} %collective-permute-done.refs_4_.refs_5_), channel_id=1, source_target_pairs={{0,254},{2,4},{4,2},{6,8},{8,6},{10,12},{12,10},{14,16},{16,14},{1... | collective-permute-start | bytes 1572872 | tf_op jit(solution)/shard_map/ppermute | solution.py:19
  32.0 0.8 select_reduce_fusion
  32.8 0.9 convert_reduce_fusion.1
  33.8 0.7 pad_add_fusion.1
  34.6 2.2 %collective-permute-done.7.refs_8_.refs_9_ = bf16[64,4096]{1,0:T(8,128)(2,1)} collective-permute-done((bf16[64,4096]{1,0:T(8,128)(2,1)}, bf16[64,4096]{1,0:T(8,128)(2,1)}, u32[]{:S(2)}, u32[]{:S(2)}) %collective-permute-start.7) | collective-permute-done | bytes 524320 | tf_op jit(solution)/shard_map/ppermute | solution.py:19
  37.0 14.6 %collective-permute-done.6.refs_6_.refs_7_ = bf16[64,4096]{1,0:T(8,128)(2,1)} collective-permute-done((bf16[64,4096]{1,0:T(8,128)(2,1)}, bf16[64,4096]{1,0:T(8,128)(2,1)}, u32[]{:S(2)}, u32[]{:S(2)}) %collective-permute-start.6) | collective-permute-done | bytes 524320 | tf_op jit(solution)/shard_map/ppermute | solution.py:19
  51.6 1.3 collective-permute-start.10
  53.1 5.3 %collective-permute-start.9 = (bf16[64,4096]{1,0:T(8,128)(2,1)}, bf16[64,4096]{1,0:T(8,128)(2,1)}, u32[]{:S(2)}, u32[]{:S(2)}) collective-permute-start(bf16[64,4096]{1,0:T(8,128)(2,1)} %collective-permute-done.4.refs_0_.refs_1_), channel_id=1, source_target_pairs={{0,0},{2,4},{4,2},{6,8},{8,6},{10,12},{12,10},{14,16},{16,14},{18,... | collective-permute-start | bytes 1572872 | tf_op jit(solution)/shard_map/ppermute | solution.py:19
  58.4 0.7 fusion
  59.9 0.6 concatenate.7.table
  60.6 1.9 %copy-done = bf16[1,2048,768]{2,1,0:T(8,128)(2,1)S(1)} copy-done((bf16[1,2048,768]{2,1,0:T(8,128)(2,1)S(1)}, bf16[1,2048,768]{2,1,0:T(8,128)(2,1)}, u32[]{:S(2)}) %copy-start) | copy-done | bytes 3145752
  62.5 1.9 %copy-done.2 = bf16[1,2048,768]{2,1,0:T(8,128)(2,1)S(1)} copy-done((bf16[1,2048,768]{2,1,0:T(8,128)(2,1)S(1)}, bf16[1,2048,768]{2,1,0:T(8,128)(2,1)}, u32[]{:S(2)}) %copy-start.2) | copy-done | bytes 3145752
  64.4 1.0 copy-done.4
  65.4 6.7 %hidden.3 = (bf16[64,768]{1,0:T(8,128)(2,1)S(1)}, bf16[64,768]{1,0:T(8,128)(2,1)S(1)}, bf16[64,768]{1,0:T(8,128)(2,1)S(1)}) custom-call(s32[52]{0:T(128)S(1)} %concatenate.7.table, bf16[64,4096]{1,0:T(8,128)(2,1)S(1)} %bitcast.28, bf16[64,4096]{1,0:T(8,128)(2,1)S(1)} %bitcast.29, bf16[64,4096]{1,0:T(8,128)(2,1)S(1)} %bitcast.30, ...), custom_call_target="tpu_custom_call" | custom-call | flops 2415919104 | bytes 15728640 | tf_op jit(solution)/shard_map/hidden/pallas_call | solution.py:129
  72.1 0.5 collective-permute-done.11.refs_2_.refs_3_.back_six
  72.7 1.6 %forward.1 = (bf16[64,4096]{1,0:T(8,128)(2,1)S(1)}, bf16[64,4096]{1,0:T(8,128)(2,1)S(1)}) custom-call(s32[52]{0:T(128)S(1)} %concatenate.7.table, bf16[64,4096]{1,0:T(8,128)(2,1)} %collective-permute-done.9.back_three.refs_6_.refs_7_, bf16[64,4096]{1,0:T(8,128)(2,1)} %collective-permute-done.10.refs_4_.refs_5_.ahead_six, ...), custom_call_target="tpu_custom_call" | custom-call | bytes 3145728 | tf_op jit(solution)/shard_map/forward/pallas_call | solution.py:206
  74.4 6.7 %collective-permute-start.13 = (bf16[64,4096]{1,0:T(8,128)(2,1)S(1)}, bf16[64,4096]{1,0:T(8,128)(2,1)S(1)}, u32[]{:S(2)}, u32[]{:S(2)}) collective-permute-start(bf16[64,4096]{1,0:T(8,128)(2,1)S(1)} %get-tuple-element.56), channel_id=1, source_target_pairs={{0,254},{2,4},{4,2},{6,8},{8,6},{10,12},{12,10},{14,16},{16,14},{1... | collective-permute-start | bytes 1572872 | tf_op jit(solution)/shard_map/ppermute | solution.py:19
  81.2 5.6 %hidden.4 = (bf16[64,768]{1,0:T(8,128)(2,1)S(1)}, bf16[64,768]{1,0:T(8,128)(2,1)S(1)}) custom-call(s32[52]{0:T(128)S(1)} %concatenate.7.table, bf16[64,4096]{1,0:T(8,128)(2,1)} %collective-permute-done.4.refs_0_.refs_1_, bf16[64,4096]{1,0:T(8,128)(2,1)} %collective-permute-done.4.refs_0_.refs_1_, ...), custom_call_target="tpu_custom_call" | custom-call | flops 1610612736 | bytes 14680064 | tf_op jit(solution)/shard_map/hidden/pallas_call | solution.py:129
  86.8 2.9 %collective-permute-start.19 = (bf16[64,768]{1,0:T(8,128)(2,1)S(1)}, bf16[64,768]{1,0:T(8,128)(2,1)S(1)}, u32[]{:S(2)}, u32[]{:S(2)}) collective-permute-start(bf16[64,768]{1,0:T(8,128)(2,1)S(1)} %get-tuple-element.52.refs_2_), channel_id=1, source_target_pairs={{0,4},{2,14},{4,8},{6,2},{8,12},{10,6},{12,0},{14,10},{16,20},{18,... | collective-permute-start | bytes 294920 | tf_op jit(solution)/shard_map/ppermute | solution.py:19
  89.6 1.0 collective-permute-start.15
  90.6 6.2 %hidden.5 = (bf16[64,768]{1,0:T(8,128)(2,1)S(1)}, bf16[64,768]{1,0:T(8,128)(2,1)S(1)}, bf16[64,768]{1,0:T(8,128)(2,1)S(1)}) custom-call(s32[52]{0:T(128)S(1)} %concatenate.7.table, bf16[64,4096]{1,0:T(8,128)(2,1)} %collective-permute-done.8.ahead_three.refs_0_.refs_1_, bf16[64,4096]{1,0:T(8,128)(2,1)} %collective-permute-done.8.ahead_three.refs_0_.refs_1_, ...), custom_call_target="tpu_custom_call" | custom-call | flops 2415919104 | bytes 15728640 | tf_op jit(solution)/shard_map/hidden/pallas_call | solution.py:129
  96.9 5.6 %collective-permute-start.17 = (bf16[64,768]{1,0:T(8,128)(2,1)S(1)}, bf16[64,768]{1,0:T(8,128)(2,1)S(1)}, u32[]{:S(2)}, u32[]{:S(2)}) collective-permute-start(bf16[64,768]{1,0:T(8,128)(2,1)S(1)} %get-tuple-element.58.refs_4_), channel_id=1, source_target_pairs={{0,8},{2,10},{4,12},{6,14},{8,0},{10,2},{12,4},{14,6},{16,24},{18,... | collective-permute-start | bytes 294920 | tf_op jit(solution)/shard_map/ppermute | solution.py:19
  102.6 5.2 %collective-permute-done.17.refs_4_ = bf16[64,768]{1,0:T(8,128)(2,1)S(1)} collective-permute-done((bf16[64,768]{1,0:T(8,128)(2,1)S(1)}, bf16[64,768]{1,0:T(8,128)(2,1)S(1)}, u32[]{:S(2)}, u32[]{:S(2)}) %collective-permute-start.17) | collective-permute-done | bytes 98336 | tf_op jit(solution)/shard_map/ppermute | solution.py:19
  107.8 1.9 %collective-permute-done.18.refs_5_ = bf16[64,768]{1,0:T(8,128)(2,1)S(1)} collective-permute-done((bf16[64,768]{1,0:T(8,128)(2,1)S(1)}, bf16[64,768]{1,0:T(8,128)(2,1)S(1)}, u32[]{:S(2)}, u32[]{:S(2)}) %collective-permute-start.18) | collective-permute-done | bytes 98336 | tf_op jit(solution)/shard_map/ppermute | solution.py:19
  109.7 0.7 share.1
  110.5 2.5 %collective-permute-start.22 = (bf16[64,768]{1,0:T(8,128)(2,1)S(1)}, bf16[64,768]{1,0:T(8,128)(2,1)S(1)}, u32[]{:S(2)}, u32[]{:S(2)}) collective-permute-start(bf16[64,768]{1,0:T(8,128)(2,1)S(1)} %get-tuple-element.64.last), channel_id=1, source_target_pairs={{0,2},{2,18},{4,6},{6,22},{8,10},{10,26},{12,14},{14,30},{16,0},{1... | collective-permute-start | bytes 294920 | tf_op jit(solution)/shard_map/ppermute | solution.py:19
  113.0 2.4 %collective-permute-done.21.came_last = bf16[64,768]{1,0:T(8,128)(2,1)S(1)} collective-permute-done((bf16[64,768]{1,0:T(8,128)(2,1)S(1)}, bf16[64,768]{1,0:T(8,128)(2,1)S(1)}, u32[]{:S(2)}, u32[]{:S(2)}) %collective-permute-start.21) | collective-permute-done | bytes 98336 | tf_op jit(solution)/shard_map/ppermute | solution.py:19
  115.4 0.8 send.1
  116.2 1.2 collective-permute-start.23
  117.4 3.1 %collective-permute-start.24 = (bf16[64,768]{1,0:T(8,128)(2,1)S(1)}, bf16[64,768]{1,0:T(8,128)(2,1)S(1)}, u32[]{:S(2)}, u32[]{:S(2)}) collective-permute-start(bf16[64,768]{1,0:T(8,128)(2,1)S(1)} %get-tuple-element.67), channel_id=1, source_target_pairs={{0,12},{2,6},{4,0},{6,10},{8,4},{10,14},{12,8},{14,2},{16,28},{18,... | collective-permute-start | bytes 294920 | tf_op jit(solution)/shard_map/ppermute | solution.py:19
  120.4 0.9 collective-permute-start.25
  121.4 1.8 %collective-permute-start.26 = (bf16[64,768]{1,0:T(8,128)(2,1)S(1)}, bf16[64,768]{1,0:T(8,128)(2,1)S(1)}, u32[]{:S(2)}, u32[]{:S(2)}) collective-permute-start(bf16[64,768]{1,0:T(8,128)(2,1)S(1)} %get-tuple-element.69), channel_id=1, source_target_pairs={{0,8},{2,10},{4,12},{6,14},{8,0},{10,2},{12,4},{14,6},{16,24},{18,... | collective-permute-start | bytes 294920 | tf_op jit(solution)/shard_map/ppermute | solution.py:19
  123.1 2.7 %collective-permute-start.27 = (bf16[64,768]{1,0:T(8,128)(2,1)S(1)}, bf16[64,768]{1,0:T(8,128)(2,1)S(1)}, u32[]{:S(2)}, u32[]{:S(2)}) collective-permute-start(bf16[64,768]{1,0:T(8,128)(2,1)S(1)} %get-tuple-element.70), channel_id=1, source_target_pairs={{0,10},{2,8},{4,14},{6,12},{8,2},{10,0},{12,6},{14,4},{16,26},{18,... | collective-permute-start | bytes 294920 | tf_op jit(solution)/shard_map/ppermute | solution.py:19
  125.8 2.4 %collective-permute-start.28 = (bf16[64,768]{1,0:T(8,128)(2,1)S(1)}, bf16[64,768]{1,0:T(8,128)(2,1)S(1)}, u32[]{:S(2)}, u32[]{:S(2)}) collective-permute-start(bf16[64,768]{1,0:T(8,128)(2,1)S(1)} %get-tuple-element.71), channel_id=1, source_target_pairs={{0,4},{2,14},{4,8},{6,2},{8,12},{10,6},{12,0},{14,10},{16,20},{18,... | collective-permute-start | bytes 294920 | tf_op jit(solution)/shard_map/ppermute | solution.py:19
  128.2 0.8 collective-permute-done.26.refs_12_
  129.0 2.1 %collective-permute-done.27.refs_13_ = bf16[64,768]{1,0:T(8,128)(2,1)S(1)} collective-permute-done((bf16[64,768]{1,0:T(8,128)(2,1)S(1)}, bf16[64,768]{1,0:T(8,128)(2,1)S(1)}, u32[]{:S(2)}, u32[]{:S(2)}) %collective-permute-start.27) | collective-permute-done | bytes 98336 | tf_op jit(solution)/shard_map/ppermute | solution.py:19
  131.1 2.2 %collective-permute-done.28.refs_14_ = bf16[64,768]{1,0:T(8,128)(2,1)S(1)} collective-permute-done((bf16[64,768]{1,0:T(8,128)(2,1)S(1)}, bf16[64,768]{1,0:T(8,128)(2,1)S(1)}, u32[]{:S(2)}, u32[]{:S(2)}) %collective-permute-start.28) | collective-permute-done | bytes 98336 | tf_op jit(solution)/shard_map/ppermute | solution.py:19
  133.3 2.3 %collective-permute-done.29.refs_15_ = bf16[64,768]{1,0:T(8,128)(2,1)S(1)} collective-permute-done((bf16[64,768]{1,0:T(8,128)(2,1)S(1)}, bf16[64,768]{1,0:T(8,128)(2,1)S(1)}, u32[]{:S(2)}, u32[]{:S(2)}) %collective-permute-start.29) | collective-permute-done | bytes 98336 | tf_op jit(solution)/shard_map/ppermute | solution.py:19
  135.6 1.9 %correlate.2 = f32[384,768]{1,0:T(8,128)S(1)} custom-call(s32[52]{0:T(128)S(1)} %concatenate.7.table, bf16[64,768]{1,0:T(8,128)(2,1)S(1)} %get-tuple-element.48.refs_0_, bf16[64,768]{1,0:T(8,128)(2,1)S(1)} %get-tuple-element.49.refs_1_, bf16[64,768]{1,0:T(8,128)(2,1)S(1)} %get-tuple-element.52.refs_2_, bf16[64,768]{1,0:T(8,128)(2,1)S(1)} %get-tuple-element.57.refs_3_, ...), custom_call_target="tpu_custom_call" | custom-call | flops 301989888 | bytes 1572864 | tf_op jit(solution)/shard_map/correlate/pallas_call | solution.py:239
  137.4 8.1 %collective-permute-start.30 = (f32[384,768]{1,0:T(8,128)S(1)}, f32[384,768]{1,0:T(8,128)S(1)}, u32[]{:S(2)}, u32[]{:S(2)}) collective-permute-start(f32[384,768]{1,0:T(8,128)S(1)} %correlate.2), channel_id=1, source_target_pairs={{0,1},{1,0},{2,3},{3,2},{4,5},{5,4},{6,7},{7,6},{8,9},{9,8},{10,11... | collective-permute-start | bytes 3538952 | tf_op jit(solution)/shard_map/ppermute | solution.py:49
  145.6 2.5 %collective-permute-done.30.refs_16_ = f32[384,768]{1,0:T(8,128)S(1)} collective-permute-done((f32[384,768]{1,0:T(8,128)S(1)}, f32[384,768]{1,0:T(8,128)S(1)}, u32[]{:S(2)}, u32[]{:S(2)}) %collective-permute-start.30) | collective-permute-done | bytes 1179680 | tf_op jit(solution)/shard_map/ppermute | solution.py:49
  148.1 2.9 %correlate.3 = f32[384,768]{1,0:T(8,128)} custom-call(s32[52]{0:T(128)S(1)} %concatenate.7.table, bf16[64,768]{1,0:T(8,128)(2,1)S(1)} %get-tuple-element.48.refs_0_, bf16[64,768]{1,0:T(8,128)(2,1)S(1)} %get-tuple-element.49.refs_1_, bf16[64,768]{1,0:T(8,128)(2,1)S(1)} %get-tuple-element.52.refs_2_, bf16[64,768]{1,0:T(8,128)(2,1)S(1)} %get-tuple-element.57.refs_3_, ...), custom_call_target="tpu_custom_call" | custom-call | flops 301989888 | bytes 1572864 | tf_op jit(solution)/shard_map/correlate/pallas_call | solution.py:239
  (45 shorter events, 1.8 us)
Async XLA Ops:
  0.0 24.7 %collective-permute-start.2 = (bf16[2048,768]{1,0:T(8,128)(2,1)}, bf16[2048,768]{1,0:T(8,128)(2,1)S(1)}, u32[]{:S(2)}, u32[]{:S(2)}) collective-permute-start(bf16[2048,768]{1,0:T(8,128)(2,1)} %bitcast.18), channel_id=1, source_target_pairs={{0,1},{1,0},{2,3},{3,2},{4,5},{5,4},{6,7},{7,6},{8,9},{9,8},{10,11... | collective-permute-start | bytes 9437192 | tf_op jit(solution)/shard_map/ppermute | solution.py:49
  3.2 21.5 %collective-permute-start.3 = (bf16[2048,768]{1,0:T(8,128)(2,1)}, bf16[2048,768]{1,0:T(8,128)(2,1)}, u32[]{:S(2)}, u32[]{:S(2)}) collective-permute-start(bf16[2048,768]{1,0:T(8,128)(2,1)} %bitcast.22), channel_id=1, source_target_pairs={{0,1},{1,0},{2,3},{3,2},{4,5},{5,4},{6,7},{7,6},{8,9},{9,8},{10,11... | collective-permute-start | bytes 9437192 | tf_op jit(solution)/shard_map/ppermute | solution.py:49
  3.2 20.6 %collective-permute-start.1 = (bf16[64,4096]{1,0:T(8,128)(2,1)}, bf16[64,4096]{1,0:T(8,128)(2,1)}, u32[]{:S(2)}, u32[]{:S(2)}) collective-permute-start(bf16[64,4096]{1,0:T(8,128)(2,1)} %bitcast.26), channel_id=1, source_target_pairs={{0,254},{2,4},{4,2},{6,8},{8,6},{10,12},{12,10},{14,16},{16,14},{1... | collective-permute-start | bytes 1572872 | tf_op jit(solution)/shard_map/ppermute | solution.py:19
  11.7 13.0 %collective-permute-start = (bf16[64,4096]{1,0:T(8,128)(2,1)}, bf16[64,4096]{1,0:T(8,128)(2,1)}, u32[]{:S(2)}, u32[]{:S(2)}) collective-permute-start(bf16[64,4096]{1,0:T(8,128)(2,1)} %bitcast.27), channel_id=1, source_target_pairs={{0,2},{2,0},{4,6},{6,4},{8,10},{10,8},{12,14},{14,12},{16,18},{18,... | collective-permute-start | bytes 1572872 | tf_op jit(solution)/shard_map/ppermute | solution.py:19
  24.7 12.1 %collective-permute-start.7 = (bf16[64,4096]{1,0:T(8,128)(2,1)}, bf16[64,4096]{1,0:T(8,128)(2,1)}, u32[]{:S(2)}, u32[]{:S(2)}) collective-permute-start(bf16[64,4096]{1,0:T(8,128)(2,1)} %collective-permute-done.1.refs_10_.refs_11_), channel_id=1, source_target_pairs={{0,240},{2,18},{4,244},{6,22},{8,248},{10,26},{12,252},{14,30},{16... | collective-permute-start | bytes 1572872 | tf_op jit(solution)/shard_map/ppermute | solution.py:19
  25.3 11.8 %collective-permute-start.4 = (bf16[64,4096]{1,0:T(8,128)(2,1)}, bf16[64,4096]{1,0:T(8,128)(2,1)}, u32[]{:S(2)}, u32[]{:S(2)}) collective-permute-start(bf16[64,4096]{1,0:T(8,128)(2,1)} %collective-permute-done.1.refs_10_.refs_11_), channel_id=1, source_target_pairs={{0,2},{2,0},{4,6},{6,4},{8,10},{10,8},{12,14},{14,12},{16,18},{18,... | collective-permute-start | bytes 1572872 | tf_op jit(solution)/shard_map/ppermute | solution.py:19
  25.3 26.3 %collective-permute-start.6 = (bf16[64,4096]{1,0:T(8,128)(2,1)}, bf16[64,4096]{1,0:T(8,128)(2,1)}, u32[]{:S(2)}, u32[]{:S(2)}) collective-permute-start(bf16[64,4096]{1,0:T(8,128)(2,1)} %collective-permute-done.refs_4_.refs_5_), channel_id=1, source_target_pairs={{0,16},{2,242},{4,20},{6,246},{8,24},{10,250},{12,28},{14,254},{16... | collective-permute-start | bytes 1572872 | tf_op jit(solution)/shard_map/ppermute | solution.py:19
  26.2 25.4 %collective-permute-start.5 = (bf16[64,4096]{1,0:T(8,128)(2,1)}, bf16[64,4096]{1,0:T(8,128)(2,1)}, u32[]{:S(2)}, u32[]{:S(2)}) collective-permute-start(bf16[64,4096]{1,0:T(8,128)(2,1)} %collective-permute-done.refs_4_.refs_5_), channel_id=1, source_target_pairs={{0,254},{2,4},{4,2},{6,8},{8,6},{10,12},{12,10},{14,16},{16,14},{1... | collective-permute-start | bytes 1572872 | tf_op jit(solution)/shard_map/ppermute | solution.py:19
  51.6 20.5 %collective-permute-start.10 = (bf16[64,4096]{1,0:T(8,128)(2,1)}, bf16[64,4096]{1,0:T(8,128)(2,1)}, u32[]{:S(2)}, u32[]{:S(2)}) collective-permute-start(bf16[64,4096]{1,0:T(8,128)(2,1)} %collective-permute-done.5.refs_6_.refs_7_), channel_id=1, source_target_pairs={{0,240},{2,18},{4,244},{6,22},{8,248},{10,26},{12,252},{14,30},{16... | collective-permute-start | bytes 1572872 | tf_op jit(solution)/shard_map/ppermute | solution.py:19
  52.9 19.2 %collective-permute-start.8 = (bf16[64,4096]{1,0:T(8,128)(2,1)}, bf16[64,4096]{1,0:T(8,128)(2,1)}, u32[]{:S(2)}, u32[]{:S(2)}) collective-permute-start(bf16[64,4096]{1,0:T(8,128)(2,1)} %collective-permute-done.5.refs_6_.refs_7_), channel_id=1, source_target_pairs={{0,2},{2,0},{4,6},{6,4},{8,10},{10,8},{12,14},{14,12},{16,18},{18,... | collective-permute-start | bytes 1572872 | tf_op jit(solution)/shard_map/ppermute | solution.py:19
  52.9 19.8 %collective-permute-start.11 = (bf16[64,4096]{1,0:T(8,128)(2,1)}, bf16[64,4096]{1,0:T(8,128)(2,1)}, u32[]{:S(2)}, u32[]{:S(2)}) collective-permute-start(bf16[64,4096]{1,0:T(8,128)(2,1)} %collective-permute-done.4.refs_0_.refs_1_), channel_id=1, source_target_pairs={{0,16},{2,242},{4,20},{6,246},{8,24},{10,250},{12,28},{14,254},{16... | collective-permute-start | bytes 1572872 | tf_op jit(solution)/shard_map/ppermute | solution.py:19
  53.1 19.6 %collective-permute-start.9 = (bf16[64,4096]{1,0:T(8,128)(2,1)}, bf16[64,4096]{1,0:T(8,128)(2,1)}, u32[]{:S(2)}, u32[]{:S(2)}) collective-permute-start(bf16[64,4096]{1,0:T(8,128)(2,1)} %collective-permute-done.4.refs_0_.refs_1_), channel_id=1, source_target_pairs={{0,0},{2,4},{4,2},{6,8},{8,6},{10,12},{12,10},{14,16},{16,14},{18,... | collective-permute-start | bytes 1572872 | tf_op jit(solution)/shard_map/ppermute | solution.py:19
  60.6 1.9 %copy-start = (bf16[1,2048,768]{2,1,0:T(8,128)(2,1)S(1)}, bf16[1,2048,768]{2,1,0:T(8,128)(2,1)}, u32[]{:S(2)}) copy-start(bf16[1,2048,768]{2,1,0:T(8,128)(2,1)} %param.6) | copy-start | bytes 9437188
  62.5 1.9 %copy-start.2 = (bf16[1,2048,768]{2,1,0:T(8,128)(2,1)S(1)}, bf16[1,2048,768]{2,1,0:T(8,128)(2,1)}, u32[]{:S(2)}) copy-start(bf16[1,2048,768]{2,1,0:T(8,128)(2,1)} %param.7) | copy-start | bytes 9437188
  64.4 1.0 copy-start.4
  65.4 15.8 %copy-start.1 = (bf16[1,2048,768]{2,1,0:T(8,128)(2,1)S(1)}, bf16[1,2048,768]{2,1,0:T(8,128)(2,1)}, u32[]{:S(2)}) copy-start(bf16[1,2048,768]{2,1,0:T(8,128)(2,1)} %param.6) | copy-start | bytes 9437188
  65.4 15.8 %copy-start.3 = (bf16[1,2048,768]{2,1,0:T(8,128)(2,1)S(1)}, bf16[1,2048,768]{2,1,0:T(8,128)(2,1)}, u32[]{:S(2)}) copy-start(bf16[1,2048,768]{2,1,0:T(8,128)(2,1)} %param.7) | copy-start | bytes 9437188
  74.3 15.3 %collective-permute-start.12 = (bf16[64,4096]{1,0:T(8,128)(2,1)S(1)}, bf16[64,4096]{1,0:T(8,128)(2,1)S(1)}, u32[]{:S(2)}, u32[]{:S(2)}) collective-permute-start(bf16[64,4096]{1,0:T(8,128)(2,1)S(1)} %get-tuple-element.55), channel_id=1, source_target_pairs={{0,2},{2,0},{4,6},{6,4},{8,10},{10,8},{12,14},{14,12},{16,18},{18,... | collective-permute-start | bytes 1572872 | tf_op jit(solution)/shard_map/ppermute | solution.py:19
  74.4 16.2 %collective-permute-start.13 = (bf16[64,4096]{1,0:T(8,128)(2,1)S(1)}, bf16[64,4096]{1,0:T(8,128)(2,1)S(1)}, u32[]{:S(2)}, u32[]{:S(2)}) collective-permute-start(bf16[64,4096]{1,0:T(8,128)(2,1)S(1)} %get-tuple-element.56), channel_id=1, source_target_pairs={{0,254},{2,4},{4,2},{6,8},{8,6},{10,12},{12,10},{14,16},{16,14},{1... | collective-permute-start | bytes 1572872 | tf_op jit(solution)/shard_map/ppermute | solution.py:19
  81.2 15.8 %collective-permute-start.14 = (bf16[64,768]{1,0:T(8,128)(2,1)S(1)}, bf16[64,768]{1,0:T(8,128)(2,1)S(1)}, u32[]{:S(2)}, u32[]{:S(2)}) collective-permute-start(bf16[64,768]{1,0:T(8,128)(2,1)S(1)} %get-tuple-element.49.refs_1_), channel_id=1, source_target_pairs={{0,2},{2,0},{4,6},{6,4},{8,10},{10,8},{12,14},{14,12},{16,18},{18,... | collective-permute-start | bytes 294920 | tf_op jit(solution)/shard_map/ppermute | solution.py:19
  81.2 21.4 %collective-permute-start.20 = (bf16[64,768]{1,0:T(8,128)(2,1)S(1)}, bf16[64,768]{1,0:T(8,128)(2,1)S(1)}, u32[]{:S(2)}, u32[]{:S(2)}) collective-permute-start(bf16[64,768]{1,0:T(8,128)(2,1)S(1)} %get-tuple-element.61.refs_7_), channel_id=1, source_target_pairs={{0,14},{2,4},{4,2},{6,8},{8,6},{10,12},{12,10},{14,0},{16,30},{18,... | collective-permute-start | bytes 294920 | tf_op jit(solution)/shard_map/ppermute | solution.py:19
  86.8 15.8 %collective-permute-start.19 = (bf16[64,768]{1,0:T(8,128)(2,1)S(1)}, bf16[64,768]{1,0:T(8,128)(2,1)S(1)}, u32[]{:S(2)}, u32[]{:S(2)}) collective-permute-start(bf16[64,768]{1,0:T(8,128)(2,1)S(1)} %get-tuple-element.52.refs_2_), channel_id=1, source_target_pairs={{0,4},{2,14},{4,8},{6,2},{8,12},{10,6},{12,0},{14,10},{16,20},{18,... | collective-permute-start | bytes 294920 | tf_op jit(solution)/shard_map/ppermute | solution.py:19
  89.6 12.9 %collective-permute-start.15 = (bf16[64,768]{1,0:T(8,128)(2,1)S(1)}, bf16[64,768]{1,0:T(8,128)(2,1)S(1)}, u32[]{:S(2)}, u32[]{:S(2)}) collective-permute-start(bf16[64,768]{1,0:T(8,128)(2,1)S(1)} %get-tuple-element.60.refs_6_), channel_id=1, source_target_pairs={{0,12},{2,6},{4,0},{6,10},{8,4},{10,14},{12,8},{14,2},{16,28},{18,... | collective-permute-start | bytes 294920 | tf_op jit(solution)/shard_map/ppermute | solution.py:19
  96.8 5.7 %collective-permute-start.16 = (bf16[64,768]{1,0:T(8,128)(2,1)S(1)}, bf16[64,768]{1,0:T(8,128)(2,1)S(1)}, u32[]{:S(2)}, u32[]{:S(2)}) collective-permute-start(bf16[64,768]{1,0:T(8,128)(2,1)S(1)} %get-tuple-element.57.refs_3_), channel_id=1, source_target_pairs={{0,6},{2,12},{4,10},{6,0},{8,14},{10,4},{12,2},{14,8},{16,22},{18,... | collective-permute-start | bytes 294920 | tf_op jit(solution)/shard_map/ppermute | solution.py:19
  96.9 10.8 %collective-permute-start.17 = (bf16[64,768]{1,0:T(8,128)(2,1)S(1)}, bf16[64,768]{1,0:T(8,128)(2,1)S(1)}, u32[]{:S(2)}, u32[]{:S(2)}) collective-permute-start(bf16[64,768]{1,0:T(8,128)(2,1)S(1)} %get-tuple-element.58.refs_4_), channel_id=1, source_target_pairs={{0,8},{2,10},{4,12},{6,14},{8,0},{10,2},{12,4},{14,6},{16,24},{18,... | collective-permute-start | bytes 294920 | tf_op jit(solution)/shard_map/ppermute | solution.py:19
  102.6 7.1 %collective-permute-start.18 = (bf16[64,768]{1,0:T(8,128)(2,1)S(1)}, bf16[64,768]{1,0:T(8,128)(2,1)S(1)}, u32[]{:S(2)}, u32[]{:S(2)}) collective-permute-start(bf16[64,768]{1,0:T(8,128)(2,1)S(1)} %get-tuple-element.59.refs_5_), channel_id=1, source_target_pairs={{0,10},{2,8},{4,14},{6,12},{8,2},{10,0},{12,6},{14,4},{16,26},{18,... | collective-permute-start | bytes 294920 | tf_op jit(solution)/shard_map/ppermute | solution.py:19
  110.4 5.0 %collective-permute-start.21 = (bf16[64,768]{1,0:T(8,128)(2,1)S(1)}, bf16[64,768]{1,0:T(8,128)(2,1)S(1)}, u32[]{:S(2)}, u32[]{:S(2)}) collective-permute-start(bf16[64,768]{1,0:T(8,128)(2,1)S(1)} %get-tuple-element.63.nxt), channel_id=1, source_target_pairs={{0,16},{2,0},{4,20},{6,4},{8,24},{10,8},{12,28},{14,12},{16,32},{1... | collective-permute-start | bytes 294920 | tf_op jit(solution)/shard_map/ppermute | solution.py:19
  110.5 4.9 %collective-permute-start.22 = (bf16[64,768]{1,0:T(8,128)(2,1)S(1)}, bf16[64,768]{1,0:T(8,128)(2,1)S(1)}, u32[]{:S(2)}, u32[]{:S(2)}) collective-permute-start(bf16[64,768]{1,0:T(8,128)(2,1)S(1)} %get-tuple-element.64.last), channel_id=1, source_target_pairs={{0,2},{2,18},{4,6},{6,22},{8,10},{10,26},{12,14},{14,30},{16,0},{1... | collective-permute-start | bytes 294920 | tf_op jit(solution)/shard_map/ppermute | solution.py:19
  116.2 9.6 %collective-permute-start.23 = (bf16[64,768]{1,0:T(8,128)(2,1)S(1)}, bf16[64,768]{1,0:T(8,128)(2,1)S(1)}, u32[]{:S(2)}, u32[]{:S(2)}) collective-permute-start(bf16[64,768]{1,0:T(8,128)(2,1)S(1)} %get-tuple-element.66), channel_id=1, source_target_pairs={{0,2},{2,0},{4,6},{6,4},{8,10},{10,8},{12,14},{14,12},{16,18},{18,... | collective-permute-start | bytes 294920 | tf_op jit(solution)/shard_map/ppermute | solution.py:19
  117.4 10.8 %collective-permute-start.24 = (bf16[64,768]{1,0:T(8,128)(2,1)S(1)}, bf16[64,768]{1,0:T(8,128)(2,1)S(1)}, u32[]{:S(2)}, u32[]{:S(2)}) collective-permute-start(bf16[64,768]{1,0:T(8,128)(2,1)S(1)} %get-tuple-element.67), channel_id=1, source_target_pairs={{0,12},{2,6},{4,0},{6,10},{8,4},{10,14},{12,8},{14,2},{16,28},{18,... | collective-permute-start | bytes 294920 | tf_op jit(solution)/shard_map/ppermute | solution.py:19
  120.4 7.8 %collective-permute-start.25 = (bf16[64,768]{1,0:T(8,128)(2,1)S(1)}, bf16[64,768]{1,0:T(8,128)(2,1)S(1)}, u32[]{:S(2)}, u32[]{:S(2)}) collective-permute-start(bf16[64,768]{1,0:T(8,128)(2,1)S(1)} %get-tuple-element.68), channel_id=1, source_target_pairs={{0,6},{2,12},{4,10},{6,0},{8,14},{10,4},{12,2},{14,8},{16,22},{18,... | collective-permute-start | bytes 294920 | tf_op jit(solution)/shard_map/ppermute | solution.py:19
  121.4 7.6 %collective-permute-start.26 = (bf16[64,768]{1,0:T(8,128)(2,1)S(1)}, bf16[64,768]{1,0:T(8,128)(2,1)S(1)}, u32[]{:S(2)}, u32[]{:S(2)}) collective-permute-start(bf16[64,768]{1,0:T(8,128)(2,1)S(1)} %get-tuple-element.69), channel_id=1, source_target_pairs={{0,8},{2,10},{4,12},{6,14},{8,0},{10,2},{12,4},{14,6},{16,24},{18,... | collective-permute-start | bytes 294920 | tf_op jit(solution)/shard_map/ppermute | solution.py:19
  123.1 7.9 %collective-permute-start.27 = (bf16[64,768]{1,0:T(8,128)(2,1)S(1)}, bf16[64,768]{1,0:T(8,128)(2,1)S(1)}, u32[]{:S(2)}, u32[]{:S(2)}) collective-permute-start(bf16[64,768]{1,0:T(8,128)(2,1)S(1)} %get-tuple-element.70), channel_id=1, source_target_pairs={{0,10},{2,8},{4,14},{6,12},{8,2},{10,0},{12,6},{14,4},{16,26},{18,... | collective-permute-start | bytes 294920 | tf_op jit(solution)/shard_map/ppermute | solution.py:19
  125.8 7.4 %collective-permute-start.28 = (bf16[64,768]{1,0:T(8,128)(2,1)S(1)}, bf16[64,768]{1,0:T(8,128)(2,1)S(1)}, u32[]{:S(2)}, u32[]{:S(2)}) collective-permute-start(bf16[64,768]{1,0:T(8,128)(2,1)S(1)} %get-tuple-element.71), channel_id=1, source_target_pairs={{0,4},{2,14},{4,8},{6,2},{8,12},{10,6},{12,0},{14,10},{16,20},{18,... | collective-permute-start | bytes 294920 | tf_op jit(solution)/shard_map/ppermute | solution.py:19
  128.2 7.4 %collective-permute-start.29 = (bf16[64,768]{1,0:T(8,128)(2,1)S(1)}, bf16[64,768]{1,0:T(8,128)(2,1)S(1)}, u32[]{:S(2)}, u32[]{:S(2)}) collective-permute-start(bf16[64,768]{1,0:T(8,128)(2,1)S(1)} %get-tuple-element.72), channel_id=1, source_target_pairs={{0,14},{2,4},{4,2},{6,8},{8,6},{10,12},{12,10},{14,0},{16,30},{18,... | collective-permute-start | bytes 294920 | tf_op jit(solution)/shard_map/ppermute | solution.py:19
  137.4 10.6 %collective-permute-start.30 = (f32[384,768]{1,0:T(8,128)S(1)}, f32[384,768]{1,0:T(8,128)S(1)}, u32[]{:S(2)}, u32[]{:S(2)}) collective-permute-start(f32[384,768]{1,0:T(8,128)S(1)} %correlate.2), channel_id=1, source_target_pairs={{0,1},{1,0},{2,3},{3,2},{4,5},{5,4},{6,7},{7,6},{8,9},{9,8},{10,11... | collective-permute-start | bytes 3538952 | tf_op jit(solution)/shard_map/ppermute | solution.py:49
